TPU v7x, 32 devices: a whole 2x2x4 slice. The times are simulated.
32 devices in a mesh: dp: 8 (over z, x), mp: 4 (over y, core).
Axes of the slice: x: 2, y: 2, z: 4, core: 2. Of those that a mesh axis runs over, the one named last changes fastest.
Arguments:
- frames: bfloat16 [2048, 16, 512], P('mp', 'dp'), may hold values from -6 to 6
- cotangent: bfloat16 [2048, 16, 512], P('mp', 'dp'), may hold values from -6 to 6
- lengths: int32 [16], P('dp'), may hold values from 128 to 2048, as said below
- weight_project: float32 [3, 512, 512], P(None, 'dp', 'mp'), may hold values from -0.25 to 0.25
- weight_combine: float32 [512, 512], P('dp', 'mp'), may hold values from -0.5 to 0.5
- weight_expand: float32 [512, 2048], P('dp', 'mp'), may hold values from -0.25 to 0.25
- weight_reduce: float32 [512, 2048], P('dp', 'mp'), may hold values from -0.125 to 0.125
- moment_project: float32 [3, 512, 512], P(None, 'dp', 'mp'), may hold values from -512 to 512
- moment_combine: float32 [512, 512], P('dp', 'mp'), may hold values from -512 to 512
- moment_expand: float32 [512, 2048], P('dp', 'mp'), may hold values from -256 to 256
- moment_reduce: float32 [512, 2048], P('dp', 'mp'), may hold values from -512 to 512
- average_project: float32 [3, 512, 512], P(None, 'dp', 'mp'), may hold values from -0.25 to 0.25
- average_combine: float32 [512, 512], P('dp', 'mp'), may hold values from -0.5 to 0.5
- average_expand: float32 [512, 2048], P('dp', 'mp'), may hold values from -0.25 to 0.25
- average_reduce: float32 [512, 2048], P('dp', 'mp'), may hold values from -0.125 to 0.125
- norm_params: float32 [4, 512], replicated, may hold values from -0.5 to 1.4, as said below
- norm_moment: float32 [4, 512], replicated, may hold values from -512 to 512
- norm_average: float32 [4, 512], replicated, may hold values from -0.5 to 1.4, as said below
Outputs:
- layer_out: bfloat16 [2048, 16, 512], P('mp', 'dp')
- input_gradient: float32 [2048, 16, 512], P('mp', 'dp')
- gradient_project: float32 [3, 512, 512], P(None, 'dp', 'mp')
- gradient_combine: float32 [512, 512], P('dp', 'mp')
- gradient_expand: float32 [512, 2048], P('dp', 'mp')
- gradient_reduce: float32 [512, 2048], P('dp', 'mp')
- momentum_project: float32 [3, 512, 512], P(None, 'dp', 'mp')
- momentum_combine: float32 [512, 512], P('dp', 'mp')
- momentum_expand: float32 [512, 2048], P('dp', 'mp')
- momentum_reduce: float32 [512, 2048], P('dp', 'mp')
- smoothed_project: float32 [3, 512, 512], P(None, 'dp', 'mp')
- smoothed_combine: float32 [512, 512], P('dp', 'mp')
- smoothed_expand: float32 [512, 2048], P('dp', 'mp')
- smoothed_reduce: float32 [512, 2048], P('dp', 'mp')
- updated_project: float32 [3, 512, 512], P(None, 'dp', 'mp')
- updated_combine: float32 [512, 512], P('dp', 'mp')
- updated_expand: float32 [512, 2048], P('dp', 'mp')
- updated_reduce: float32 [512, 2048], P('dp', 'mp')
- rounded_project: bfloat16 [3, 512, 512], P(None, 'dp', 'mp')
- rounded_combine: bfloat16 [512, 512], P('dp', 'mp')
- rounded_expand: bfloat16 [512, 2048], P('dp', 'mp')
- rounded_reduce: bfloat16 [512, 2048], P('dp', 'mp')
- norm_gradient: float32 [4, 512], replicated
- norm_momentum: float32 [4, 512], replicated
- norm_smoothed: float32 [4, 512], replicated
- norm_updated: float32 [4, 512], replicated
Inputs may be any that keep to these rules, and one draw needn't show every extreme that they name: `lengths`: among the 2 utterances of each index of dp, at least one has 2048 frames. `norm_params`: rows 0 and 2 are gains, rows 1 and 3 shifts. `norm_average`: rows 0 and 2 are gains, rows 1 and 3 shifts.
All inputs are finite; a program needn't handle non-finite values.
Results may differ from a plain program's by a relative error of at most 0.014.
Values may be sent and summed in bfloat16 or wider, within the bound.
No kernel may reach another device: no remote copies, remote signals or barrier semaphores. Data moves between devices by JAX's collectives and lax.ppermute only.
A program may use at most 192 MiB of HBM per device.

v0:
```python
import functools
import math

import jax
import jax.numpy as jnp
from jax import lax
from jax.experimental import pallas as pl
from jax.experimental.pallas import tpu as pltpu
from jax.sharding import PartitionSpec as P

HEADS = 8
HEAD_DIM = 64
WINDOW = 10
HALO = 16

eps_norm = 1e-05
momentum_decay = 0.9
average_decay = 0.6
matrix_rate = 0.0001
norm_rate = 0.001
masked_score = -1e30

GROUP = 4
LANES = GROUP * HEAD_DIM
QUERIES = 112
KEYS = QUERIES + HALO

f32 = jnp.float32
bf16 = jnp.bfloat16


def mm(a, b):
    return lax.dot_general(a, b, (((1,), (0,)), ((), ())), preferred_element_type=f32)


def mm_bt(a, b):
    return lax.dot_general(a, b, (((1,), (1,)), ((), ())), preferred_element_type=f32)


def mm_at(a, b):
    return lax.dot_general(a, b, (((0,), (0,)), ((), ())), preferred_element_type=f32)


def normalise(values):
    center = values - jnp.mean(values, axis=-1, keepdims=True)
    spread = jnp.mean(center * center, axis=-1, keepdims=True)
    inverse = lax.rsqrt(spread + eps_norm)
    return center * inverse, inverse


def norm_backward(values, gain, upstream):
    scaled, inverse = normalise(values)
    weighted = upstream * gain
    inner = (
        weighted
        - jnp.mean(weighted, axis=-1, keepdims=True)
        - scaled * jnp.mean(weighted * scaled, axis=-1, keepdims=True)
    )
    return inner * inverse, upstream * scaled


def query_blocks(total):
    blocks = []
    at = HALO
    while at < total:
        rows = min(QUERIES, total - at)
        blocks.append((at, rows, min(at - HALO, total - KEYS)))
        at += rows
    return blocks


def band(block, start, length):
    q0, rows, k0 = block
    query = lax.broadcasted_iota(jnp.int32, (rows, KEYS), 0)
    key = lax.broadcasted_iota(jnp.int32, (rows, KEYS), 1)
    behind = query - key + (q0 - k0)
    time = key + (start + k0 - HALO)
    inside = (time < length) | (behind == 0)
    return (behind >= 0) & (behind <= WINDOW) & (time >= 0) & inside


def head_lanes():
    lane = lax.broadcasted_iota(jnp.int32, (1, LANES), 1)
    return [(lane >= h * HEAD_DIM) & (lane < (h + 1) * HEAD_DIM) for h in range(GROUP)]


def stack_heads(block):
    zero = jnp.zeros_like(block)
    return jnp.concatenate([jnp.where(m, block, zero) for m in head_lanes()], axis=0)


def merge_heads(stacked, rows):
    masks = head_lanes()
    out = jnp.where(masks[0], stacked[:rows], 0.0)
    for h in range(1, GROUP):
        out = jnp.where(masks[h], stacked[h * rows : (h + 1) * rows], out)
    return out


def softmax_rows(scores, allowed):
    scores = jnp.where(allowed, scores * (1.0 / math.sqrt(HEAD_DIM)), masked_score)
    raised = jnp.exp(scores - jnp.max(scores, axis=-1, keepdims=True))
    return raised / jnp.sum(raised, axis=-1, keepdims=True)


def block_order(n_dp, near_first, split=False):
    row, near, far_bits = -1, 0, list(range(1, (n_dp - 1).bit_length()))
    first, second = (near, row) if near_first else (row, near)
    bits = [first, far_bits[0], second, *far_bits[1:]] if split else [first, second, *far_bits]
    blocks = []
    for at in range(2 * n_dp):
        value = {bit: (at >> (len(bits) - 1 - i)) & 1 for i, bit in enumerate(bits)}
        blocks.append((value[row], sum(value[bit] << bit for bit in bits if bit != row)))
    return blocks


def place_weights(n_dp, core, own_a, own_b, got_a, got_b, wp_ref, wc_ref):
    width, cols = wc_ref.shape[0], own_a.shape[1]
    r = width // n_dp
    for which, ref_a, ref_b in ((core, own_a, own_b), (1 - core, got_a, got_b)):
        for ref, first, near_first in ((ref_a, 0, True), (ref_b, 2, False)):
            for p, (y, d) in enumerate(block_order(n_dp, near_first)):
                at = pl.multiple_of((2 * y + which) * cols, cols)
                for i in range(2):
                    block = ref[(2 * p + i) * r : (2 * p + i + 1) * r]
                    if first + i < 3:
                        wp_ref[d * r : (d + 1) * r, pl.ds((first + i) * width + at, cols)] = block
                    else:
                        wc_ref[d * r : (d + 1) * r, pl.ds(at, cols)] = block


def edge_kernel(place_ref, frames_ref, cotangent_ref, near_ref, over_ref):
    last = frames_ref.shape[1] - HALO
    for core, early, late in ((0, over_ref, near_ref), (1, near_ref, over_ref)):

        @pl.when(place_ref[1] == core)
        def _():
            early[0] = frames_ref[:, :HALO]
            early[1] = cotangent_ref[:, :HALO]
            late[0] = frames_ref[:, last:]
            late[1] = frames_ref[:, last:]


def frames_kernel(place_ref, frames_ref, near_ref, over_ref, *outs):
    own = frames_ref.shape[1]
    for u, out in enumerate(outs):
        out[HALO : HALO + own] = frames_ref[u]
    for core, left, right in ((0, over_ref, near_ref), (1, near_ref, over_ref)):

        @pl.when(place_ref[1] == core)
        def _():
            for u, out in enumerate(outs):
                out[:HALO] = left[0, u]
                out[HALO + own :] = right[0, u]


def seed_kernel(place_ref, cotangent_ref, near_ref, over_ref, seed_ref, seed_t_ref):
    own = cotangent_ref.shape[1]
    for u in range(seed_ref.shape[0]):

        def valid(first, count):
            time = lax.broadcasted_iota(jnp.int32, (count, 1), 0) + (place_ref[0] + first)
            return time < place_ref[2 + u]

        mine = cotangent_ref[u]
        mine = jnp.where(valid(0, own), mine, jnp.zeros_like(mine))
        seed_ref[u, :own] = mine
        seed_t_ref[:, u * own : (u + 1) * own] = mine.T
        theirs = jnp.where(place_ref[1] == 0, near_ref[1, u], over_ref[1, u])
        seed_ref[u, own:] = jnp.where(valid(own, HALO), theirs, jnp.zeros_like(theirs))


def attend_one(
    u, place_ref, frames_ref, norms_ref, wp_ref, wc_ref,
    qkv_ref, probs_ref, first_ref, mixed_ref, residual_ref, second_ref, second_t_ref,
):
    total, width = frames_ref.shape
    own = first_ref.shape[0]
    start, length = place_ref[0], place_ref[2 + u]
    scaled, _ = normalise(frames_ref[...].astype(f32))
    normed = (scaled * norms_ref[0:1] + norms_ref[1:2]).astype(bf16)
    first_ref[...] = normed[HALO : HALO + own]
    qkv_ref[...] = mm(normed, wp_ref[...]).astype(bf16)
    def group(hg, carry):
        at = pl.multiple_of(hg * LANES, LANES)
        here = pl.ds(pl.multiple_of(hg * KEYS, KEYS), KEYS)
        for b, block in enumerate(query_blocks(total)):
            q0, rows, k0 = block
            allowed = band(block, start, length)
            queries = stack_heads(qkv_ref[q0 : q0 + rows, pl.ds(at, LANES)])
            keys = qkv_ref[k0 : k0 + KEYS, pl.ds(width + at, LANES)]
            values = qkv_ref[k0 : k0 + KEYS, pl.ds(2 * width + at, LANES)]
            scores = mm_bt(queries, keys)
            low_probs = []
            for h in range(GROUP):
                probs = softmax_rows(scores[h * rows : (h + 1) * rows], allowed)
                probs_ref[b, h, :rows, here] = probs
                low_probs.append(probs.astype(bf16))
            out = merge_heads(mm(jnp.concatenate(low_probs, axis=0), values), rows)
            mixed_ref[q0 - HALO : q0 - HALO + rows, pl.ds(at, LANES)] = out.astype(bf16)
        return carry

    lax.fori_loop(0, width // LANES, group, 0)
    residual = frames_ref[HALO:total].astype(f32) + mm_bt(mixed_ref[...], wc_ref[...])
    residual_ref[...] = residual
    scaled, _ = normalise(residual)
    second_ref[...] = (scaled * norms_ref[2:3] + norms_ref[3:4]).astype(bf16)
    second_t_ref[...] = second_ref[:own].T


def attend_first_kernel(
    n_dp, place_ref, frames_ref, norms_ref, own_a, own_b, got_a, got_b, *refs
):
    *outs, wp_ref, wc_ref = refs
    place_weights(n_dp, place_ref[1], own_a, own_b, got_a, got_b, wp_ref, wc_ref)
    attend_one(0, place_ref, frames_ref, norms_ref, wp_ref, wc_ref, *outs)


def attend_next_kernel(place_ref, frames_ref, norms_ref, wp_ref, wc_ref, *refs):
    attend_one(1, place_ref, frames_ref, norms_ref, wp_ref, wc_ref, *refs)


def gelu_parts(value):
    slope = math.sqrt(2.0 / math.pi)
    square = value * value
    tanh = jnp.tanh(value * (slope + (slope * 0.044715) * square))
    half = 0.5 + 0.5 * tanh
    curve = half + (0.5 * value) * (1.0 - tanh * tanh) * (
        slope + (slope * 3.0 * 0.044715) * square
    )
    return value * half, curve


def feed_half(
    n_dp, seconds, seconds_t, seed_ref, seed_t_ref, we_ref, wr_ref, ge_ref, gr_ref,
    wide_e, wide_r, active_ref, grad_ref, second_ref, add_fed, add_back,
):
    own = seconds_t[0].shape[1]
    width, hidden = wide_e.shape[0], we_ref.shape[1]
    r = width // n_dp
    for ref, wide, near_first in ((we_ref, wide_e, True), (wr_ref, wide_r, False)):
        for p, (y, d) in enumerate(block_order(n_dp, near_first)):
            wide[d * r : (d + 1) * r, y * hidden : (y + 1) * hidden] = ref[p * r : (p + 1) * r]
    for u, ref in enumerate(seconds):
        second_ref[u] = ref[...]

    def one(u, carry):
        rows = pl.ds(pl.multiple_of(u * own, own), own)
        active, curve = gelu_parts(mm(second_ref[u], wide_e[...]))
        active_ref[rows] = active[:own].astype(bf16)
        grad_ref[u] = (mm(seed_ref[u], wide_r[...]) * curve).astype(bf16)
        add_fed(u, mm_bt(active_ref[rows], wide_r[...]))
        add_back(u, mm_bt(grad_ref[u], wide_e[...]))
        return carry

    lax.fori_loop(0, len(seconds), one, 0)
    total_r = mm(seed_t_ref[...], active_ref[...])
    total_e = mm(seconds_t[0][...], grad_ref[0, :own]) + mm(seconds_t[1][...], grad_ref[1, :own])
    for total, ref, near_first in ((total_e, ge_ref, True), (total_r, gr_ref, False)):
        for p, (y, d) in enumerate(block_order(n_dp, near_first, True)):
            block = total[d * r : (d + 1) * r, y * hidden : (y + 1) * hidden]
            ref[p * r : (p + 1) * r] = block.astype(bf16)


def feed_first_kernel(n_dp, we_ref, wr_ref, n0, seed_ref, n1, seed_t_ref, t0, t1, *refs):
    fed_ref, back_ref, ge_ref, gr_ref, *scratch = refs

    def add_fed(u, value):
        fed_ref[u] = value

    def add_back(u, value):
        back_ref[u] = value

    feed_half(
        n_dp, (n0, n1), (t0, t1), seed_ref, seed_t_ref, we_ref, wr_ref, ge_ref, gr_ref,
        *scratch, add_fed, add_back,
    )


def feed_last_kernel(
    n_dp, we_ref, wr_ref, n0, seed_ref, fed_in, back_in, n1, r0, r1, seed_t_ref, t0, t1, *refs
):
    out_ref, back_ref, ge_ref, gr_ref, *scratch = refs
    own = out_ref.shape[1]

    def add_fed(u, value):
        residual = jnp.where(u == 0, r0[:own], r1[:own])
        out_ref[u] = (residual + (fed_in[u] + value)).astype(bf16)

    def add_back(u, value):
        back_ref[u] = back_in[u] + value

    feed_half(
        n_dp, (n0, n1), (t0, t1), seed_ref, seed_t_ref, we_ref, wr_ref, ge_ref, gr_ref,
        *scratch, add_fed, add_back,
    )


def pull_one(
    u, back_ref, residual_ref, seed_ref, wc_ref, norms_ref, qkv_ref, probs_ref,
    wide_ref, low_ref, grad_ref, norm_ref, grad_kv_ref, mixed_g_ref,
):
    total = qkv_ref.shape[0]
    own, width = low_ref.shape
    upstream = back_ref[u]
    back, gained = norm_backward(residual_ref[...], norms_ref[2:3], upstream)
    norm_ref[0:1] = jnp.sum(gained[:own], axis=0, keepdims=True)
    norm_ref[1:2] = jnp.sum(upstream[:own], axis=0, keepdims=True)
    wide = seed_ref[u].astype(f32) + back
    wide_ref[...] = wide[:own]
    low = wide.astype(bf16)
    low_ref[...] = low[:own]
    mixed_g_ref[...] = mm(low, wc_ref[...]).astype(bf16)
    grad_kv_ref[...] = jnp.zeros_like(grad_kv_ref)
    scale = 1.0 / math.sqrt(HEAD_DIM)
    def group(hg, carry):
        at = pl.multiple_of(hg * LANES, LANES)
        here = pl.ds(pl.multiple_of(hg * KEYS, KEYS), KEYS)
        first_lanes, second_lanes = pl.ds(at, LANES), pl.ds(width + at, LANES)
        for b, block in enumerate(query_blocks(total)):
            q0, rows, k0 = block
            queries = stack_heads(qkv_ref[q0 : q0 + rows, first_lanes])
            keys = qkv_ref[k0 : k0 + KEYS, second_lanes]
            values = qkv_ref[k0 : k0 + KEYS, pl.ds(2 * width + at, LANES)]
            upper = stack_heads(mixed_g_ref[q0 - HALO : q0 - HALO + rows, first_lanes])
            grad_probs = mm_bt(upper, values)
            low_probs, grad_scores = [], []
            for h in range(GROUP):
                probs = probs_ref[b, h, :rows, here]
                grad = grad_probs[h * rows : (h + 1) * rows]
                inner = jnp.sum(probs * grad, axis=-1, keepdims=True)
                low_probs.append(probs.astype(bf16))
                grad_scores.append((probs * (grad - inner)).astype(bf16))
            low_probs = jnp.concatenate(low_probs, axis=0)
            grad_scores = jnp.concatenate(grad_scores, axis=0)
            grad_q = merge_heads(mm(grad_scores, keys), rows) * scale
            mine = min(rows, HALO + own - q0)
            if mine > 0:
                grad_ref[q0 - HALO : q0 - HALO + mine, first_lanes] = grad_q[:mine].astype(bf16)
            grad_kv_ref[k0 : k0 + KEYS, first_lanes] += mm_at(grad_scores, queries) * scale
            grad_kv_ref[k0 : k0 + KEYS, second_lanes] += mm_at(low_probs, upper)
        return carry

    lax.fori_loop(0, width // LANES, group, 0)
    grad_ref[:, width:] = grad_kv_ref[HALO : HALO + own].astype(bf16)


def pull_first_kernel(*refs):
    pull_one(0, *refs)


def pull_last_kernel(
    n_dp, place_ref, back_ref, residual_ref, seed_ref, wc_ref, norms_ref, qkv_ref, probs_ref,
    first_0, first_1, mixed_0, mixed_1, grad_0, low_0, *refs,
):
    wide_ref, low_ref, grad_ref, norm_ref, keep_a, keep_b, send_a, send_b, grad_kv_ref, mixed_g_ref = refs
    pull_one(
        1, back_ref, residual_ref, seed_ref, wc_ref, norms_ref, qkv_ref, probs_ref,
        wide_ref, low_ref, grad_ref, norm_ref, grad_kv_ref, mixed_g_ref,
    )
    own, width = low_ref.shape
    core, cols, r = place_ref[1], keep_a.shape[1], width // n_dp
    firsts = first_0[...].T, first_1[...].T
    lows = low_0[...].T, low_ref[...].T
    where = {
        near_first: {block: p for p, block in enumerate(block_order(n_dp, near_first))}
        for near_first in (True, False)
    }
    for i in range(4):
        keep, send, at = (keep_a, send_a, where[True]) if i < 2 else (keep_b, send_b, where[False])
        for y in range(2):
            lanes = slice(2 * y * cols, 2 * (y + 1) * cols)
            if i < 3:
                inner = slice(i * width + lanes.start, i * width + lanes.stop)
                value = mm(firsts[0], grad_0[:, inner]) + mm(firsts[1], grad_ref[:, inner])
            else:
                value = mm(lows[0], mixed_0[:own, lanes]) + mm(lows[1], mixed_1[:own, lanes])
            mine = jnp.where(core == 0, value[:, :cols], value[:, cols:])
            other = jnp.where(core == 0, value[:, cols:], value[:, :cols])
            for d in range(n_dp):
                to = (2 * at[y, d] + i % 2) * r
                keep[to : to + r] = mine[d * r : (d + 1) * r].astype(bf16)
                send[to : to + r] = other[d * r : (d + 1) * r].astype(bf16)


def fold_norm(ref, first, value):
    cols = ref.shape[1]
    for j in range(value.shape[1] // cols):
        ref[4 * j + first : 4 * j + first + value.shape[0]] = value[:, j * cols : (j + 1) * cols]


def finish_kernel(norms_ref, wp_ref, grad_0, frames_0, wide_0, grad_1, frames_1, wide_1, norm_0, norm_1, out_0, out_1, norm_ref):
    own = out_0.shape[0]
    gains, shifts = [], []
    for grad_ref, frames_ref, wide_ref, out_ref in (
        (grad_0, frames_0, wide_0, out_0),
        (grad_1, frames_1, wide_1, out_1),
    ):
        upstream = mm_bt(grad_ref[...], wp_ref[...])
        back, gained = norm_backward(
            frames_ref[HALO : HALO + own].astype(f32), norms_ref[0:1], upstream
        )
        gains.append(jnp.sum(gained, axis=0, keepdims=True))
        shifts.append(jnp.sum(upstream, axis=0, keepdims=True))
        out_ref[...] = wide_ref[...] + back
    fold_norm(norm_ref, 0, gains[0] + gains[1])
    fold_norm(norm_ref, 1, shifts[0] + shifts[1])
    fold_norm(norm_ref, 2, norm_0[...] + norm_1[...])


VM = pl.BlockSpec(memory_space=pltpu.VMEM)
SM = pl.BlockSpec(memory_space=pltpu.SMEM)
MIB = 1024 * 1024


def call(kernel, ins, outs, scratch=(), waits=(), flops=1e9, smem=1, mib=16):
    n, m = len(ins), len(outs)
    away = pl.BlockSpec(memory_space=pl.ANY)

    def body(*refs):
        kernel(*refs[:n], *refs[n + len(waits) :])

    return pl.pallas_call(
        body,
        out_shape=tuple(jax.ShapeDtypeStruct(shape, kind) for shape, kind in outs),
        in_specs=[SM] * smem + [VM] * (n - smem) + [away] * len(waits),
        out_specs=(VM,) * m,
        scratch_shapes=[pltpu.VMEM(shape, kind) for shape, kind in scratch],
        compiler_params=pltpu.CompilerParams(vmem_limit_bytes=mib * MIB),
        cost_estimate=pl.CostEstimate(flops=int(flops), bytes_accessed=6000000, transcendentals=0),
    )(*ins, *waits)


def swap(value, axis, bit):
    n = lax.axis_size(axis)
    return lax.ppermute(value, axis, [(i, i ^ (1 << bit)) for i in range(n)])


CORE, ROW, NEAR = ("mp", 0), ("mp", 1), ("dp", 0)


def far():
    return [("dp", b) for b in range(1, (lax.axis_size("dp") - 1).bit_length())]


def side(label):
    return (lax.axis_index(label[0]) >> label[1]) & 1


def spot(label):
    return {CORE: 1, ROW: 4, NEAR: 5}.get(label, 5 + label[1])


def paired(place, streams, waits=()):
    def kernel(place_ref, *refs):
        outs = list(refs[2 * len(streams) :])
        for i, (_, _, label, parts) in enumerate(streams):
            mine, got = refs[2 * i], refs[2 * i + 1]
            high = place_ref[spot(label)]
            for part in range(parts):
                out = outs.pop(0)
                out[high] = mine[:, part]
                out[1 - high] = got[:, part]

    ins, outs = [place], []
    for mine, got, label, parts in streams:
        blocks = lax.axis_size("dp") // 4 if parts > 1 else 1
        shape = (blocks, parts, mine.shape[0] // blocks // parts, mine.shape[1])
        ins += [mine.reshape(shape), got.reshape(shape)]
        outs += [((2, blocks, *shape[2:]), mine.dtype)] * parts
    return [x.reshape(-1, x.shape[-1]) for x in call(kernel, ins, outs, waits=waits, flops=1e8, mib=8)]


def lowered(arrays, waits):
    rows = [x.shape[0] for x in arrays]

    def kernel(*refs):
        at = 0
        for ref, count in zip(refs, rows):
            refs[-1][at : at + count] = ref[...].astype(bf16)
            at += count

    return call(kernel, arrays, [((sum(rows), arrays[0].shape[1]), bf16)], waits=waits, flops=1e8, smem=0, mib=8)[0]


def halved(place, streams, joint=0, waits=()):
    counts = [len(terms) for terms, _ in streams]
    n = len(streams)

    def kernel(place_ref, *refs):
        refs = list(refs)
        groups = [[refs.pop(0) for _ in range(count)] for count in counts]
        kept, sent = refs[:n], refs[n:]
        for i, (group, (_, label)) in enumerate(zip(groups, streams)):
            mine = place_ref[spot(label)]
            kept[i][...] = total([ref[mine] for ref in group])
            gone = total([ref[1 - mine] for ref in group]).astype(bf16)
            if i < joint:
                sent[0][i] = gone
            else:
                sent[i - max(0, joint - 1)][...] = gone

    ins, keeps, sends = [place], [], []
    for terms, _ in streams:
        half, cols = terms[0].size // terms[0].shape[-1] // 2, terms[0].shape[-1]
        ins += [term.reshape(2, half, cols) for term in terms]
        keeps.append(((half, cols), f32))
        sends.append(((half, cols), bf16))
    if joint:
        sends = [((joint, *sends[0][0]), bf16), *sends[joint:]]
    done = call(kernel, ins, keeps + sends, waits=waits, flops=1e8, mib=8)
    return done[:n], done[n:]


def halved_joint(place, keeps, got, labels, joint=True, waits=()):
    n = len(keeps)
    half, cols = keeps[0].shape[0] // 2, keeps[0].shape[1]

    def kernel(place_ref, *refs):
        for i in range(n):
            mine = place_ref[spot(labels[i])]
            kept = refs[i][mine] + refs[n][i, mine].astype(f32)
            gone = refs[i][1 - mine] + refs[n][i, 1 - mine].astype(f32)
            refs[n + 1 + i][...] = kept
            if joint:
                refs[2 * n + 1][i] = gone.astype(bf16)
            else:
                refs[2 * n + 1 + i][...] = gone.astype(bf16)

    ins = [place, *[keep.reshape(2, half, cols) for keep in keeps], got.reshape(n, 2, half, cols)]
    sends = [((n, half, cols), bf16)] if joint else [((half, cols), bf16)] * n
    done = call(kernel, ins, [((half, cols), f32)] * n + sends, waits=waits, flops=1e8, mib=8)
    return done[:n], done[n:]


def halved_norm(place, keeps, gots, labels, norms, joint, waits=()):
    rows, cols = keeps[0].shape
    half, extra = rows // 2, norms[0].shape[0]
    n = len(gots)

    def kernel(place_ref, *refs):
        keep, got, norm, outs = refs[:2], refs[2 : 2 + n], refs[2 + n : -5 if not joint else -4], refs[-5 if not joint else -4 :]
        arrived = [(got[0], 0), (got[-1], 0 if n == 2 else rows)]
        for i in range(2):
            mine = place_ref[spot(labels[i])]
            ref, at = arrived[i]
            here = keep[i][pl.ds(pl.multiple_of(mine * half, half), half)].astype(f32)
            there = keep[i][pl.ds(pl.multiple_of((1 - mine) * half, half), half)].astype(f32)
            here += ref[pl.ds(pl.multiple_of(at + mine * half, half), half)].astype(f32)
            there += ref[pl.ds(pl.multiple_of(at + (1 - mine) * half, half), half)].astype(f32)
            outs[i][...] = here
            if joint:
                outs[3][i * half : (i + 1) * half] = there.astype(bf16)
            else:
                outs[3 + i][:half] = there.astype(bf16)
        if len(norm) == 2:
            value = norm[0][...] + norm[1][...]
        else:
            ref, at = arrived[1]
            value = joined_norm(norm[0][...], ref[at + rows : at + rows + 2 * extra])
        outs[2][...] = value
        split_norm(value, outs[-1], 2 * half if joint else half)

    small = [((half, cols), f32)] * 2 + [((extra, cols), f32)]
    if joint:
        sends = [((2 * half + 2 * extra, cols), bf16)]
    else:
        sends = [((half, cols), bf16), ((half + 2 * extra, cols), bf16)]
    done = call(kernel, (place, *keeps, *gots, *norms), small + sends, waits=waits, flops=1e8, mib=8)
    return done[:2], done[2], done[3:]


def split_norm(value, ref, at):
    rows = value.shape[0]
    high = value.astype(bf16)
    ref[at : at + rows] = high
    ref[at + rows : at + 2 * rows] = (value - high.astype(f32)).astype(bf16)


def joined_norm(value, got):
    rows = value.shape[0]
    high = value.astype(bf16).astype(f32)
    low = (value - high).astype(bf16).astype(f32)
    return (high + low) + (got[:rows].astype(f32) + got[rows:].astype(f32))


def total(terms):
    terms = [term.astype(f32) for term in terms]
    return functools.reduce(jnp.add, terms)


def write_update(outs, at, gradient, states, rate):
    values = advance(*states[:1], gradient, *states[1:], rate)
    for out, value in zip(outs, (gradient, *values)):
        out[at] = value
    if len(outs) > 4:
        outs[4][at] = values[2].astype(bf16)


def update_feed_kernel(keep_e, keep_r, got_ref, *refs):
    states, outs = refs[:6], refs[6:]
    for i, keep in enumerate((keep_e, keep_r)):
        gradient = keep[...] + got_ref[i].astype(f32)
        state = [ref[...] for ref in states[3 * i : 3 * i + 3]]
        write_update(outs[5 * i : 5 * i + 5], slice(None), gradient, state, matrix_rate)


def update_rest_kernel(keep_a, keep_b, got_ref, norm_ref, *refs):
    states, outs = refs[:9], refs[9:]
    rows, cols = keep_a.shape
    r, extra = rows // 2, norm_ref.shape[0]
    for i in range(4):
        keep = (keep_a, keep_b)[i // 2]
        at = (i % 2) * r
        gradient = keep[at : at + r] + got_ref[i * r : (i + 1) * r].astype(f32)
        which, entry = (0, i) if i < 3 else (1, slice(None))
        state = [ref[entry] for ref in states[3 * which : 3 * which + 3]]
        write_update(outs[5 * which : 5 * which + 5], entry, gradient, state, matrix_rate)
    value = joined_norm(norm_ref[...], got_ref[2 * rows : 2 * rows + 2 * extra])
    for j in range(extra // 4):
        at = (slice(None), slice(j * cols, (j + 1) * cols))
        state = [ref[at] for ref in states[6:]]
        write_update(outs[10:], at, value[4 * j : 4 * j + 4], state, norm_rate)


def advance(weight, gradient, moment, average, rate):
    momentum = momentum_decay * moment + gradient
    updated = weight - rate * (gradient + momentum_decay * momentum)
    smoothed = average_decay * average + (1.0 - average_decay) * updated
    return (momentum, smoothed, updated)


def on_device(
    frames,
    cotangent,
    lengths,
    weight_project,
    weight_combine,
    weight_expand,
    weight_reduce,
    moment_project,
    moment_combine,
    moment_expand,
    moment_reduce,
    average_project,
    average_combine,
    average_expand,
    average_reduce,
    norm_params,
    norm_moment,
    norm_average,
):
    own, batch, width = frames.shape
    long, rows = own + 2 * HALO, own + HALO
    parts, n_dp = lax.axis_size("mp"), lax.axis_size("dp")
    me = lax.axis_index("mp")
    start = me * own
    cols, hidden = width // parts, weight_expand.shape[1]
    r = width // n_dp

    sides = [side(label) for label in (ROW, NEAR, *far())]
    place = jnp.concatenate(
        [jnp.stack([start, side(CORE)]).astype(jnp.int32), lengths, jnp.stack(sides).astype(jnp.int32)]
    )
    *outer, last = reversed(far())

    matrices = jnp.concatenate([weight_project, weight_combine[None]], axis=0).astype(bf16)
    one = matrices.reshape(-1, cols)
    for label in outer:
        (one,) = paired(place, [(one, swap(one, *label), label, 1)])
    one_got = swap(one, *last)

    two = lowered([weight_expand, weight_reduce], waits=(one,))
    one_a, one_b = paired(place, [(one, one_got, last, 2)])
    frames_u = jnp.transpose(frames, (1, 0, 2))
    cotangent_u = jnp.transpose(cotangent, (1, 0, 2))
    strip = ((2, batch, HALO, width), bf16)
    near, over = call(
        edge_kernel,
        (place, frames_u, cotangent_u),
        [strip] * 2,
        waits=(one_got,),
        flops=1e8,
        mib=8,
    )
    near = swap(near, *CORE)
    pairs = [(i, i + 1) for i in range(1, parts - 1, 2)]
    over = lax.ppermute(over, "mp", pairs + [(b, a) for a, b in pairs])
    frames_x = call(
        frames_kernel, (place, frames_u, near, over), [((long, width), bf16)] * 2, flops=1e8, mib=8
    )
    got_a, got_b = swap(one_a, *ROW), swap(one_b, *NEAR)
    for label in outer:
        (two,) = paired(place, [(two, swap(two, *label), label, 1)])
    one_a, one_b = paired(
        place, [(one_a, got_a, ROW, 1), (one_b, got_b, NEAR, 1)], waits=(two,)
    )
    got_a, got_b = swap(one_a, *NEAR), swap(one_b, *ROW)
    two_a, two_b = paired(place, [(two, swap(two, *last), last, 2)])
    one_a, one_b = paired(
        place, [(one_a, got_a, NEAR, 1), (one_b, got_b, ROW, 1)], waits=(two_a, *frames_x)
    )
    core_a, core_b = swap(one_a, *CORE), swap(one_b, *CORE)

    per_u = [
        ((long, 3 * width), bf16),
        ((-(-rows // QUERIES), GROUP, QUERIES, width // LANES * KEYS), f32),
        ((own, width), bf16),
        ((rows, width), bf16),
        ((rows, width), f32),
        ((rows, width), bf16),
        ((width, own), bf16),
    ]
    qkv_0, probs_0, first_0, mixed_0, residual_0, second_0, second_t_0, wp, wc = call(
        functools.partial(attend_first_kernel, n_dp),
        (place, frames_x[0], norm_params, one_a, one_b, core_a, core_b),
        per_u + [((width, 3 * width), bf16), ((width, width), bf16)],
        flops=5e9,
    )
    seed, seed_t = call(
        seed_kernel,
        (place, cotangent_u, near, over),
        [((batch, rows, width), bf16), ((width, batch * own), bf16)],
        waits=(second_0,),
        flops=1e8,
        mib=8,
    )

    got_a, got_b = swap(two_a, *ROW), swap(two_b, *NEAR)
    two_a, two_b = paired(place, [(two_a, got_a, ROW, 1), (two_b, got_b, NEAR, 1)], waits=(seed,))
    qkv_1, probs_1, first_1, mixed_1, residual_1, second_1, second_t_1 = call(
        attend_next_kernel,
        (place, frames_x[1], norm_params, wp, wc),
        per_u,
        flops=5e9,
    )
    got_a, got_b = swap(two_a, *NEAR), swap(two_b, *ROW)
    expand, reduce_w = paired(
        place, [(two_a, got_a, NEAR, 1), (two_b, got_b, ROW, 1)], waits=(second_1,)
    )
    expand_got, reduce_got = swap(expand, *CORE), swap(reduce_w, *CORE)

    grads = [((2 * width, hidden), bf16)] * 2
    carried = [((batch, own, width), f32), ((batch, rows, width), f32)]
    feed_scratch = [((width, 2 * hidden), bf16)] * 2 + [
        ((batch * own, 2 * hidden), bf16),
        ((batch, rows, 2 * hidden), bf16),
        ((batch, rows, width), bf16),
    ]
    transposed = (seed_t, second_t_0, second_t_1)
    fed, back, keep_e, keep_r = call(
        functools.partial(feed_first_kernel, n_dp),
        (expand, reduce_w, second_0, seed, second_1, *transposed),
        carried + grads,
        feed_scratch,
        flops=8e9,
        smem=0,
    )
    layer, back, send_e, send_r = call(
        functools.partial(feed_last_kernel, n_dp),
        (expand_got, reduce_got, second_0, seed, fed, back, second_1, residual_0, residual_1, *transposed),
        [((batch, own, width), bf16), carried[1]] + grads,
        feed_scratch,
        flops=8e9,
        smem=0,
    )

    two_a, two_b = [keep_e, swap(send_e, *CORE)], [keep_r, swap(send_r, *CORE)]
    pulled = [((own, width), f32), ((own, width), bf16), ((own, 3 * width), bf16), ((2, width), f32)]
    pull_scratch = [((long, 2 * width), f32), ((rows, width), bf16)]
    wide_0, low_0, grad_0, norm_0 = call(
        pull_first_kernel,
        (back, residual_0, seed, wc, norm_params, qkv_0, probs_0),
        pulled,
        pull_scratch,
        flops=8e9,
        smem=0,
    )
    (keep_e, keep_r), (send_e, send_r) = halved(place, [(two_a, NEAR), (two_b, ROW)], waits=(grad_0,))
    two_a, two_b = [keep_e, swap(send_e, *NEAR)], [keep_r, swap(send_r, *ROW)]
    wide_1, low_1, grad_1, norm_1, keep_a, keep_b, send_a, send_b = call(
        functools.partial(pull_last_kernel, n_dp),
        (
            place, back, residual_1, seed, wc, norm_params, qkv_1, probs_1,
            first_0, first_1, mixed_0, mixed_1, grad_0, low_0,
        ),
        pulled + [((4 * width, cols), bf16)] * 4,
        pull_scratch,
        waits=(send_e,),
        flops=10e9,
    )
    one_a, one_b = [keep_a, swap(send_a, *CORE)], [keep_b, swap(send_b, *CORE)]
    first, *others = far()
    (keep_e, keep_r), (sent,) = halved(
        place, [(two_a, first), (two_b, first)], joint=2, waits=(keep_a,)
    )
    (keep_a, keep_b), (send_a, send_b) = halved(place, [(one_a, NEAR), (one_b, ROW)], waits=(sent,))
    gots = swap(send_a, *NEAR), swap(send_b, *ROW)
    two_got = swap(sent, *first)
    grad_in_0, grad_in_1, norm = call(
        finish_kernel,
        (norm_params, wp, grad_0, frames_x[0], wide_0, grad_1, frames_x[1], wide_1, norm_0, norm_1),
        [((own, width), f32), ((own, width), f32), ((4 * parts, cols), f32)],
        waits=(send_a,),
        flops=3e9,
        smem=0,
    )
    norm = norm + swap(norm, *CORE)
    norms = (norm, swap(norm, *ROW))
    (keep_a, keep_b), norm, (send_a, send_b) = halved_norm(
        place, (keep_a, keep_b), gots, (ROW, NEAR), norms, False
    )
    gots = swap(send_a, *ROW), swap(send_b, *NEAR)
    (keep_e, keep_r), (send_e, send_r) = halved_joint(
        place, (keep_e, keep_r), two_got, (ROW, NEAR), joint=False, waits=(send_a,)
    )
    two_a, two_b = [keep_e, swap(send_e, *ROW)], [keep_r, swap(send_r, *NEAR)]
    pending = (send_e,)
    second, *others = others
    (keep_e, keep_r), (sent,) = halved(place, [(two_a, second), (two_b, second)], joint=2)
    two_got = swap(sent, *second)
    for label in others:
        (keep_e, keep_r), (sent,) = halved_joint(place, (keep_e, keep_r), two_got, (label, label))
        two_got = swap(sent, *label)
    for label in far():
        (keep_a, keep_b), norm, (sent,) = halved_norm(
            place, (keep_a, keep_b), gots, (label, label), (norm,), True, waits=pending
        )
        gots, pending = (swap(sent, *label),), ()

    plain = lambda x: [(x.shape, f32)] * 4
    weighed = lambda x: plain(x) + [(x.shape, bf16)]
    updated = call(
        update_feed_kernel,
        (
            keep_e, keep_r, two_got, weight_expand, moment_expand, average_expand,
            weight_reduce, moment_reduce, average_reduce,
        ),
        weighed(weight_expand) + weighed(weight_reduce),
        flops=1e8,
        smem=0,
        mib=8,
    )
    gradient_expand, mom_expand, avg_expand, new_expand, low_expand = updated[:5]
    gradient_reduce, mom_reduce, avg_reduce, new_reduce, low_reduce = updated[5:]
    updated = call(
        update_rest_kernel,
        (
            keep_a, keep_b, gots[0], norm, weight_project, moment_project, average_project,
            weight_combine, moment_combine, average_combine, norm_params, norm_moment, norm_average,
        ),
        weighed(weight_project) + weighed(weight_combine) + plain(norm_params),
        flops=1e8,
        smem=0,
        mib=8,
    )
    gradient_project, mom_project, avg_project, new_project, low_project = updated[:5]
    gradient_combine, mom_combine, avg_combine, new_combine, low_combine = updated[5:10]
    norm_gradient, mom_norms, avg_norms, new_norms = updated[10:]
    layer_out = jnp.transpose(layer, (1, 0, 2))
    input_gradient = jnp.transpose(jnp.stack([grad_in_0, grad_in_1]), (1, 0, 2))
    return (
        layer_out,
        input_gradient,
        gradient_project,
        gradient_combine,
        gradient_expand,
        gradient_reduce,
        mom_project,
        mom_combine,
        mom_expand,
        mom_reduce,
        avg_project,
        avg_combine,
        avg_expand,
        avg_reduce,
        new_project,
        new_combine,
        new_expand,
        new_reduce,
        low_project,
        low_combine,
        low_expand,
        low_reduce,
        norm_gradient,
        mom_norms,
        avg_norms,
        new_norms,
    )


def solution(mesh):
    tokens = P("mp", "dp", None)
    stacked, matrix = P(None, "dp", "mp"), P("dp", "mp")
    weights = (stacked, matrix, matrix, matrix)
    in_specs = (tokens, tokens, P("dp")) + weights * 3 + (P(),) * 3
    out_specs = (tokens, tokens) + weights * 5 + (P(),) * 4
    return jax.shard_map(
        on_device, mesh=mesh, in_specs=in_specs, out_specs=out_specs, check_vma=False
    )
```

profile of v0, /device:TPU:0, one launch (start us, length us, event | category | flops | bytes accessed | tf_op | source)
XLA Modules:
  0.0 137.8 jit_solution(6098220298428175475)
XLA Ops:
  1.6 4.1 %collective-permute-start = (bf16[256,128]{1,0:T(8,128)(2,1)S(1)}, bf16[256,128]{1,0:T(8,128)(2,1)S(1)}, u32[]{:S(2)}, u32[]{:S(2)}) collective-permute-start(bf16[256,128]{1,0:T(8,128)(2,1)S(1)} %bitcast.132), channel_id=1, source_target_pairs={{0,16},{4,20},{8,24},{12,28},{16,0},{20,4},{24,8},{28,12},{1,17},{... | collective-permute-start | bytes 196616 | tf_op jit(solution)/shard_map/ppermute | solution.py:436
  6.4 2.9 %collective-permute-done = bf16[256,128]{1,0:T(8,128)(2,1)S(1)} collective-permute-done((bf16[256,128]{1,0:T(8,128)(2,1)S(1)}, bf16[256,128]{1,0:T(8,128)(2,1)S(1)}, u32[]{:S(2)}, u32[]{:S(2)}) %collective-permute-start) | collective-permute-done | bytes 65568 | tf_op jit(solution)/shard_map/ppermute | solution.py:436
  12.4 3.4 %collective-permute-start.1 = (bf16[128,512]{1,0:T(8,128)(2,1)S(1)}, bf16[128,512]{1,0:T(8,128)(2,1)S(1)}, u32[]{:S(2)}, u32[]{:S(2)}) collective-permute-start(bf16[128,512]{1,0:T(8,128)(2,1)S(1)} %shard_map.378), channel_id=1, source_target_pairs={{0,16},{4,20},{8,24},{12,28},{16,0},{20,4},{24,8},{28,12},{1,17},{... | collective-permute-start | bytes 393224 | tf_op jit(solution)/shard_map/ppermute | solution.py:436
  16.4 1.6 %collective-permute-start.9 = (bf16[512,128]{1,0:T(8,128)(2,1)S(1)}, bf16[512,128]{1,0:T(8,128)(2,1)S(1)}, u32[]{:S(2)}, u32[]{:S(2)}) collective-permute-start(bf16[512,128]{1,0:T(8,128)(2,1)S(1)} %bitcast.125), channel_id=1, source_target_pairs={{0,4},{4,0},{8,12},{12,8},{16,20},{20,16},{24,28},{28,24},{1,5},{5... | collective-permute-start | bytes 393224 | tf_op jit(solution)/shard_map/ppermute | solution.py:436
  17.9 1.5 %collective-permute-start.8 = (bf16[512,128]{1,0:T(8,128)(2,1)S(1)}, bf16[512,128]{1,0:T(8,128)(2,1)S(1)}, u32[]{:S(2)}, u32[]{:S(2)}) collective-permute-start(bf16[512,128]{1,0:T(8,128)(2,1)S(1)} %bitcast.123), channel_id=1, source_target_pairs={{0,2},{1,3},{2,0},{3,1},{4,6},{5,7},{6,4},{7,5},{8,10},{9,11},{10,... | collective-permute-start | bytes 393224 | tf_op jit(solution)/shard_map/ppermute | solution.py:436
  19.5 2.1 %collective-permute-done.1 = bf16[128,512]{1,0:T(8,128)(2,1)S(1)} collective-permute-done((bf16[128,512]{1,0:T(8,128)(2,1)S(1)}, bf16[128,512]{1,0:T(8,128)(2,1)S(1)}, u32[]{:S(2)}, u32[]{:S(2)}) %collective-permute-start.1) | collective-permute-done | bytes 131104 | tf_op jit(solution)/shard_map/ppermute | solution.py:436
  23.5 1.6 %collective-permute-start.11 = (bf16[1024,128]{1,0:T(8,128)(2,1)S(1)}, bf16[1024,128]{1,0:T(8,128)(2,1)S(1)}, u32[]{:S(2)}, u32[]{:S(2)}) collective-permute-start(bf16[1024,128]{1,0:T(8,128)(2,1)S(1)} %bitcast.114), channel_id=1, source_target_pairs={{0,2},{1,3},{2,0},{3,1},{4,6},{5,7},{6,4},{7,5},{8,10},{9,11},{10,... | collective-permute-start | bytes 786440 | tf_op jit(solution)/shard_map/ppermute | solution.py:436
  30.5 1.2 collective-permute-done.10
  32.4 2.5 %collective-permute-start.13 = (bf16[2048,128]{1,0:T(8,128)(2,1)S(1)}, bf16[2048,128]{1,0:T(8,128)(2,1)S(1)}, u32[]{:S(2)}, u32[]{:S(2)}) collective-permute-start(bf16[2048,128]{1,0:T(8,128)(2,1)S(1)} %bitcast.140), channel_id=1, source_target_pairs={{0,1},{1,0},{2,3},{3,2},{4,5},{5,4},{6,7},{7,6},{8,9},{9,8},{10,11... | collective-permute-start | bytes 1572872 | tf_op jit(solution)/shard_map/ppermute | solution.py:436
  35.4 1.2 collective-permute-start.4
  37.2 6.4 %shard_map.386 = (bf16[544,1536]{1,0:T(8,128)(2,1)S(1)}, f32[5,4,112,256]{3,2,1,0:T(8,128)S(1)}, bf16[512,512]{1,0:T(8,128)(2,1)S(1)}, bf16[528,512]{1,0:T(8,128...) custom-call(s32[8]{0:T(128)S(1)} %concatenate.6.refs_0_, ...), custom_call_target="tpu_custom_call" | custom-call | flops 5000000000 | bytes 6000000 | tf_op jit(solution)/shard_map/pallas_call | solution.py:423
  47.3 6.0 %shard_map.389 = (bf16[544,1536]{1,0:T(8,128)(2,1)S(1)}, f32[5,4,112,256]{3,2,1,0:T(8,128)S(1)}, bf16[512,512]{1,0:T(8,128)(2,1)S(1)}, bf16[528,512]{1,0:T(8,128...) custom-call(s32[8]{0:T(128)S(1)} %concatenate.6.refs_0_, ...), custom_call_target="tpu_custom_call" | custom-call | flops 5000000000 | bytes 6000000 | tf_op jit(solution)/shard_map/pallas_call | solution.py:423
  53.3 6.1 %collective-permute-done.15 = bf16[512,512]{1,0:T(8,128)(2,1)S(1)} collective-permute-done((bf16[512,512]{1,0:T(8,128)(2,1)S(1)}, bf16[512,512]{1,0:T(8,128)(2,1)S(1)}, u32[]{:S(2)}, u32[]{:S(2)}) %collective-permute-start.15) | collective-permute-done | bytes 524320 | tf_op jit(solution)/shard_map/ppermute | solution.py:436
  61.0 9.0 %shard_map.391 = (f32[2,512,512]{2,1,0:T(8,128)S(1)}, f32[2,528,512]{2,1,0:T(8,128)S(1)}, bf16[1024,512]{1,0:T(8,128)(2,1)S(1)}, bf16[1024,512]{1,0:T(8,128)(2,1)S(1)}) custom-call(bf16[1024,512]{1,0:T(8,128)(2,1)S(1)} %bitcast.135, bf16[1024,512]{1,0:T(8,128)(2,1)S(1)} %bitcast.137, bf16[528,512]{1,0:T(8,128)(2,1)S(1)} %get-tuple-element.149.refs_4_.refs_2_, ...), custom_call_target="tpu_custom_call" | custom-call | flops 8000000000 | bytes 6000000 | tf_op jit(solution)/shard_map/pallas_call | solution.py:423
  70.0 9.4 %shard_map.392 = (bf16[2,512,512]{2,1,0:T(8,128)(2,1)S(1)}, f32[2,528,512]{2,1,0:T(8,128)S(1)}, bf16[1024,512]{1,0:T(8,128)(2,1)S(1)}, bf16[1024,512]{1,0:T(8,128)(2,1)S(1)}) custom-call(bf16[1024,512]{1,0:T(8,128)(2,1)S(1)} %collective-permute-done.16.refs_0_, bf16[1024,512]{1,0:T(8,128)(2,1)S(1)} %collective-permute-done.17.refs_1_, ...), custom_call_target="tpu_custom_call" | custom-call | flops 8000000000 | bytes 6000000 | tf_op jit(solution)/shard_map/pallas_call | solution.py:423
  80.0 5.6 %shard_map.393 = (f32[512,512]{1,0:T(8,128)S(1)}, bf16[512,512]{1,0:T(8,128)(2,1)S(1)}, bf16[512,1536]{1,0:T(8,128)(2,1)S(1)}, f32[2,512]{1,0:T(2,128)S(1)}) custom-call(f32[2,528,512]{2,1,0:T(8,128)S(1)} %get-tuple-element.166.refs_0_.refs_1_, f32[528,512]{1,0:T(8,128)S(1)} %get-tuple-element.163.refs_7_.refs_1_, ...), custom_call_target="tpu_custom_call" | custom-call | flops 8000000000 | bytes 6000000 | tf_op jit(solution)/shard_map/pallas_call | solution.py:423
  86.7 1.5 %collective-permute-start.23 = (bf16[512,512]{1,0:T(8,128)(2,1)S(1)}, bf16[512,512]{1,0:T(8,128)(2,1)S(1)}, u32[]{:S(2)}, u32[]{:S(2)}) collective-permute-start(bf16[512,512]{1,0:T(8,128)(2,1)S(1)} %get-tuple-element.193), channel_id=1, source_target_pairs={{0,2},{1,3},{2,0},{3,1},{4,6},{5,7},{6,4},{7,5},{8,10},{9,11},{10,... | collective-permute-start | bytes 1572872 | tf_op jit(solution)/shard_map/ppermute | solution.py:436
  88.2 1.3 collective-permute-start.22
  89.4 8.9 %shard_map.395 = (f32[512,512]{1,0:T(8,128)S(1)}, bf16[512,512]{1,0:T(8,128)(2,1)}, bf16[512,1536]{1,0:T(8,128)(2,1)S(1)}, f32[2,512]{1,0:T(2,128)S(1)}, bf16[20...) custom-call(s32[8]{0:T(128)S(1)} %concatenate.6.refs_0_, ...), custom_call_target="tpu_custom_call" | custom-call | flops 10000000000 | bytes 6000000 | tf_op jit(solution)/shard_map/pallas_call | solution.py:423
  98.8 1.8 %collective-permute-done.23 = bf16[512,512]{1,0:T(8,128)(2,1)S(1)} collective-permute-done((bf16[512,512]{1,0:T(8,128)(2,1)S(1)}, bf16[512,512]{1,0:T(8,128)(2,1)S(1)}, u32[]{:S(2)}, u32[]{:S(2)}) %collective-permute-start.23) | collective-permute-done | bytes 524320 | tf_op jit(solution)/shard_map/ppermute | solution.py:436
  100.6 1.2 collective-permute-done.22
  102.6 2.1 %collective-permute-start.30 = (bf16[2,256,512]{2,1,0:T(8,128)(2,1)S(1)}, bf16[2,256,512]{2,1,0:T(8,128)(2,1)S(1)}, u32[]{:S(2)}, u32[]{:S(2)}) collective-permute-start(bf16[2,256,512]{2,1,0:T(8,128)(2,1)S(1)} %get-tuple-element.194.refs_5_), channel_id=1, source_target_pairs={{0,8},{4,12},{8,0},{12,4},{16,24},{20,28},{24,16},{28,20},{1,9},{5... | collective-permute-start | bytes 1572872 | tf_op jit(solution)/shard_map/ppermute | solution.py:436
  106.8 2.6 %shard_map.398 = (f32[512,512]{1,0:T(8,128)S(1)}, f32[512,512]{1,0:T(8,128)S(1)}, f32[16,128]{1,0:T(8,128)S(1)}) custom-call(f32[4,512]{1,0:T(4,128)S(1)} %copy-done.14, bf16[512,1536]{1,0:T(8,128)(2,1)S(1)} %get-tuple-element.153.refs_3_.refs_1_, bf16[512,1536]{1,0:T(8,128)(2,1)S(1)} %get-tuple-element.169.refs_5_.refs_12_.refs_2_, ...), custom_call_target="tpu_custom_call" | custom-call | flops 3000000000 | bytes 6000000 | tf_op jit(solution)/shard_map/pallas_call | solution.py:423
  109.6 1.2 collective-permute-done.26
  110.7 1.2 collective-permute-start.27
  111.9 2.5 %collective-permute-done.27.refs_6_ = f32[16,128]{1,0:T(8,128)S(1)} collective-permute-done((f32[16,128]{1,0:T(8,128)S(1)}, f32[16,128]{1,0:T(8,128)S(1)}, u32[]{:S(2)}, u32[]{:S(2)}) %collective-permute-start.27) | collective-permute-done | bytes 8224 | tf_op jit(solution)/shard_map/ppermute | solution.py:436
  116.1 1.7 %collective-permute-start.28 = (bf16[512,128]{1,0:T(8,128)(2,1)S(1)}, bf16[512,128]{1,0:T(8,128)(2,1)S(1)}, u32[]{:S(2)}, u32[]{:S(2)}) collective-permute-start(bf16[512,128]{1,0:T(8,128)(2,1)S(1)} %get-tuple-element.204.refs_4_), channel_id=1, source_target_pairs={{0,2},{1,3},{2,0},{3,1},{4,6},{5,7},{6,4},{7,5},{8,10},{9,11},{10,... | collective-permute-start | bytes 393224 | tf_op jit(solution)/shard_map/ppermute | solution.py:436
  119.9 2.3 %collective-permute-done.28.refs_3_ = bf16[512,128]{1,0:T(8,128)(2,1)S(1)} collective-permute-done((bf16[512,128]{1,0:T(8,128)(2,1)S(1)}, bf16[512,128]{1,0:T(8,128)(2,1)S(1)}, u32[]{:S(2)}, u32[]{:S(2)}) %collective-permute-start.28) | collective-permute-done | bytes 131104 | tf_op jit(solution)/shard_map/ppermute | solution.py:436
  122.9 2.0 %copy.46 = bf16[512,2,512]{2,1,0:T(2,128)(2,1)} copy(bf16[512,2,512]{2,0,1:T(8,128)(2,1)S(1)} %bitcast.78) | data formatting | bytes 2097152
  125.5 3.2 %collective-permute-start.35 = (bf16[2,64,512]{2,1,0:T(8,128)(2,1)S(1)}, bf16[2,64,512]{2,1,0:T(8,128)(2,1)S(1)}, u32[]{:S(2)}, u32[]{:S(2)}) collective-permute-start(bf16[2,64,512]{2,1,0:T(8,128)(2,1)S(1)} %get-tuple-element.225), channel_id=1, source_target_pairs={{0,16},{4,20},{8,24},{12,28},{16,0},{20,4},{24,8},{28,12},{1,17},{... | collective-permute-start | bytes 393224 | tf_op jit(solution)/shard_map/ppermute | solution.py:436
  131.2 2.9 %copy.47 = f32[512,2,512]{2,1,0:T(2,128)} copy(f32[512,2,512]{2,0,1:T(8,128)S(1)} %maximum_bitcast_fusion) | data formatting | bytes 4194304
  134.1 1.6 %collective-permute-done.32.refs_2_ = bf16[288,128]{1,0:T(8,128)(2,1)S(1)} collective-permute-done((bf16[288,128]{1,0:T(8,128)(2,1)S(1)}, bf16[288,128]{1,0:T(8,128)(2,1)S(1)}, u32[]{:S(2)}, u32[]{:S(2)}) %collective-permute-start.32) | collective-permute-done | bytes 73760 | tf_op jit(solution)/shard_map/ppermute | solution.py:436
  (114 shorter events, 34.0 us)
Async XLA Ops:
  1.6 7.8 %collective-permute-start = (bf16[256,128]{1,0:T(8,128)(2,1)S(1)}, bf16[256,128]{1,0:T(8,128)(2,1)S(1)}, u32[]{:S(2)}, u32[]{:S(2)}) collective-permute-start(bf16[256,128]{1,0:T(8,128)(2,1)S(1)} %bitcast.132), channel_id=1, source_target_pairs={{0,16},{4,20},{8,24},{12,28},{16,0},{20,4},{24,8},{28,12},{1,17},{... | collective-permute-start | bytes 196616 | tf_op jit(solution)/shard_map/ppermute | solution.py:436
  9.9 5.9 %collective-permute-start.5 = (bf16[512,128]{1,0:T(8,128)(2,1)S(1)}, bf16[512,128]{1,0:T(8,128)(2,1)S(1)}, u32[]{:S(2)}, u32[]{:S(2)}) collective-permute-start(bf16[512,128]{1,0:T(8,128)(2,1)S(1)} %bitcast.129), channel_id=1, source_target_pairs={{0,8},{4,12},{8,0},{12,4},{16,24},{20,28},{24,16},{28,20},{1,9},{5... | collective-permute-start | bytes 393224 | tf_op jit(solution)/shard_map/ppermute | solution.py:436
  12.4 9.2 %collective-permute-start.1 = (bf16[128,512]{1,0:T(8,128)(2,1)S(1)}, bf16[128,512]{1,0:T(8,128)(2,1)S(1)}, u32[]{:S(2)}, u32[]{:S(2)}) collective-permute-start(bf16[128,512]{1,0:T(8,128)(2,1)S(1)} %shard_map.378), channel_id=1, source_target_pairs={{0,16},{4,20},{8,24},{12,28},{16,0},{20,4},{24,8},{28,12},{1,17},{... | collective-permute-start | bytes 393224 | tf_op jit(solution)/shard_map/ppermute | solution.py:436
  16.4 5.8 %collective-permute-start.9 = (bf16[512,128]{1,0:T(8,128)(2,1)S(1)}, bf16[512,128]{1,0:T(8,128)(2,1)S(1)}, u32[]{:S(2)}, u32[]{:S(2)}) collective-permute-start(bf16[512,128]{1,0:T(8,128)(2,1)S(1)} %bitcast.125), channel_id=1, source_target_pairs={{0,4},{4,0},{8,12},{12,8},{16,20},{20,16},{24,28},{28,24},{1,5},{5... | collective-permute-start | bytes 393224 | tf_op jit(solution)/shard_map/ppermute | solution.py:436
  17.9 5.0 %collective-permute-start.8 = (bf16[512,128]{1,0:T(8,128)(2,1)S(1)}, bf16[512,128]{1,0:T(8,128)(2,1)S(1)}, u32[]{:S(2)}, u32[]{:S(2)}) collective-permute-start(bf16[512,128]{1,0:T(8,128)(2,1)S(1)} %bitcast.123), channel_id=1, source_target_pairs={{0,2},{1,3},{2,0},{3,1},{4,6},{5,7},{6,4},{7,5},{8,10},{9,11},{10,... | collective-permute-start | bytes 393224 | tf_op jit(solution)/shard_map/ppermute | solution.py:436
  22.1 7.7 %collective-permute-start.2 = (bf16[256,512]{1,0:T(8,128)(2,1)S(1)}, bf16[256,512]{1,0:T(8,128)(2,1)S(1)}, u32[]{:S(2)}, u32[]{:S(2)}) collective-permute-start(bf16[256,512]{1,0:T(8,128)(2,1)S(1)} %bitcast.74), channel_id=1, source_target_pairs={{0,8},{4,12},{8,0},{12,4},{16,24},{20,28},{24,16},{28,20},{1,9},{5... | collective-permute-start | bytes 786440 | tf_op jit(solution)/shard_map/ppermute | solution.py:436
  23.5 7.0 %collective-permute-start.11 = (bf16[1024,128]{1,0:T(8,128)(2,1)S(1)}, bf16[1024,128]{1,0:T(8,128)(2,1)S(1)}, u32[]{:S(2)}, u32[]{:S(2)}) collective-permute-start(bf16[1024,128]{1,0:T(8,128)(2,1)S(1)} %bitcast.114), channel_id=1, source_target_pairs={{0,2},{1,3},{2,0},{3,1},{4,6},{5,7},{6,4},{7,5},{8,10},{9,11},{10,... | collective-permute-start | bytes 786440 | tf_op jit(solution)/shard_map/ppermute | solution.py:436
  25.1 6.6 %collective-permute-start.10 = (bf16[1024,128]{1,0:T(8,128)(2,1)S(1)}, bf16[1024,128]{1,0:T(8,128)(2,1)S(1)}, u32[]{:S(2)}, u32[]{:S(2)}) collective-permute-start(bf16[1024,128]{1,0:T(8,128)(2,1)S(1)} %bitcast.112), channel_id=1, source_target_pairs={{0,4},{4,0},{8,12},{12,8},{16,20},{20,16},{24,28},{28,24},{1,5},{5... | collective-permute-start | bytes 786440 | tf_op jit(solution)/shard_map/ppermute | solution.py:436
  32.4 4.3 %collective-permute-start.13 = (bf16[2048,128]{1,0:T(8,128)(2,1)S(1)}, bf16[2048,128]{1,0:T(8,128)(2,1)S(1)}, u32[]{:S(2)}, u32[]{:S(2)}) collective-permute-start(bf16[2048,128]{1,0:T(8,128)(2,1)S(1)} %bitcast.140), channel_id=1, source_target_pairs={{0,1},{1,0},{2,3},{3,2},{4,5},{5,4},{6,7},{7,6},{8,9},{9,8},{10,11... | collective-permute-start | bytes 1572872 | tf_op jit(solution)/shard_map/ppermute | solution.py:436
  35.0 9.6 %collective-permute-start.3 = (bf16[256,512]{1,0:T(8,128)(2,1)S(1)}, bf16[256,512]{1,0:T(8,128)(2,1)S(1)}, u32[]{:S(2)}, u32[]{:S(2)}) collective-permute-start(bf16[256,512]{1,0:T(8,128)(2,1)S(1)} %bitcast.88), channel_id=1, source_target_pairs={{0,2},{1,3},{2,0},{3,1},{4,6},{5,7},{6,4},{7,5},{8,10},{9,11},{10,... | collective-permute-start | bytes 786440 | tf_op jit(solution)/shard_map/ppermute | solution.py:436
  35.4 9.1 %collective-permute-start.4 = (bf16[256,512]{1,0:T(8,128)(2,1)S(1)}, bf16[256,512]{1,0:T(8,128)(2,1)S(1)}, u32[]{:S(2)}, u32[]{:S(2)}) collective-permute-start(bf16[256,512]{1,0:T(8,128)(2,1)S(1)} %bitcast.105), channel_id=1, source_target_pairs={{0,4},{4,0},{8,12},{12,8},{16,20},{20,16},{24,28},{28,24},{1,5},{5... | collective-permute-start | bytes 786440 | tf_op jit(solution)/shard_map/ppermute | solution.py:436
  45.2 14.3 %collective-permute-start.15 = (bf16[512,512]{1,0:T(8,128)(2,1)S(1)}, bf16[512,512]{1,0:T(8,128)(2,1)S(1)}, u32[]{:S(2)}, u32[]{:S(2)}) collective-permute-start(bf16[512,512]{1,0:T(8,128)(2,1)S(1)} %bitcast.101), channel_id=1, source_target_pairs={{0,2},{1,3},{2,0},{3,1},{4,6},{5,7},{6,4},{7,5},{8,10},{9,11},{10,... | collective-permute-start | bytes 1572872 | tf_op jit(solution)/shard_map/ppermute | solution.py:436
  46.3 13.4 %collective-permute-start.14 = (bf16[512,512]{1,0:T(8,128)(2,1)S(1)}, bf16[512,512]{1,0:T(8,128)(2,1)S(1)}, u32[]{:S(2)}, u32[]{:S(2)}) collective-permute-start(bf16[512,512]{1,0:T(8,128)(2,1)S(1)} %bitcast.99), channel_id=1, source_target_pairs={{0,4},{4,0},{8,12},{12,8},{16,20},{20,16},{24,28},{28,24},{1,5},{5... | collective-permute-start | bytes 1572872 | tf_op jit(solution)/shard_map/ppermute | solution.py:436
  60.4 9.6 %collective-permute-start.17 = (bf16[1024,512]{1,0:T(8,128)(2,1)S(1)}, bf16[1024,512]{1,0:T(8,128)(2,1)S(1)}, u32[]{:S(2)}, u32[]{:S(2)}) collective-permute-start(bf16[1024,512]{1,0:T(8,128)(2,1)S(1)} %bitcast.136), channel_id=1, source_target_pairs={{0,1},{1,0},{2,3},{3,2},{4,5},{5,4},{6,7},{7,6},{8,9},{9,8},{10,11... | collective-permute-start | bytes 3145736 | tf_op jit(solution)/shard_map/ppermute | solution.py:436
  60.5 9.5 %collective-permute-start.16 = (bf16[1024,512]{1,0:T(8,128)(2,1)S(1)}, bf16[1024,512]{1,0:T(8,128)(2,1)S(1)}, u32[]{:S(2)}, u32[]{:S(2)}) collective-permute-start(bf16[1024,512]{1,0:T(8,128)(2,1)S(1)} %bitcast.134), channel_id=1, source_target_pairs={{0,1},{1,0},{2,3},{3,2},{4,5},{5,4},{6,7},{7,6},{8,9},{9,8},{10,11... | collective-permute-start | bytes 3145736 | tf_op jit(solution)/shard_map/ppermute | solution.py:436
  79.4 6.2 %collective-permute-start.18 = (bf16[1024,512]{1,0:T(8,128)(2,1)S(1)}, bf16[1024,512]{1,0:T(8,128)(2,1)S(1)}, u32[]{:S(2)}, u32[]{:S(2)}) collective-permute-start(bf16[1024,512]{1,0:T(8,128)(2,1)S(1)} %get-tuple-element.179), channel_id=1, source_target_pairs={{0,1},{1,0},{2,3},{3,2},{4,5},{5,4},{6,7},{7,6},{8,9},{9,8},{10,11... | collective-permute-start | bytes 3145736 | tf_op jit(solution)/shard_map/ppermute | solution.py:436
  79.6 6.1 %collective-permute-start.19 = (bf16[1024,512]{1,0:T(8,128)(2,1)S(1)}, bf16[1024,512]{1,0:T(8,128)(2,1)S(1)}, u32[]{:S(2)}, u32[]{:S(2)}) collective-permute-start(bf16[1024,512]{1,0:T(8,128)(2,1)S(1)} %get-tuple-element.181), channel_id=1, source_target_pairs={{0,1},{1,0},{2,3},{3,2},{4,5},{5,4},{6,7},{7,6},{8,9},{9,8},{10,11... | collective-permute-start | bytes 3145736 | tf_op jit(solution)/shard_map/ppermute | solution.py:436
  86.7 14.0 %collective-permute-start.23 = (bf16[512,512]{1,0:T(8,128)(2,1)S(1)}, bf16[512,512]{1,0:T(8,128)(2,1)S(1)}, u32[]{:S(2)}, u32[]{:S(2)}) collective-permute-start(bf16[512,512]{1,0:T(8,128)(2,1)S(1)} %get-tuple-element.193), channel_id=1, source_target_pairs={{0,2},{1,3},{2,0},{3,1},{4,6},{5,7},{6,4},{7,5},{8,10},{9,11},{10,... | collective-permute-start | bytes 1572872 | tf_op jit(solution)/shard_map/ppermute | solution.py:436
  88.2 13.6 %collective-permute-start.22 = (bf16[512,512]{1,0:T(8,128)(2,1)S(1)}, bf16[512,512]{1,0:T(8,128)(2,1)S(1)}, u32[]{:S(2)}, u32[]{:S(2)}) collective-permute-start(bf16[512,512]{1,0:T(8,128)(2,1)S(1)} %get-tuple-element.182.refs_14_), channel_id=1, source_target_pairs={{0,4},{4,0},{8,12},{12,8},{16,20},{20,16},{24,28},{28,24},{1,5},{5... | collective-permute-start | bytes 1572872 | tf_op jit(solution)/shard_map/ppermute | solution.py:436
  98.3 6.3 %collective-permute-start.20 = (bf16[2048,128]{1,0:T(8,128)(2,1)S(1)}, bf16[2048,128]{1,0:T(8,128)(2,1)S(1)}, u32[]{:S(2)}, u32[]{:S(2)}) collective-permute-start(bf16[2048,128]{1,0:T(8,128)(2,1)S(1)} %get-tuple-element.188), channel_id=1, source_target_pairs={{0,1},{1,0},{2,3},{3,2},{4,5},{5,4},{6,7},{7,6},{8,9},{9,8},{10,11... | collective-permute-start | bytes 1572872 | tf_op jit(solution)/shard_map/ppermute | solution.py:436
  98.3 6.3 %collective-permute-start.21 = (bf16[2048,128]{1,0:T(8,128)(2,1)S(1)}, bf16[2048,128]{1,0:T(8,128)(2,1)S(1)}, u32[]{:S(2)}, u32[]{:S(2)}) collective-permute-start(bf16[2048,128]{1,0:T(8,128)(2,1)S(1)} %get-tuple-element.190), channel_id=1, source_target_pairs={{0,1},{1,0},{2,3},{3,2},{4,5},{5,4},{6,7},{7,6},{8,9},{9,8},{10,11... | collective-permute-start | bytes 1572872 | tf_op jit(solution)/shard_map/ppermute | solution.py:436
  102.6 15.2 %collective-permute-start.30 = (bf16[2,256,512]{2,1,0:T(8,128)(2,1)S(1)}, bf16[2,256,512]{2,1,0:T(8,128)(2,1)S(1)}, u32[]{:S(2)}, u32[]{:S(2)}) collective-permute-start(bf16[2,256,512]{2,1,0:T(8,128)(2,1)S(1)} %get-tuple-element.194.refs_5_), channel_id=1, source_target_pairs={{0,8},{4,12},{8,0},{12,4},{16,24},{20,28},{24,16},{28,20},{1,9},{5... | collective-permute-start | bytes 1572872 | tf_op jit(solution)/shard_map/ppermute | solution.py:436
  105.4 9.0 %collective-permute-start.25 = (bf16[1024,128]{1,0:T(8,128)(2,1)S(1)}, bf16[1024,128]{1,0:T(8,128)(2,1)S(1)}, u32[]{:S(2)}, u32[]{:S(2)}) collective-permute-start(bf16[1024,128]{1,0:T(8,128)(2,1)S(1)} %get-tuple-element.200), channel_id=1, source_target_pairs={{0,2},{1,3},{2,0},{3,1},{4,6},{5,7},{6,4},{7,5},{8,10},{9,11},{10,... | collective-permute-start | bytes 786440 | tf_op jit(solution)/shard_map/ppermute | solution.py:436
  105.8 8.6 %collective-permute-start.24 = (bf16[1024,128]{1,0:T(8,128)(2,1)S(1)}, bf16[1024,128]{1,0:T(8,128)(2,1)S(1)}, u32[]{:S(2)}, u32[]{:S(2)}) collective-permute-start(bf16[1024,128]{1,0:T(8,128)(2,1)S(1)} %get-tuple-element.195.refs_10_), channel_id=1, source_target_pairs={{0,4},{4,0},{8,12},{12,8},{16,20},{20,16},{24,28},{28,24},{1,5},{5... | collective-permute-start | bytes 786440 | tf_op jit(solution)/shard_map/ppermute | solution.py:436
  110.7 3.7 %collective-permute-start.27 = (f32[16,128]{1,0:T(8,128)S(1)}, f32[16,128]{1,0:T(8,128)S(1)}, u32[]{:S(2)}, u32[]{:S(2)}) collective-permute-start(f32[16,128]{1,0:T(8,128)S(1)} %add.3.refs_5_), channel_id=1, source_target_pairs={{0,2},{1,3},{2,0},{3,1},{4,6},{5,7},{6,4},{7,5},{8,10},{9,11},{10,... | collective-permute-start | bytes 24584 | tf_op jit(solution)/shard_map/ppermute | solution.py:436
  115.1 7.1 %collective-permute-start.29 = (bf16[544,128]{1,0:T(8,128)(2,1)S(1)}, bf16[544,128]{1,0:T(8,128)(2,1)S(1)}, u32[]{:S(2)}, u32[]{:S(2)}) collective-permute-start(bf16[544,128]{1,0:T(8,128)(2,1)S(1)} %get-tuple-element.205), channel_id=1, source_target_pairs={{0,4},{4,0},{8,12},{12,8},{16,20},{20,16},{24,28},{28,24},{1,5},{5... | collective-permute-start | bytes 417800 | tf_op jit(solution)/shard_map/ppermute | solution.py:436
  116.1 6.1 %collective-permute-start.28 = (bf16[512,128]{1,0:T(8,128)(2,1)S(1)}, bf16[512,128]{1,0:T(8,128)(2,1)S(1)}, u32[]{:S(2)}, u32[]{:S(2)}) collective-permute-start(bf16[512,128]{1,0:T(8,128)(2,1)S(1)} %get-tuple-element.204.refs_4_), channel_id=1, source_target_pairs={{0,2},{1,3},{2,0},{3,1},{4,6},{5,7},{6,4},{7,5},{8,10},{9,11},{10,... | collective-permute-start | bytes 393224 | tf_op jit(solution)/shard_map/ppermute | solution.py:436
  118.4 6.5 %collective-permute-start.34 = (bf16[128,512]{1,0:T(8,128)(2,1)S(1)}, bf16[128,512]{1,0:T(8,128)(2,1)S(1)}, u32[]{:S(2)}, u32[]{:S(2)}) collective-permute-start(bf16[128,512]{1,0:T(8,128)(2,1)S(1)} %get-tuple-element.222), channel_id=1, source_target_pairs={{0,4},{4,0},{8,12},{12,8},{16,20},{20,16},{24,28},{28,24},{1,5},{5... | collective-permute-start | bytes 393224 | tf_op jit(solution)/shard_map/ppermute | solution.py:436
  119.0 5.9 %collective-permute-start.33 = (bf16[128,512]{1,0:T(8,128)(2,1)S(1)}, bf16[128,512]{1,0:T(8,128)(2,1)S(1)}, u32[]{:S(2)}, u32[]{:S(2)}) collective-permute-start(bf16[128,512]{1,0:T(8,128)(2,1)S(1)} %get-tuple-element.209.refs_6_), channel_id=1, source_target_pairs={{0,2},{1,3},{2,0},{3,1},{4,6},{5,7},{6,4},{7,5},{8,10},{9,11},{10,... | collective-permute-start | bytes 393224 | tf_op jit(solution)/shard_map/ppermute | solution.py:436
  122.8 6.5 %collective-permute-start.31 = (bf16[544,128]{1,0:T(8,128)(2,1)S(1)}, bf16[544,128]{1,0:T(8,128)(2,1)S(1)}, u32[]{:S(2)}, u32[]{:S(2)}) collective-permute-start(bf16[544,128]{1,0:T(8,128)(2,1)S(1)} %get-tuple-element.212), channel_id=1, source_target_pairs={{0,8},{4,12},{8,0},{12,4},{16,24},{20,28},{24,16},{28,20},{1,9},{5... | collective-permute-start | bytes 417800 | tf_op jit(solution)/shard_map/ppermute | solution.py:436
  125.5 11.1 %collective-permute-start.35 = (bf16[2,64,512]{2,1,0:T(8,128)(2,1)S(1)}, bf16[2,64,512]{2,1,0:T(8,128)(2,1)S(1)}, u32[]{:S(2)}, u32[]{:S(2)}) collective-permute-start(bf16[2,64,512]{2,1,0:T(8,128)(2,1)S(1)} %get-tuple-element.225), channel_id=1, source_target_pairs={{0,16},{4,20},{8,24},{12,28},{16,0},{20,4},{24,8},{28,12},{1,17},{... | collective-permute-start | bytes 393224 | tf_op jit(solution)/shard_map/ppermute | solution.py:436
  129.9 5.8 %collective-permute-start.32 = (bf16[288,128]{1,0:T(8,128)(2,1)S(1)}, bf16[288,128]{1,0:T(8,128)(2,1)S(1)}, u32[]{:S(2)}, u32[]{:S(2)}) collective-permute-start(bf16[288,128]{1,0:T(8,128)(2,1)S(1)} %get-tuple-element.216), channel_id=1, source_target_pairs={{0,16},{4,20},{8,24},{12,28},{16,0},{20,4},{24,8},{28,12},{1,17},{... | collective-permute-start | bytes 221192 | tf_op jit(solution)/shard_map/ppermute | solution.py:436
  (23 other events, 115.7 us)
where the time goes:
time: 138 us
  Pallas kernels  62.4 us (45%)
  starting transfers between devices  38.4 us (28%)
  waiting for transfers between devices  26.7 us (19%)
  local copies, waits for them, and re-layouts  7.97 us (6%)
    pallas_call x29, Pallas kernels, call(): pl.pallas_call(body, out_shape=tuple((jax.ShapeDtypeStruct(shape, kind) f...  62.4 us
    ppermute x35, starting transfers between devices, swap(): return lax.ppermute(value, axis, [(i, i ^ 1 << bit) for i in range(n)])  37.7 us
    ppermute x35, waiting for transfers between devices, swap(): return lax.ppermute(value, axis, [(i, i ^ 1 << bit) for i in range(n)])  26.7 us
    unnamed x40, local copies, waits for them, and re-layouts  6.9 us
  transfers between devices with their start and end apart: 36, of which 17 were waited for; matrix products, arithmetic and copies ran while one was open for 5% of the time, Pallas kernels for 35%

commit v1 on v0

--- a/solution.py
+++ b/solution.py
@@ -233,7 +233,7 @@
 
 def feed_half(
     n_dp, seconds, seconds_t, seed_ref, seed_t_ref, we_ref, wr_ref, ge_ref, gr_ref,
-    wide_e, wide_r, active_ref, grad_ref, second_ref, add_fed, add_back,
+    wide_e, wide_r, active_ref, grad_ref, add_fed, add_back,
 ):
     own = seconds_t[0].shape[1]
     width, hidden = wide_e.shape[0], we_ref.shape[1]
@@ -241,19 +241,13 @@
     for ref, wide, near_first in ((we_ref, wide_e, True), (wr_ref, wide_r, False)):
         for p, (y, d) in enumerate(block_order(n_dp, near_first)):
             wide[d * r : (d + 1) * r, y * hidden : (y + 1) * hidden] = ref[p * r : (p + 1) * r]
-    for u, ref in enumerate(seconds):
-        second_ref[u] = ref[...]
-
-    def one(u, carry):
-        rows = pl.ds(pl.multiple_of(u * own, own), own)
-        active, curve = gelu_parts(mm(second_ref[u], wide_e[...]))
+    for u, second_ref in enumerate(seconds):
+        rows = slice(u * own, (u + 1) * own)
+        active, curve = gelu_parts(mm(second_ref[...], wide_e[...]))
         active_ref[rows] = active[:own].astype(bf16)
         grad_ref[u] = (mm(seed_ref[u], wide_r[...]) * curve).astype(bf16)
         add_fed(u, mm_bt(active_ref[rows], wide_r[...]))
         add_back(u, mm_bt(grad_ref[u], wide_e[...]))
-        return carry
-
-    lax.fori_loop(0, len(seconds), one, 0)
     total_r = mm(seed_t_ref[...], active_ref[...])
     total_e = mm(seconds_t[0][...], grad_ref[0, :own]) + mm(seconds_t[1][...], grad_ref[1, :own])
     for total, ref, near_first in ((total_e, ge_ref, True), (total_r, gr_ref, False)):
@@ -284,8 +278,7 @@
     own = out_ref.shape[1]
 
     def add_fed(u, value):
-        residual = jnp.where(u == 0, r0[:own], r1[:own])
-        out_ref[u] = (residual + (fed_in[u] + value)).astype(bf16)
+        out_ref[u] = ((r0, r1)[u][:own] + (fed_in[u] + value)).astype(bf16)
 
     def add_back(u, value):
         back_ref[u] = back_in[u] + value
@@ -390,21 +383,29 @@
 
 
 def finish_kernel(norms_ref, wp_ref, grad_0, frames_0, wide_0, grad_1, frames_1, wide_1, norm_0, norm_1, out_0, out_1, norm_ref):
-    own = out_0.shape[0]
-    gains, shifts = [], []
+    own, width = out_0.shape
+    step = own // 2
+    gain, shift = jnp.zeros((1, width), f32), jnp.zeros((1, width), f32)
     for grad_ref, frames_ref, wide_ref, out_ref in (
         (grad_0, frames_0, wide_0, out_0),
         (grad_1, frames_1, wide_1, out_1),
     ):
-        upstream = mm_bt(grad_ref[...], wp_ref[...])
-        back, gained = norm_backward(
-            frames_ref[HALO : HALO + own].astype(f32), norms_ref[0:1], upstream
-        )
-        gains.append(jnp.sum(gained, axis=0, keepdims=True))
-        shifts.append(jnp.sum(upstream, axis=0, keepdims=True))
-        out_ref[...] = wide_ref[...] + back
-    fold_norm(norm_ref, 0, gains[0] + gains[1])
-    fold_norm(norm_ref, 1, shifts[0] + shifts[1])
+
+        def one(i, carry):
+            at = pl.ds(pl.multiple_of(i * step, step), step)
+            frames = frames_ref[pl.ds(pl.multiple_of(HALO + i * step, HALO), step)]
+            upstream = mm_bt(grad_ref[at], wp_ref[...])
+            back, gained = norm_backward(frames.astype(f32), norms_ref[0:1], upstream)
+            out_ref[at] = wide_ref[at] + back
+            gain, shift = carry
+            return (
+                gain + jnp.sum(gained, axis=0, keepdims=True),
+                shift + jnp.sum(upstream, axis=0, keepdims=True),
+            )
+
+        gain, shift = lax.fori_loop(0, own // step, one, (gain, shift))
+    fold_norm(norm_ref, 0, gain)
+    fold_norm(norm_ref, 1, shift)
     fold_norm(norm_ref, 2, norm_0[...] + norm_1[...])
 
 
@@ -447,6 +448,19 @@
     return (lax.axis_index(label[0]) >> label[1]) & 1
 
 
+def by_rows(rows, body):
+    step = 128
+    if rows <= step or rows % step:
+        body(slice(None))
+        return
+
+    def one(i, carry):
+        body(pl.ds(pl.multiple_of(i * step, step), step))
+        return carry
+
+    lax.fori_loop(0, rows // step, one, 0)
+
+
 def spot(label):
     return {CORE: 1, ROW: 4, NEAR: 5}.get(label, 5 + label[1])
 
@@ -459,8 +473,12 @@
             high = place_ref[spot(label)]
             for part in range(parts):
                 out = outs.pop(0)
-                out[high] = mine[:, part]
-                out[1 - high] = got[:, part]
+
+                def body(at):
+                    out[high, :, at] = mine[:, part, at]
+                    out[1 - high, :, at] = got[:, part, at]
+
+                by_rows(out.shape[2], body)
 
     ins, outs = [place], []
     for mine, got, label, parts in streams:
@@ -493,12 +511,16 @@
         kept, sent = refs[:n], refs[n:]
         for i, (group, (_, label)) in enumerate(zip(groups, streams)):
             mine = place_ref[spot(label)]
-            kept[i][...] = total([ref[mine] for ref in group])
-            gone = total([ref[1 - mine] for ref in group]).astype(bf16)
-            if i < joint:
-                sent[0][i] = gone
-            else:
-                sent[i - max(0, joint - 1)][...] = gone
+
+            def body(at):
+                kept[i][at] = total([ref[mine, at] for ref in group])
+                gone = total([ref[1 - mine, at] for ref in group]).astype(bf16)
+                if i < joint:
+                    sent[0][i, at] = gone
+                else:
+                    sent[i - max(0, joint - 1)][at] = gone
+
+            by_rows(kept[i].shape[0], body)
 
     ins, keeps, sends = [place], [], []
     for terms, _ in streams:
@@ -519,13 +541,17 @@
     def kernel(place_ref, *refs):
         for i in range(n):
             mine = place_ref[spot(labels[i])]
-            kept = refs[i][mine] + refs[n][i, mine].astype(f32)
-            gone = refs[i][1 - mine] + refs[n][i, 1 - mine].astype(f32)
-            refs[n + 1 + i][...] = kept
-            if joint:
-                refs[2 * n + 1][i] = gone.astype(bf16)
-            else:
-                refs[2 * n + 1 + i][...] = gone.astype(bf16)
+
+            def body(at):
+                kept = refs[i][mine, at] + refs[n][i, mine, at].astype(f32)
+                gone = refs[i][1 - mine, at] + refs[n][i, 1 - mine, at].astype(f32)
+                refs[n + 1 + i][at] = kept
+                if joint:
+                    refs[2 * n + 1][i, at] = gone.astype(bf16)
+                else:
+                    refs[2 * n + 1 + i][at] = gone.astype(bf16)
+
+            by_rows(half, body)
 
     ins = [place, *[keep.reshape(2, half, cols) for keep in keeps], got.reshape(n, 2, half, cols)]
     sends = [((n, half, cols), bf16)] if joint else [((half, cols), bf16)] * n
@@ -745,7 +771,6 @@
     feed_scratch = [((width, 2 * hidden), bf16)] * 2 + [
         ((batch * own, 2 * hidden), bf16),
         ((batch, rows, 2 * hidden), bf16),
-        ((batch, rows, width), bf16),
     ]
     transposed = (seed_t, second_t_0, second_t_1)
     fed, back, keep_e, keep_r = call(

time: 138 us -> 136 us (0.986)
  Pallas kernels: 62.4 us -> 60.1 us
    pallas_call x29, Pallas kernels: 62.4 us -> 60.1 us  [call(): pl.pallas_call(body, out_shape=tuple((jax.ShapeDtypeStruct(shape, kind) f...]
where the time goes in v1:
time: 136 us
  Pallas kernels  60.1 us (44%)
  starting transfers between devices  38.1 us (28%)
  waiting for transfers between devices  27.3 us (20%)
  local copies, waits for them, and re-layouts  7.97 us (6%)
    pallas_call x29, Pallas kernels, call(): pl.pallas_call(body, out_shape=tuple((jax.ShapeDtypeStruct(shape, kind) f...  60.1 us
    ppermute x35, starting transfers between devices, swap(): return lax.ppermute(value, axis, [(i, i ^ 1 << bit) for i in range(n)])  37.4 us
    ppermute x35, waiting for transfers between devices, swap(): return lax.ppermute(value, axis, [(i, i ^ 1 << bit) for i in range(n)])  27.3 us
    unnamed x40, local copies, waits for them, and re-layouts  6.9 us
  transfers between devices with their start and end apart: 36, of which 17 were waited for; matrix products, arithmetic and copies ran while one was open for 5% of the time, Pallas kernels for 35%

profile of v1, /device:TPU:0, one launch (start us, length us, event | category | flops | bytes accessed | tf_op | source)
XLA Modules:
  0.0 135.8 jit_solution(10356028844373032901)
XLA Ops:
  1.6 4.1 %collective-permute-start = (bf16[256,128]{1,0:T(8,128)(2,1)S(1)}, bf16[256,128]{1,0:T(8,128)(2,1)S(1)}, u32[]{:S(2)}, u32[]{:S(2)}) collective-permute-start(bf16[256,128]{1,0:T(8,128)(2,1)S(1)} %bitcast.132), channel_id=1, source_target_pairs={{0,16},{4,20},{8,24},{12,28},{16,0},{20,4},{24,8},{28,12},{1,17},{... | collective-permute-start | bytes 196616 | tf_op jit(solution)/shard_map/ppermute | solution.py:437
  6.4 2.9 %collective-permute-done = bf16[256,128]{1,0:T(8,128)(2,1)S(1)} collective-permute-done((bf16[256,128]{1,0:T(8,128)(2,1)S(1)}, bf16[256,128]{1,0:T(8,128)(2,1)S(1)}, u32[]{:S(2)}, u32[]{:S(2)}) %collective-permute-start) | collective-permute-done | bytes 65568 | tf_op jit(solution)/shard_map/ppermute | solution.py:437
  12.4 3.4 %collective-permute-start.1 = (bf16[128,512]{1,0:T(8,128)(2,1)S(1)}, bf16[128,512]{1,0:T(8,128)(2,1)S(1)}, u32[]{:S(2)}, u32[]{:S(2)}) collective-permute-start(bf16[128,512]{1,0:T(8,128)(2,1)S(1)} %shard_map.378), channel_id=1, source_target_pairs={{0,16},{4,20},{8,24},{12,28},{16,0},{20,4},{24,8},{28,12},{1,17},{... | collective-permute-start | bytes 393224 | tf_op jit(solution)/shard_map/ppermute | solution.py:437
  16.4 1.6 %collective-permute-start.9 = (bf16[512,128]{1,0:T(8,128)(2,1)S(1)}, bf16[512,128]{1,0:T(8,128)(2,1)S(1)}, u32[]{:S(2)}, u32[]{:S(2)}) collective-permute-start(bf16[512,128]{1,0:T(8,128)(2,1)S(1)} %bitcast.125), channel_id=1, source_target_pairs={{0,4},{4,0},{8,12},{12,8},{16,20},{20,16},{24,28},{28,24},{1,5},{5... | collective-permute-start | bytes 393224 | tf_op jit(solution)/shard_map/ppermute | solution.py:437
  18.0 1.5 %collective-permute-start.8 = (bf16[512,128]{1,0:T(8,128)(2,1)S(1)}, bf16[512,128]{1,0:T(8,128)(2,1)S(1)}, u32[]{:S(2)}, u32[]{:S(2)}) collective-permute-start(bf16[512,128]{1,0:T(8,128)(2,1)S(1)} %bitcast.123), channel_id=1, source_target_pairs={{0,2},{1,3},{2,0},{3,1},{4,6},{5,7},{6,4},{7,5},{8,10},{9,11},{10,... | collective-permute-start | bytes 393224 | tf_op jit(solution)/shard_map/ppermute | solution.py:437
  19.5 2.1 %collective-permute-done.1 = bf16[128,512]{1,0:T(8,128)(2,1)S(1)} collective-permute-done((bf16[128,512]{1,0:T(8,128)(2,1)S(1)}, bf16[128,512]{1,0:T(8,128)(2,1)S(1)}, u32[]{:S(2)}, u32[]{:S(2)}) %collective-permute-start.1) | collective-permute-done | bytes 131104 | tf_op jit(solution)/shard_map/ppermute | solution.py:437
  23.5 1.6 %collective-permute-start.11 = (bf16[1024,128]{1,0:T(8,128)(2,1)S(1)}, bf16[1024,128]{1,0:T(8,128)(2,1)S(1)}, u32[]{:S(2)}, u32[]{:S(2)}) collective-permute-start(bf16[1024,128]{1,0:T(8,128)(2,1)S(1)} %bitcast.114), channel_id=1, source_target_pairs={{0,2},{1,3},{2,0},{3,1},{4,6},{5,7},{6,4},{7,5},{8,10},{9,11},{10,... | collective-permute-start | bytes 786440 | tf_op jit(solution)/shard_map/ppermute | solution.py:437
  30.5 1.2 collective-permute-done.10
  32.5 2.5 %collective-permute-start.13 = (bf16[2048,128]{1,0:T(8,128)(2,1)S(1)}, bf16[2048,128]{1,0:T(8,128)(2,1)S(1)}, u32[]{:S(2)}, u32[]{:S(2)}) collective-permute-start(bf16[2048,128]{1,0:T(8,128)(2,1)S(1)} %bitcast.140), channel_id=1, source_target_pairs={{0,1},{1,0},{2,3},{3,2},{4,5},{5,4},{6,7},{7,6},{8,9},{9,8},{10,11... | collective-permute-start | bytes 1572872 | tf_op jit(solution)/shard_map/ppermute | solution.py:437
  35.5 1.2 collective-permute-start.4
  37.3 6.2 %shard_map.386 = (bf16[544,1536]{1,0:T(8,128)(2,1)S(1)}, f32[5,4,112,256]{3,2,1,0:T(8,128)S(1)}, bf16[512,512]{1,0:T(8,128)(2,1)S(1)}, bf16[528,512]{1,0:T(8,128...) custom-call(s32[8]{0:T(128)S(1)} %concatenate.6.refs_0_, ...), custom_call_target="tpu_custom_call" | custom-call | flops 5000000000 | bytes 6000000 | tf_op jit(solution)/shard_map/pallas_call | solution.py:424
  46.2 1.2 collective-permute-start.14
  47.4 6.0 %shard_map.389 = (bf16[544,1536]{1,0:T(8,128)(2,1)S(1)}, f32[5,4,112,256]{3,2,1,0:T(8,128)S(1)}, bf16[512,512]{1,0:T(8,128)(2,1)S(1)}, bf16[528,512]{1,0:T(8,128...) custom-call(s32[8]{0:T(128)S(1)} %concatenate.6.refs_0_, ...), custom_call_target="tpu_custom_call" | custom-call | flops 5000000000 | bytes 6000000 | tf_op jit(solution)/shard_map/pallas_call | solution.py:424
  53.4 5.9 %collective-permute-done.15 = bf16[512,512]{1,0:T(8,128)(2,1)S(1)} collective-permute-done((bf16[512,512]{1,0:T(8,128)(2,1)S(1)}, bf16[512,512]{1,0:T(8,128)(2,1)S(1)}, u32[]{:S(2)}, u32[]{:S(2)}) %collective-permute-start.15) | collective-permute-done | bytes 524320 | tf_op jit(solution)/shard_map/ppermute | solution.py:437
  61.2 7.5 %shard_map.391 = (f32[2,512,512]{2,1,0:T(8,128)S(1)}, f32[2,528,512]{2,1,0:T(8,128)S(1)}, bf16[1024,512]{1,0:T(8,128)(2,1)S(1)}, bf16[1024,512]{1,0:T(8,128)(2,1)S(1)}) custom-call(bf16[1024,512]{1,0:T(8,128)(2,1)S(1)} %bitcast.135, bf16[1024,512]{1,0:T(8,128)(2,1)S(1)} %bitcast.137, bf16[528,512]{1,0:T(8,128)(2,1)S(1)} %get-tuple-element.149.refs_4_.refs_2_, ...), custom_call_target="tpu_custom_call" | custom-call | flops 8000000000 | bytes 6000000 | tf_op jit(solution)/shard_map/pallas_call | solution.py:424
  68.7 7.9 %shard_map.392 = (bf16[2,512,512]{2,1,0:T(8,128)(2,1)S(1)}, f32[2,528,512]{2,1,0:T(8,128)S(1)}, bf16[1024,512]{1,0:T(8,128)(2,1)S(1)}, bf16[1024,512]{1,0:T(8,128)(2,1)S(1)}) custom-call(bf16[1024,512]{1,0:T(8,128)(2,1)S(1)} %collective-permute-done.16.refs_0_, bf16[1024,512]{1,0:T(8,128)(2,1)S(1)} %collective-permute-done.17.refs_1_, ...), custom_call_target="tpu_custom_call" | custom-call | flops 8000000000 | bytes 6000000 | tf_op jit(solution)/shard_map/pallas_call | solution.py:424
  77.1 5.6 %shard_map.393 = (f32[512,512]{1,0:T(8,128)S(1)}, bf16[512,512]{1,0:T(8,128)(2,1)S(1)}, bf16[512,1536]{1,0:T(8,128)(2,1)S(1)}, f32[2,512]{1,0:T(2,128)S(1)}) custom-call(f32[2,528,512]{2,1,0:T(8,128)S(1)} %get-tuple-element.166.refs_0_.refs_1_, f32[528,512]{1,0:T(8,128)S(1)} %get-tuple-element.163.refs_7_.refs_1_, ...), custom_call_target="tpu_custom_call" | custom-call | flops 8000000000 | bytes 6000000 | tf_op jit(solution)/shard_map/pallas_call | solution.py:424
  83.8 1.5 %collective-permute-start.23 = (bf16[512,512]{1,0:T(8,128)(2,1)S(1)}, bf16[512,512]{1,0:T(8,128)(2,1)S(1)}, u32[]{:S(2)}, u32[]{:S(2)}) collective-permute-start(bf16[512,512]{1,0:T(8,128)(2,1)S(1)} %get-tuple-element.193), channel_id=1, source_target_pairs={{0,2},{1,3},{2,0},{3,1},{4,6},{5,7},{6,4},{7,5},{8,10},{9,11},{10,... | collective-permute-start | bytes 1572872 | tf_op jit(solution)/shard_map/ppermute | solution.py:437
  85.3 1.3 collective-permute-start.22
  86.5 8.6 %shard_map.395 = (f32[512,512]{1,0:T(8,128)S(1)}, bf16[512,512]{1,0:T(8,128)(2,1)}, bf16[512,1536]{1,0:T(8,128)(2,1)S(1)}, f32[2,512]{1,0:T(2,128)S(1)}, bf16[20...) custom-call(s32[8]{0:T(128)S(1)} %concatenate.6.refs_0_, ...), custom_call_target="tpu_custom_call" | custom-call | flops 10000000000 | bytes 6000000 | tf_op jit(solution)/shard_map/pallas_call | solution.py:424
  95.7 2.1 %collective-permute-done.23 = bf16[512,512]{1,0:T(8,128)(2,1)S(1)} collective-permute-done((bf16[512,512]{1,0:T(8,128)(2,1)S(1)}, bf16[512,512]{1,0:T(8,128)(2,1)S(1)}, u32[]{:S(2)}, u32[]{:S(2)}) %collective-permute-start.23) | collective-permute-done | bytes 524320 | tf_op jit(solution)/shard_map/ppermute | solution.py:437
  99.7 2.1 %collective-permute-start.30 = (bf16[2,256,512]{2,1,0:T(8,128)(2,1)S(1)}, bf16[2,256,512]{2,1,0:T(8,128)(2,1)S(1)}, u32[]{:S(2)}, u32[]{:S(2)}) collective-permute-start(bf16[2,256,512]{2,1,0:T(8,128)(2,1)S(1)} %get-tuple-element.194.refs_5_), channel_id=1, source_target_pairs={{0,8},{4,12},{8,0},{12,4},{16,24},{20,28},{24,16},{28,20},{1,9},{5... | collective-permute-start | bytes 1572872 | tf_op jit(solution)/shard_map/ppermute | solution.py:437
  104.1 3.4 %shard_map.398 = (f32[512,512]{1,0:T(8,128)S(1)}, f32[512,512]{1,0:T(8,128)S(1)}, f32[16,128]{1,0:T(8,128)S(1)}) custom-call(f32[4,512]{1,0:T(4,128)S(1)} %copy-done.14, bf16[512,1536]{1,0:T(8,128)(2,1)S(1)} %get-tuple-element.153.refs_3_.refs_1_, bf16[512,1536]{1,0:T(8,128)(2,1)S(1)} %get-tuple-element.169.refs_5_.refs_12_.refs_2_, ...), custom_call_target="tpu_custom_call" | custom-call | flops 3000000000 | bytes 6000000 | tf_op jit(solution)/shard_map/pallas_call | solution.py:424
  107.6 1.2 collective-permute-done.26
  108.7 1.2 collective-permute-start.27
  109.9 2.5 %collective-permute-done.27.refs_6_ = f32[16,128]{1,0:T(8,128)S(1)} collective-permute-done((f32[16,128]{1,0:T(8,128)S(1)}, f32[16,128]{1,0:T(8,128)S(1)}, u32[]{:S(2)}, u32[]{:S(2)}) %collective-permute-start.27) | collective-permute-done | bytes 8224 | tf_op jit(solution)/shard_map/ppermute | solution.py:437
  114.2 1.7 %collective-permute-start.28 = (bf16[512,128]{1,0:T(8,128)(2,1)S(1)}, bf16[512,128]{1,0:T(8,128)(2,1)S(1)}, u32[]{:S(2)}, u32[]{:S(2)}) collective-permute-start(bf16[512,128]{1,0:T(8,128)(2,1)S(1)} %get-tuple-element.204.refs_4_), channel_id=1, source_target_pairs={{0,2},{1,3},{2,0},{3,1},{4,6},{5,7},{6,4},{7,5},{8,10},{9,11},{10,... | collective-permute-start | bytes 393224 | tf_op jit(solution)/shard_map/ppermute | solution.py:437
  117.9 2.4 %collective-permute-done.28.refs_3_ = bf16[512,128]{1,0:T(8,128)(2,1)S(1)} collective-permute-done((bf16[512,128]{1,0:T(8,128)(2,1)S(1)}, bf16[512,128]{1,0:T(8,128)(2,1)S(1)}, u32[]{:S(2)}, u32[]{:S(2)}) %collective-permute-start.28) | collective-permute-done | bytes 131104 | tf_op jit(solution)/shard_map/ppermute | solution.py:437
  121.0 2.0 %copy.46 = bf16[512,2,512]{2,1,0:T(2,128)(2,1)} copy(bf16[512,2,512]{2,0,1:T(8,128)(2,1)S(1)} %bitcast.78) | data formatting | bytes 2097152
  123.6 3.0 %collective-permute-start.35 = (bf16[2,64,512]{2,1,0:T(8,128)(2,1)S(1)}, bf16[2,64,512]{2,1,0:T(8,128)(2,1)S(1)}, u32[]{:S(2)}, u32[]{:S(2)}) collective-permute-start(bf16[2,64,512]{2,1,0:T(8,128)(2,1)S(1)} %get-tuple-element.225), channel_id=1, source_target_pairs={{0,16},{4,20},{8,24},{12,28},{16,0},{20,4},{24,8},{28,12},{1,17},{... | collective-permute-start | bytes 393224 | tf_op jit(solution)/shard_map/ppermute | solution.py:437
  129.0 2.9 %copy.47 = f32[512,2,512]{2,1,0:T(2,128)} copy(f32[512,2,512]{2,0,1:T(8,128)S(1)} %maximum_bitcast_fusion) | data formatting | bytes 4194304
  131.9 1.8 %collective-permute-done.32.refs_2_ = bf16[288,128]{1,0:T(8,128)(2,1)S(1)} collective-permute-done((bf16[288,128]{1,0:T(8,128)(2,1)S(1)}, bf16[288,128]{1,0:T(8,128)(2,1)S(1)}, u32[]{:S(2)}, u32[]{:S(2)}) %collective-permute-start.32) | collective-permute-done | bytes 73760 | tf_op jit(solution)/shard_map/ppermute | solution.py:437
  (114 shorter events, 34.4 us)
Async XLA Ops:
  1.6 7.8 %collective-permute-start = (bf16[256,128]{1,0:T(8,128)(2,1)S(1)}, bf16[256,128]{1,0:T(8,128)(2,1)S(1)}, u32[]{:S(2)}, u32[]{:S(2)}) collective-permute-start(bf16[256,128]{1,0:T(8,128)(2,1)S(1)} %bitcast.132), channel_id=1, source_target_pairs={{0,16},{4,20},{8,24},{12,28},{16,0},{20,4},{24,8},{28,12},{1,17},{... | collective-permute-start | bytes 196616 | tf_op jit(solution)/shard_map/ppermute | solution.py:437
  9.9 5.9 %collective-permute-start.5 = (bf16[512,128]{1,0:T(8,128)(2,1)S(1)}, bf16[512,128]{1,0:T(8,128)(2,1)S(1)}, u32[]{:S(2)}, u32[]{:S(2)}) collective-permute-start(bf16[512,128]{1,0:T(8,128)(2,1)S(1)} %bitcast.129), channel_id=1, source_target_pairs={{0,8},{4,12},{8,0},{12,4},{16,24},{20,28},{24,16},{28,20},{1,9},{5... | collective-permute-start | bytes 393224 | tf_op jit(solution)/shard_map/ppermute | solution.py:437
  12.4 9.2 %collective-permute-start.1 = (bf16[128,512]{1,0:T(8,128)(2,1)S(1)}, bf16[128,512]{1,0:T(8,128)(2,1)S(1)}, u32[]{:S(2)}, u32[]{:S(2)}) collective-permute-start(bf16[128,512]{1,0:T(8,128)(2,1)S(1)} %shard_map.378), channel_id=1, source_target_pairs={{0,16},{4,20},{8,24},{12,28},{16,0},{20,4},{24,8},{28,12},{1,17},{... | collective-permute-start | bytes 393224 | tf_op jit(solution)/shard_map/ppermute | solution.py:437
  16.4 5.8 %collective-permute-start.9 = (bf16[512,128]{1,0:T(8,128)(2,1)S(1)}, bf16[512,128]{1,0:T(8,128)(2,1)S(1)}, u32[]{:S(2)}, u32[]{:S(2)}) collective-permute-start(bf16[512,128]{1,0:T(8,128)(2,1)S(1)} %bitcast.125), channel_id=1, source_target_pairs={{0,4},{4,0},{8,12},{12,8},{16,20},{20,16},{24,28},{28,24},{1,5},{5... | collective-permute-start | bytes 393224 | tf_op jit(solution)/shard_map/ppermute | solution.py:437
  18.0 5.0 %collective-permute-start.8 = (bf16[512,128]{1,0:T(8,128)(2,1)S(1)}, bf16[512,128]{1,0:T(8,128)(2,1)S(1)}, u32[]{:S(2)}, u32[]{:S(2)}) collective-permute-start(bf16[512,128]{1,0:T(8,128)(2,1)S(1)} %bitcast.123), channel_id=1, source_target_pairs={{0,2},{1,3},{2,0},{3,1},{4,6},{5,7},{6,4},{7,5},{8,10},{9,11},{10,... | collective-permute-start | bytes 393224 | tf_op jit(solution)/shard_map/ppermute | solution.py:437
  22.1 7.7 %collective-permute-start.2 = (bf16[256,512]{1,0:T(8,128)(2,1)S(1)}, bf16[256,512]{1,0:T(8,128)(2,1)S(1)}, u32[]{:S(2)}, u32[]{:S(2)}) collective-permute-start(bf16[256,512]{1,0:T(8,128)(2,1)S(1)} %bitcast.74), channel_id=1, source_target_pairs={{0,8},{4,12},{8,0},{12,4},{16,24},{20,28},{24,16},{28,20},{1,9},{5... | collective-permute-start | bytes 786440 | tf_op jit(solution)/shard_map/ppermute | solution.py:437
  23.5 7.0 %collective-permute-start.11 = (bf16[1024,128]{1,0:T(8,128)(2,1)S(1)}, bf16[1024,128]{1,0:T(8,128)(2,1)S(1)}, u32[]{:S(2)}, u32[]{:S(2)}) collective-permute-start(bf16[1024,128]{1,0:T(8,128)(2,1)S(1)} %bitcast.114), channel_id=1, source_target_pairs={{0,2},{1,3},{2,0},{3,1},{4,6},{5,7},{6,4},{7,5},{8,10},{9,11},{10,... | collective-permute-start | bytes 786440 | tf_op jit(solution)/shard_map/ppermute | solution.py:437
  25.1 6.6 %collective-permute-start.10 = (bf16[1024,128]{1,0:T(8,128)(2,1)S(1)}, bf16[1024,128]{1,0:T(8,128)(2,1)S(1)}, u32[]{:S(2)}, u32[]{:S(2)}) collective-permute-start(bf16[1024,128]{1,0:T(8,128)(2,1)S(1)} %bitcast.112), channel_id=1, source_target_pairs={{0,4},{4,0},{8,12},{12,8},{16,20},{20,16},{24,28},{28,24},{1,5},{5... | collective-permute-start | bytes 786440 | tf_op jit(solution)/shard_map/ppermute | solution.py:437
  32.5 4.3 %collective-permute-start.13 = (bf16[2048,128]{1,0:T(8,128)(2,1)S(1)}, bf16[2048,128]{1,0:T(8,128)(2,1)S(1)}, u32[]{:S(2)}, u32[]{:S(2)}) collective-permute-start(bf16[2048,128]{1,0:T(8,128)(2,1)S(1)} %bitcast.140), channel_id=1, source_target_pairs={{0,1},{1,0},{2,3},{3,2},{4,5},{5,4},{6,7},{7,6},{8,9},{9,8},{10,11... | collective-permute-start | bytes 1572872 | tf_op jit(solution)/shard_map/ppermute | solution.py:437
  35.1 9.4 %collective-permute-start.3 = (bf16[256,512]{1,0:T(8,128)(2,1)S(1)}, bf16[256,512]{1,0:T(8,128)(2,1)S(1)}, u32[]{:S(2)}, u32[]{:S(2)}) collective-permute-start(bf16[256,512]{1,0:T(8,128)(2,1)S(1)} %bitcast.88), channel_id=1, source_target_pairs={{0,2},{1,3},{2,0},{3,1},{4,6},{5,7},{6,4},{7,5},{8,10},{9,11},{10,... | collective-permute-start | bytes 786440 | tf_op jit(solution)/shard_map/ppermute | solution.py:437
  35.5 8.9 %collective-permute-start.4 = (bf16[256,512]{1,0:T(8,128)(2,1)S(1)}, bf16[256,512]{1,0:T(8,128)(2,1)S(1)}, u32[]{:S(2)}, u32[]{:S(2)}) collective-permute-start(bf16[256,512]{1,0:T(8,128)(2,1)S(1)} %bitcast.105), channel_id=1, source_target_pairs={{0,4},{4,0},{8,12},{12,8},{16,20},{20,16},{24,28},{28,24},{1,5},{5... | collective-permute-start | bytes 786440 | tf_op jit(solution)/shard_map/ppermute | solution.py:437
  45.1 14.3 %collective-permute-start.15 = (bf16[512,512]{1,0:T(8,128)(2,1)S(1)}, bf16[512,512]{1,0:T(8,128)(2,1)S(1)}, u32[]{:S(2)}, u32[]{:S(2)}) collective-permute-start(bf16[512,512]{1,0:T(8,128)(2,1)S(1)} %bitcast.101), channel_id=1, source_target_pairs={{0,2},{1,3},{2,0},{3,1},{4,6},{5,7},{6,4},{7,5},{8,10},{9,11},{10,... | collective-permute-start | bytes 1572872 | tf_op jit(solution)/shard_map/ppermute | solution.py:437
  46.2 13.4 %collective-permute-start.14 = (bf16[512,512]{1,0:T(8,128)(2,1)S(1)}, bf16[512,512]{1,0:T(8,128)(2,1)S(1)}, u32[]{:S(2)}, u32[]{:S(2)}) collective-permute-start(bf16[512,512]{1,0:T(8,128)(2,1)S(1)} %bitcast.99), channel_id=1, source_target_pairs={{0,4},{4,0},{8,12},{12,8},{16,20},{20,16},{24,28},{28,24},{1,5},{5... | collective-permute-start | bytes 1572872 | tf_op jit(solution)/shard_map/ppermute | solution.py:437
  60.6 8.1 %collective-permute-start.17 = (bf16[1024,512]{1,0:T(8,128)(2,1)S(1)}, bf16[1024,512]{1,0:T(8,128)(2,1)S(1)}, u32[]{:S(2)}, u32[]{:S(2)}) collective-permute-start(bf16[1024,512]{1,0:T(8,128)(2,1)S(1)} %bitcast.136), channel_id=1, source_target_pairs={{0,1},{1,0},{2,3},{3,2},{4,5},{5,4},{6,7},{7,6},{8,9},{9,8},{10,11... | collective-permute-start | bytes 3145736 | tf_op jit(solution)/shard_map/ppermute | solution.py:437
  60.7 8.0 %collective-permute-start.16 = (bf16[1024,512]{1,0:T(8,128)(2,1)S(1)}, bf16[1024,512]{1,0:T(8,128)(2,1)S(1)}, u32[]{:S(2)}, u32[]{:S(2)}) collective-permute-start(bf16[1024,512]{1,0:T(8,128)(2,1)S(1)} %bitcast.134), channel_id=1, source_target_pairs={{0,1},{1,0},{2,3},{3,2},{4,5},{5,4},{6,7},{7,6},{8,9},{9,8},{10,11... | collective-permute-start | bytes 3145736 | tf_op jit(solution)/shard_map/ppermute | solution.py:437
  76.5 6.2 %collective-permute-start.18 = (bf16[1024,512]{1,0:T(8,128)(2,1)S(1)}, bf16[1024,512]{1,0:T(8,128)(2,1)S(1)}, u32[]{:S(2)}, u32[]{:S(2)}) collective-permute-start(bf16[1024,512]{1,0:T(8,128)(2,1)S(1)} %get-tuple-element.179), channel_id=1, source_target_pairs={{0,1},{1,0},{2,3},{3,2},{4,5},{5,4},{6,7},{7,6},{8,9},{9,8},{10,11... | collective-permute-start | bytes 3145736 | tf_op jit(solution)/shard_map/ppermute | solution.py:437
  76.7 6.1 %collective-permute-start.19 = (bf16[1024,512]{1,0:T(8,128)(2,1)S(1)}, bf16[1024,512]{1,0:T(8,128)(2,1)S(1)}, u32[]{:S(2)}, u32[]{:S(2)}) collective-permute-start(bf16[1024,512]{1,0:T(8,128)(2,1)S(1)} %get-tuple-element.181), channel_id=1, source_target_pairs={{0,1},{1,0},{2,3},{3,2},{4,5},{5,4},{6,7},{7,6},{8,9},{9,8},{10,11... | collective-permute-start | bytes 3145736 | tf_op jit(solution)/shard_map/ppermute | solution.py:437
  83.8 14.0 %collective-permute-start.23 = (bf16[512,512]{1,0:T(8,128)(2,1)S(1)}, bf16[512,512]{1,0:T(8,128)(2,1)S(1)}, u32[]{:S(2)}, u32[]{:S(2)}) collective-permute-start(bf16[512,512]{1,0:T(8,128)(2,1)S(1)} %get-tuple-element.193), channel_id=1, source_target_pairs={{0,2},{1,3},{2,0},{3,1},{4,6},{5,7},{6,4},{7,5},{8,10},{9,11},{10,... | collective-permute-start | bytes 1572872 | tf_op jit(solution)/shard_map/ppermute | solution.py:437
  85.3 13.6 %collective-permute-start.22 = (bf16[512,512]{1,0:T(8,128)(2,1)S(1)}, bf16[512,512]{1,0:T(8,128)(2,1)S(1)}, u32[]{:S(2)}, u32[]{:S(2)}) collective-permute-start(bf16[512,512]{1,0:T(8,128)(2,1)S(1)} %get-tuple-element.182.refs_14_), channel_id=1, source_target_pairs={{0,4},{4,0},{8,12},{12,8},{16,20},{20,16},{24,28},{28,24},{1,5},{5... | collective-permute-start | bytes 1572872 | tf_op jit(solution)/shard_map/ppermute | solution.py:437
  95.2 6.6 %collective-permute-start.20 = (bf16[2048,128]{1,0:T(8,128)(2,1)S(1)}, bf16[2048,128]{1,0:T(8,128)(2,1)S(1)}, u32[]{:S(2)}, u32[]{:S(2)}) collective-permute-start(bf16[2048,128]{1,0:T(8,128)(2,1)S(1)} %get-tuple-element.188), channel_id=1, source_target_pairs={{0,1},{1,0},{2,3},{3,2},{4,5},{5,4},{6,7},{7,6},{8,9},{9,8},{10,11... | collective-permute-start | bytes 1572872 | tf_op jit(solution)/shard_map/ppermute | solution.py:437
  95.2 6.6 %collective-permute-start.21 = (bf16[2048,128]{1,0:T(8,128)(2,1)S(1)}, bf16[2048,128]{1,0:T(8,128)(2,1)S(1)}, u32[]{:S(2)}, u32[]{:S(2)}) collective-permute-start(bf16[2048,128]{1,0:T(8,128)(2,1)S(1)} %get-tuple-element.190), channel_id=1, source_target_pairs={{0,1},{1,0},{2,3},{3,2},{4,5},{5,4},{6,7},{7,6},{8,9},{9,8},{10,11... | collective-permute-start | bytes 1572872 | tf_op jit(solution)/shard_map/ppermute | solution.py:437
  99.7 16.2 %collective-permute-start.30 = (bf16[2,256,512]{2,1,0:T(8,128)(2,1)S(1)}, bf16[2,256,512]{2,1,0:T(8,128)(2,1)S(1)}, u32[]{:S(2)}, u32[]{:S(2)}) collective-permute-start(bf16[2,256,512]{2,1,0:T(8,128)(2,1)S(1)} %get-tuple-element.194.refs_5_), channel_id=1, source_target_pairs={{0,8},{4,12},{8,0},{12,4},{16,24},{20,28},{24,16},{28,20},{1,9},{5... | collective-permute-start | bytes 1572872 | tf_op jit(solution)/shard_map/ppermute | solution.py:437
  102.7 9.7 %collective-permute-start.25 = (bf16[1024,128]{1,0:T(8,128)(2,1)S(1)}, bf16[1024,128]{1,0:T(8,128)(2,1)S(1)}, u32[]{:S(2)}, u32[]{:S(2)}) collective-permute-start(bf16[1024,128]{1,0:T(8,128)(2,1)S(1)} %get-tuple-element.200), channel_id=1, source_target_pairs={{0,2},{1,3},{2,0},{3,1},{4,6},{5,7},{6,4},{7,5},{8,10},{9,11},{10,... | collective-permute-start | bytes 786440 | tf_op jit(solution)/shard_map/ppermute | solution.py:437
  103.1 9.3 %collective-permute-start.24 = (bf16[1024,128]{1,0:T(8,128)(2,1)S(1)}, bf16[1024,128]{1,0:T(8,128)(2,1)S(1)}, u32[]{:S(2)}, u32[]{:S(2)}) collective-permute-start(bf16[1024,128]{1,0:T(8,128)(2,1)S(1)} %get-tuple-element.195.refs_10_), channel_id=1, source_target_pairs={{0,4},{4,0},{8,12},{12,8},{16,20},{20,16},{24,28},{28,24},{1,5},{5... | collective-permute-start | bytes 786440 | tf_op jit(solution)/shard_map/ppermute | solution.py:437
  108.7 3.7 %collective-permute-start.27 = (f32[16,128]{1,0:T(8,128)S(1)}, f32[16,128]{1,0:T(8,128)S(1)}, u32[]{:S(2)}, u32[]{:S(2)}) collective-permute-start(f32[16,128]{1,0:T(8,128)S(1)} %add.3.refs_5_), channel_id=1, source_target_pairs={{0,2},{1,3},{2,0},{3,1},{4,6},{5,7},{6,4},{7,5},{8,10},{9,11},{10,... | collective-permute-start | bytes 24584 | tf_op jit(solution)/shard_map/ppermute | solution.py:437
  113.0 7.2 %collective-permute-start.29 = (bf16[544,128]{1,0:T(8,128)(2,1)S(1)}, bf16[544,128]{1,0:T(8,128)(2,1)S(1)}, u32[]{:S(2)}, u32[]{:S(2)}) collective-permute-start(bf16[544,128]{1,0:T(8,128)(2,1)S(1)} %get-tuple-element.205), channel_id=1, source_target_pairs={{0,4},{4,0},{8,12},{12,8},{16,20},{20,16},{24,28},{28,24},{1,5},{5... | collective-permute-start | bytes 417800 | tf_op jit(solution)/shard_map/ppermute | solution.py:437
  114.2 6.1 %collective-permute-start.28 = (bf16[512,128]{1,0:T(8,128)(2,1)S(1)}, bf16[512,128]{1,0:T(8,128)(2,1)S(1)}, u32[]{:S(2)}, u32[]{:S(2)}) collective-permute-start(bf16[512,128]{1,0:T(8,128)(2,1)S(1)} %get-tuple-element.204.refs_4_), channel_id=1, source_target_pairs={{0,2},{1,3},{2,0},{3,1},{4,6},{5,7},{6,4},{7,5},{8,10},{9,11},{10,... | collective-permute-start | bytes 393224 | tf_op jit(solution)/shard_map/ppermute | solution.py:437
  116.5 6.5 %collective-permute-start.34 = (bf16[128,512]{1,0:T(8,128)(2,1)S(1)}, bf16[128,512]{1,0:T(8,128)(2,1)S(1)}, u32[]{:S(2)}, u32[]{:S(2)}) collective-permute-start(bf16[128,512]{1,0:T(8,128)(2,1)S(1)} %get-tuple-element.222), channel_id=1, source_target_pairs={{0,4},{4,0},{8,12},{12,8},{16,20},{20,16},{24,28},{28,24},{1,5},{5... | collective-permute-start | bytes 393224 | tf_op jit(solution)/shard_map/ppermute | solution.py:437
  117.0 6.0 %collective-permute-start.33 = (bf16[128,512]{1,0:T(8,128)(2,1)S(1)}, bf16[128,512]{1,0:T(8,128)(2,1)S(1)}, u32[]{:S(2)}, u32[]{:S(2)}) collective-permute-start(bf16[128,512]{1,0:T(8,128)(2,1)S(1)} %get-tuple-element.209.refs_6_), channel_id=1, source_target_pairs={{0,2},{1,3},{2,0},{3,1},{4,6},{5,7},{6,4},{7,5},{8,10},{9,11},{10,... | collective-permute-start | bytes 393224 | tf_op jit(solution)/shard_map/ppermute | solution.py:437
  120.9 6.6 %collective-permute-start.31 = (bf16[544,128]{1,0:T(8,128)(2,1)S(1)}, bf16[544,128]{1,0:T(8,128)(2,1)S(1)}, u32[]{:S(2)}, u32[]{:S(2)}) collective-permute-start(bf16[544,128]{1,0:T(8,128)(2,1)S(1)} %get-tuple-element.212), channel_id=1, source_target_pairs={{0,8},{4,12},{8,0},{12,4},{16,24},{20,28},{24,16},{28,20},{1,9},{5... | collective-permute-start | bytes 417800 | tf_op jit(solution)/shard_map/ppermute | solution.py:437
  123.6 11.0 %collective-permute-start.35 = (bf16[2,64,512]{2,1,0:T(8,128)(2,1)S(1)}, bf16[2,64,512]{2,1,0:T(8,128)(2,1)S(1)}, u32[]{:S(2)}, u32[]{:S(2)}) collective-permute-start(bf16[2,64,512]{2,1,0:T(8,128)(2,1)S(1)} %get-tuple-element.225), channel_id=1, source_target_pairs={{0,16},{4,20},{8,24},{12,28},{16,0},{20,4},{24,8},{28,12},{1,17},{... | collective-permute-start | bytes 393224 | tf_op jit(solution)/shard_map/ppermute | solution.py:437
  128.0 5.6 %collective-permute-start.32 = (bf16[288,128]{1,0:T(8,128)(2,1)S(1)}, bf16[288,128]{1,0:T(8,128)(2,1)S(1)}, u32[]{:S(2)}, u32[]{:S(2)}) collective-permute-start(bf16[288,128]{1,0:T(8,128)(2,1)S(1)} %get-tuple-element.216), channel_id=1, source_target_pairs={{0,16},{4,20},{8,24},{12,28},{16,0},{20,4},{24,8},{28,12},{1,17},{... | collective-permute-start | bytes 221192 | tf_op jit(solution)/shard_map/ppermute | solution.py:437
  (23 other events, 118.6 us)

commit v2 on v1

--- a/solution.py
+++ b/solution.py
@@ -122,7 +122,10 @@
             for p, (y, d) in enumerate(block_order(n_dp, near_first)):
                 at = pl.multiple_of((2 * y + which) * cols, cols)
                 for i in range(2):
-                    block = ref[(2 * p + i) * r : (2 * p + i + 1) * r]
+                    source, to = ref, (2 * p + i) * r
+                    if isinstance(ref, tuple):
+                        source, to = ref[to // ref[0].shape[0]], to % ref[0].shape[0]
+                    block = source[to : to + r]
                     if first + i < 3:
                         wp_ref[d * r : (d + 1) * r, pl.ds((first + i) * width + at, cols)] = block
                     else:
@@ -182,8 +185,10 @@
     first_ref[...] = normed[HALO : HALO + own]
     qkv_ref[...] = mm(normed, wp_ref[...]).astype(bf16)
     def group(hg, carry):
-        at = pl.multiple_of(hg * LANES, LANES)
-        here = pl.ds(pl.multiple_of(hg * KEYS, KEYS), KEYS)
+        at, here = hg * LANES, hg * KEYS
+        if u > 0:
+            at, here = pl.multiple_of(at, LANES), pl.multiple_of(here, KEYS)
+        here = pl.ds(here, KEYS)
         for b, block in enumerate(query_blocks(total)):
             q0, rows, k0 = block
             allowed = band(block, start, length)
@@ -200,7 +205,11 @@
             mixed_ref[q0 - HALO : q0 - HALO + rows, pl.ds(at, LANES)] = out.astype(bf16)
         return carry
 
-    lax.fori_loop(0, width // LANES, group, 0)
+    if u == 0:
+        for hg in range(width // LANES):
+            group(hg, 0)
+    else:
+        lax.fori_loop(0, width // LANES, group, 0)
     residual = frames_ref[HALO:total].astype(f32) + mm_bt(mixed_ref[...], wc_ref[...])
     residual_ref[...] = residual
     scaled, _ = normalise(residual)
@@ -209,10 +218,11 @@
 
 
 def attend_first_kernel(
-    n_dp, place_ref, frames_ref, norms_ref, own_a, own_b, got_a, got_b, *refs
+    n_dp, place_ref, frames_ref, norms_ref, own_a, own_b, got_a0, got_a1, got_b0, got_b1, *refs
 ):
     *outs, wp_ref, wc_ref = refs
-    place_weights(n_dp, place_ref[1], own_a, own_b, got_a, got_b, wp_ref, wc_ref)
+    got = (got_a0, got_a1), (got_b0, got_b1)
+    place_weights(n_dp, place_ref[1], own_a, own_b, *got, wp_ref, wc_ref)
     attend_one(0, place_ref, frames_ref, norms_ref, wp_ref, wc_ref, *outs)
 
 
@@ -306,35 +316,54 @@
     mixed_g_ref[...] = mm(low, wc_ref[...]).astype(bf16)
     grad_kv_ref[...] = jnp.zeros_like(grad_kv_ref)
     scale = 1.0 / math.sqrt(HEAD_DIM)
-    def group(hg, carry):
+    blocks = query_blocks(total)
+    even = len(blocks) - 1
+
+    def one_block(hg, b, o0, k0, rows, mine):
+        q0 = o0 + HALO
         at = pl.multiple_of(hg * LANES, LANES)
         here = pl.ds(pl.multiple_of(hg * KEYS, KEYS), KEYS)
         first_lanes, second_lanes = pl.ds(at, LANES), pl.ds(width + at, LANES)
-        for b, block in enumerate(query_blocks(total)):
-            q0, rows, k0 = block
-            queries = stack_heads(qkv_ref[q0 : q0 + rows, first_lanes])
-            keys = qkv_ref[k0 : k0 + KEYS, second_lanes]
-            values = qkv_ref[k0 : k0 + KEYS, pl.ds(2 * width + at, LANES)]
-            upper = stack_heads(mixed_g_ref[q0 - HALO : q0 - HALO + rows, first_lanes])
-            grad_probs = mm_bt(upper, values)
-            low_probs, grad_scores = [], []
-            for h in range(GROUP):
-                probs = probs_ref[b, h, :rows, here]
-                grad = grad_probs[h * rows : (h + 1) * rows]
-                inner = jnp.sum(probs * grad, axis=-1, keepdims=True)
-                low_probs.append(probs.astype(bf16))
-                grad_scores.append((probs * (grad - inner)).astype(bf16))
-            low_probs = jnp.concatenate(low_probs, axis=0)
-            grad_scores = jnp.concatenate(grad_scores, axis=0)
-            grad_q = merge_heads(mm(grad_scores, keys), rows) * scale
-            mine = min(rows, HALO + own - q0)
-            if mine > 0:
-                grad_ref[q0 - HALO : q0 - HALO + mine, first_lanes] = grad_q[:mine].astype(bf16)
-            grad_kv_ref[k0 : k0 + KEYS, first_lanes] += mm_at(grad_scores, queries) * scale
-            grad_kv_ref[k0 : k0 + KEYS, second_lanes] += mm_at(low_probs, upper)
+        queries = stack_heads(qkv_ref[pl.ds(q0, rows), first_lanes])
+        keys = qkv_ref[pl.ds(k0, KEYS), second_lanes]
+        values = qkv_ref[pl.ds(k0, KEYS), pl.ds(2 * width + at, LANES)]
+        upper = stack_heads(mixed_g_ref[pl.ds(o0, rows), first_lanes])
+        grad_probs = mm_bt(upper, values)
+        low_probs, grad_scores = [], []
+        for h in range(GROUP):
+            probs = probs_ref[b, h, :rows, here]
+            grad = grad_probs[h * rows : (h + 1) * rows]
+            inner = jnp.sum(probs * grad, axis=-1, keepdims=True)
+            low_probs.append(probs.astype(bf16))
+            grad_scores.append((probs * (grad - inner)).astype(bf16))
+        low_probs = jnp.concatenate(low_probs, axis=0)
+        grad_scores = jnp.concatenate(grad_scores, axis=0)
+        grad_q = merge_heads(mm(grad_scores, keys), rows) * scale
+        grad_ref[pl.ds(o0, mine), first_lanes] = grad_q[:mine].astype(bf16)
+        grad_kv_ref[pl.ds(k0, KEYS), first_lanes] += mm_at(grad_scores, queries) * scale
+        grad_kv_ref[pl.ds(k0, KEYS), second_lanes] += mm_at(low_probs, upper)
+
+    def some(i, carry):
+        b = i % even
+        o0 = pl.multiple_of(b * QUERIES, HALO)
+        one_block(i // even, b, o0, o0, QUERIES, QUERIES)
         return carry
 
-    lax.fori_loop(0, width // LANES, group, 0)
+    def rest(hg, carry):
+        q0, rows, k0 = blocks[-1]
+        one_block(hg, even, q0 - HALO, k0, rows, HALO + own - q0)
+        return carry
+
+    def every(hg, carry):
+        for b, (q0, rows, k0) in enumerate(blocks):
+            one_block(hg, b, q0 - HALO, k0, rows, min(rows, HALO + own - q0))
+        return carry
+
+    if u == 0:
+        lax.fori_loop(0, width // LANES, every, 0)
+    else:
+        lax.fori_loop(0, even * (width // LANES), some, 0)
+        lax.fori_loop(0, width // LANES, rest, 0)
     grad_ref[:, width:] = grad_kv_ref[HALO : HALO + own].astype(bf16)
 
 
@@ -726,7 +755,8 @@
     one_a, one_b = paired(
         place, [(one_a, got_a, NEAR, 1), (one_b, got_b, ROW, 1)], waits=(two_a, *frames_x)
     )
-    core_a, core_b = swap(one_a, *CORE), swap(one_b, *CORE)
+    cut = one_a.shape[0] // 2
+    core_parts = [swap(x, *CORE) for x in (one_a[:cut], one_a[cut:], one_b[:cut], one_b[cut:])]
 
     per_u = [
         ((long, 3 * width), bf16),
@@ -737,23 +767,24 @@
         ((rows, width), bf16),
         ((width, own), bf16),
     ]
-    qkv_0, probs_0, first_0, mixed_0, residual_0, second_0, second_t_0, wp, wc = call(
-        functools.partial(attend_first_kernel, n_dp),
-        (place, frames_x[0], norm_params, one_a, one_b, core_a, core_b),
-        per_u + [((width, 3 * width), bf16), ((width, width), bf16)],
-        flops=5e9,
-    )
     seed, seed_t = call(
         seed_kernel,
         (place, cotangent_u, near, over),
         [((batch, rows, width), bf16), ((width, batch * own), bf16)],
-        waits=(second_0,),
+        waits=(one_a,),
         flops=1e8,
         mib=8,
     )
 
     got_a, got_b = swap(two_a, *ROW), swap(two_b, *NEAR)
     two_a, two_b = paired(place, [(two_a, got_a, ROW, 1), (two_b, got_b, NEAR, 1)], waits=(seed,))
+    qkv_0, probs_0, first_0, mixed_0, residual_0, second_0, second_t_0, wp, wc = call(
+        functools.partial(attend_first_kernel, n_dp),
+        (place, frames_x[0], norm_params, one_a, one_b, *core_parts),
+        per_u + [((width, 3 * width), bf16), ((width, width), bf16)],
+        waits=(two_a, two_b),
+        flops=5e9,
+    )
     qkv_1, probs_1, first_1, mixed_1, residual_1, second_1, second_t_1 = call(
         attend_next_kernel,
         (place, frames_x[1], norm_params, wp, wc),

time: 136 us -> 133 us (0.978)
  waiting for transfers between devices: 27.3 us -> 17.5 us
  starting transfers between devices: 38.1 us -> 44.4 us
    ppermute x35 -> x37, waiting for transfers between devices: 27.3 us -> 17.5 us  [swap(): return lax.ppermute(value, axis, [(i, i ^ 1 << bit) for i in range(n)])]
    ppermute x35 -> x37, starting transfers between devices: 37.4 us -> 43.8 us  [swap(): return lax.ppermute(value, axis, [(i, i ^ 1 << bit) for i in range(n)])]
  transfers between devices with their start and end apart: 36 -> 38, of which waited for: 17 -> 15; matrix products, arithmetic and copies ran while one was open for 5% -> 5% of each run, Pallas kernels for 35% -> 37%
where the time goes in v2:
time: 133 us
  Pallas kernels  60.9 us (46%)
  starting transfers between devices  44.4 us (33%)
  waiting for transfers between devices  17.5 us (13%)
  local copies, waits for them, and re-layouts  8.05 us (6%)
    pallas_call x29, Pallas kernels, call(): pl.pallas_call(body, out_shape=tuple((jax.ShapeDtypeStruct(shape, kind) f...  60.9 us
    ppermute x37, starting transfers between devices, swap(): return lax.ppermute(value, axis, [(i, i ^ 1 << bit) for i in range(n)])  43.8 us
    ppermute x37, waiting for transfers between devices, swap(): return lax.ppermute(value, axis, [(i, i ^ 1 << bit) for i in range(n)])  17.5 us
    unnamed x40, local copies, waits for them, and re-layouts  6.89 us
  transfers between devices with their start and end apart: 38, of which 15 were waited for; matrix products, arithmetic and copies ran while one was open for 5% of the time, Pallas kernels for 37%

profile of v2, /device:TPU:0, one launch (start us, length us, event | category | flops | bytes accessed | tf_op | source)
XLA Modules:
  0.0 133.2 jit_solution(16632704558675858390)
XLA Ops:
  1.6 4.1 %collective-permute-start = (bf16[256,128]{1,0:T(8,128)(2,1)S(1)}, bf16[256,128]{1,0:T(8,128)(2,1)S(1)}, u32[]{:S(2)}, u32[]{:S(2)}) collective-permute-start(bf16[256,128]{1,0:T(8,128)(2,1)S(1)} %bitcast.145), channel_id=1, source_target_pairs={{0,16},{4,20},{8,24},{12,28},{16,0},{20,4},{24,8},{28,12},{1,17},{... | collective-permute-start | bytes 196616 | tf_op jit(solution)/shard_map/ppermute | solution.py:466
  6.4 2.9 %collective-permute-done = bf16[256,128]{1,0:T(8,128)(2,1)S(1)} collective-permute-done((bf16[256,128]{1,0:T(8,128)(2,1)S(1)}, bf16[256,128]{1,0:T(8,128)(2,1)S(1)}, u32[]{:S(2)}, u32[]{:S(2)}) %collective-permute-start) | collective-permute-done | bytes 65568 | tf_op jit(solution)/shard_map/ppermute | solution.py:466
  12.4 3.4 %collective-permute-start.1 = (bf16[128,512]{1,0:T(8,128)(2,1)S(1)}, bf16[128,512]{1,0:T(8,128)(2,1)S(1)}, u32[]{:S(2)}, u32[]{:S(2)}) collective-permute-start(bf16[128,512]{1,0:T(8,128)(2,1)S(1)} %shard_map.378), channel_id=1, source_target_pairs={{0,16},{4,20},{8,24},{12,28},{16,0},{20,4},{24,8},{28,12},{1,17},{... | collective-permute-start | bytes 393224 | tf_op jit(solution)/shard_map/ppermute | solution.py:466
  16.4 1.6 %collective-permute-start.9 = (bf16[512,128]{1,0:T(8,128)(2,1)S(1)}, bf16[512,128]{1,0:T(8,128)(2,1)S(1)}, u32[]{:S(2)}, u32[]{:S(2)}) collective-permute-start(bf16[512,128]{1,0:T(8,128)(2,1)S(1)} %bitcast.138), channel_id=1, source_target_pairs={{0,4},{4,0},{8,12},{12,8},{16,20},{20,16},{24,28},{28,24},{1,5},{5... | collective-permute-start | bytes 393224 | tf_op jit(solution)/shard_map/ppermute | solution.py:466
  18.0 1.5 %collective-permute-start.8 = (bf16[512,128]{1,0:T(8,128)(2,1)S(1)}, bf16[512,128]{1,0:T(8,128)(2,1)S(1)}, u32[]{:S(2)}, u32[]{:S(2)}) collective-permute-start(bf16[512,128]{1,0:T(8,128)(2,1)S(1)} %bitcast.136), channel_id=1, source_target_pairs={{0,2},{1,3},{2,0},{3,1},{4,6},{5,7},{6,4},{7,5},{8,10},{9,11},{10,... | collective-permute-start | bytes 393224 | tf_op jit(solution)/shard_map/ppermute | solution.py:466
  19.5 2.1 %collective-permute-done.1 = bf16[128,512]{1,0:T(8,128)(2,1)S(1)} collective-permute-done((bf16[128,512]{1,0:T(8,128)(2,1)S(1)}, bf16[128,512]{1,0:T(8,128)(2,1)S(1)}, u32[]{:S(2)}, u32[]{:S(2)}) %collective-permute-start.1) | collective-permute-done | bytes 131104 | tf_op jit(solution)/shard_map/ppermute | solution.py:466
  23.5 1.6 %collective-permute-start.11 = (bf16[1024,128]{1,0:T(8,128)(2,1)S(1)}, bf16[1024,128]{1,0:T(8,128)(2,1)S(1)}, u32[]{:S(2)}, u32[]{:S(2)}) collective-permute-start(bf16[1024,128]{1,0:T(8,128)(2,1)S(1)} %bitcast.127), channel_id=1, source_target_pairs={{0,2},{1,3},{2,0},{3,1},{4,6},{5,7},{6,4},{7,5},{8,10},{9,11},{10,... | collective-permute-start | bytes 786440 | tf_op jit(solution)/shard_map/ppermute | solution.py:466
  30.4 1.6 %collective-permute-start.4 = (bf16[256,512]{1,0:T(8,128)(2,1)S(1)}, bf16[256,512]{1,0:T(8,128)(2,1)S(1)}, u32[]{:S(2)}, u32[]{:S(2)}) collective-permute-start(bf16[256,512]{1,0:T(8,128)(2,1)S(1)} %bitcast.118), channel_id=1, source_target_pairs={{0,4},{4,0},{8,12},{12,8},{16,20},{20,16},{24,28},{28,24},{1,5},{5... | collective-permute-start | bytes 786440 | tf_op jit(solution)/shard_map/ppermute | solution.py:466
  32.0 3.6 %collective-permute-start.3 = (bf16[256,512]{1,0:T(8,128)(2,1)S(1)}, bf16[256,512]{1,0:T(8,128)(2,1)S(1)}, u32[]{:S(2)}, u32[]{:S(2)}) collective-permute-start(bf16[256,512]{1,0:T(8,128)(2,1)S(1)} %bitcast.97), channel_id=1, source_target_pairs={{0,2},{1,3},{2,0},{3,1},{4,6},{5,7},{6,4},{7,5},{8,10},{9,11},{10,... | collective-permute-start | bytes 786440 | tf_op jit(solution)/shard_map/ppermute | solution.py:466
  37.1 2.7 %collective-permute-start.16 = (bf16[1024,128]{1,0:T(8,128)(2,1)S(1)}, bf16[1024,128]{1,0:T(8,128)(2,1)S(1)}, u32[]{:S(2)}, u32[]{:S(2)}) collective-permute-start(bf16[1024,128]{1,0:T(8,128)(2,1)S(1)} %get-tuple-element.275), channel_id=1, source_target_pairs={{0,1},{1,0},{2,3},{3,2},{4,5},{5,4},{6,7},{7,6},{8,9},{9,8},{10,11... | collective-permute-start | bytes 786440 | tf_op jit(solution)/shard_map/ppermute | solution.py:466
  40.7 1.3 collective-permute-done.3
  42.6 1.8 %collective-permute-start.13 = (bf16[512,512]{1,0:T(8,128)(2,1)S(1)}, bf16[512,512]{1,0:T(8,128)(2,1)S(1)}, u32[]{:S(2)}, u32[]{:S(2)}) collective-permute-start(bf16[512,512]{1,0:T(8,128)(2,1)S(1)} %bitcast.108), channel_id=1, source_target_pairs={{0,2},{1,3},{2,0},{3,1},{4,6},{5,7},{6,4},{7,5},{8,10},{9,11},{10,... | collective-permute-start | bytes 1572872 | tf_op jit(solution)/shard_map/ppermute | solution.py:466
  45.2 5.1 %shard_map.388 = (bf16[544,1536]{1,0:T(8,128)(2,1)S(1)}, f32[5,4,112,256]{3,2,1,0:T(8,128)S(1)}, bf16[512,512]{1,0:T(8,128)(2,1)S(1)}, bf16[528,512]{1,0:T(8,128...) custom-call(s32[8]{0:T(128)S(1)} %concatenate.6.refs_0_, ...), custom_call_target="tpu_custom_call" | custom-call | flops 5000000000 | bytes 6000000 | tf_op jit(solution)/shard_map/pallas_call | solution.py:453
  50.4 6.0 %shard_map.389 = (bf16[544,1536]{1,0:T(8,128)(2,1)S(1)}, f32[5,4,112,256]{3,2,1,0:T(8,128)S(1)}, bf16[512,512]{1,0:T(8,128)(2,1)S(1)}, bf16[528,512]{1,0:T(8,128...) custom-call(s32[8]{0:T(128)S(1)} %concatenate.6.refs_0_, ...), custom_call_target="tpu_custom_call" | custom-call | flops 5000000000 | bytes 6000000 | tf_op jit(solution)/shard_map/pallas_call | solution.py:453
  58.6 7.5 %shard_map.391 = (f32[2,512,512]{2,1,0:T(8,128)S(1)}, f32[2,528,512]{2,1,0:T(8,128)S(1)}, bf16[1024,512]{1,0:T(8,128)(2,1)S(1)}, bf16[1024,512]{1,0:T(8,128)(2,1)S(1)}) custom-call(bf16[1024,512]{1,0:T(8,128)(2,1)S(1)} %bitcast.148, bf16[1024,512]{1,0:T(8,128)(2,1)S(1)} %bitcast.150, bf16[528,512]{1,0:T(8,128)(2,1)S(1)} %get-tuple-element.157.refs_2_, ...), custom_call_target="tpu_custom_call" | custom-call | flops 8000000000 | bytes 6000000 | tf_op jit(solution)/shard_map/pallas_call | solution.py:453
  66.1 7.9 %shard_map.392 = (bf16[2,512,512]{2,1,0:T(8,128)(2,1)S(1)}, f32[2,528,512]{2,1,0:T(8,128)S(1)}, bf16[1024,512]{1,0:T(8,128)(2,1)S(1)}, bf16[1024,512]{1,0:T(8,128)(2,1)S(1)}) custom-call(bf16[1024,512]{1,0:T(8,128)(2,1)S(1)} %collective-permute-done.18.refs_0_, bf16[1024,512]{1,0:T(8,128)(2,1)S(1)} %collective-permute-done.19.refs_1_, ...), custom_call_target="tpu_custom_call" | custom-call | flops 8000000000 | bytes 6000000 | tf_op jit(solution)/shard_map/pallas_call | solution.py:453
  74.6 5.6 %shard_map.393 = (f32[512,512]{1,0:T(8,128)S(1)}, bf16[512,512]{1,0:T(8,128)(2,1)S(1)}, bf16[512,1536]{1,0:T(8,128)(2,1)S(1)}, f32[2,512]{1,0:T(2,128)S(1)}) custom-call(f32[2,528,512]{2,1,0:T(8,128)S(1)} %get-tuple-element.166.refs_0_.refs_1_, f32[528,512]{1,0:T(8,128)S(1)} %get-tuple-element.163.refs_7_.refs_1_, ...), custom_call_target="tpu_custom_call" | custom-call | flops 8000000000 | bytes 6000000 | tf_op jit(solution)/shard_map/pallas_call | solution.py:453
  81.3 1.7 %collective-permute-start.25 = (bf16[512,512]{1,0:T(8,128)(2,1)S(1)}, bf16[512,512]{1,0:T(8,128)(2,1)S(1)}, u32[]{:S(2)}, u32[]{:S(2)}) collective-permute-start(bf16[512,512]{1,0:T(8,128)(2,1)S(1)} %get-tuple-element.193), channel_id=1, source_target_pairs={{0,2},{1,3},{2,0},{3,1},{4,6},{5,7},{6,4},{7,5},{8,10},{9,11},{10,... | collective-permute-start | bytes 1572872 | tf_op jit(solution)/shard_map/ppermute | solution.py:466
  83.8 10.5 %shard_map.395 = (f32[512,512]{1,0:T(8,128)S(1)}, bf16[512,512]{1,0:T(8,128)(2,1)}, bf16[512,1536]{1,0:T(8,128)(2,1)S(1)}, f32[2,512]{1,0:T(2,128)S(1)}, bf16[20...) custom-call(s32[8]{0:T(128)S(1)} %concatenate.6.refs_0_, ...), custom_call_target="tpu_custom_call" | custom-call | flops 10000000000 | bytes 6000000 | tf_op jit(solution)/shard_map/pallas_call | solution.py:453
  95.3 1.4 %collective-permute-done.24 = bf16[512,512]{1,0:T(8,128)(2,1)S(1)} collective-permute-done((bf16[512,512]{1,0:T(8,128)(2,1)S(1)}, bf16[512,512]{1,0:T(8,128)(2,1)S(1)}, u32[]{:S(2)}, u32[]{:S(2)}) %collective-permute-start.24) | collective-permute-done | bytes 524320 | tf_op jit(solution)/shard_map/ppermute | solution.py:466
  97.4 1.8 %collective-permute-start.32 = (bf16[2,256,512]{2,1,0:T(8,128)(2,1)S(1)}, bf16[2,256,512]{2,1,0:T(8,128)(2,1)S(1)}, u32[]{:S(2)}, u32[]{:S(2)}) collective-permute-start(bf16[2,256,512]{2,1,0:T(8,128)(2,1)S(1)} %get-tuple-element.194.refs_5_), channel_id=1, source_target_pairs={{0,8},{4,12},{8,0},{12,4},{16,24},{20,28},{24,16},{28,20},{1,9},{5... | collective-permute-start | bytes 1572872 | tf_op jit(solution)/shard_map/ppermute | solution.py:466
  100.5 1.7 %collective-permute-start.26 = (bf16[1024,128]{1,0:T(8,128)(2,1)S(1)}, bf16[1024,128]{1,0:T(8,128)(2,1)S(1)}, u32[]{:S(2)}, u32[]{:S(2)}) collective-permute-start(bf16[1024,128]{1,0:T(8,128)(2,1)S(1)} %get-tuple-element.195.refs_10_), channel_id=1, source_target_pairs={{0,4},{4,0},{8,12},{12,8},{16,20},{20,16},{24,28},{28,24},{1,5},{5... | collective-permute-start | bytes 786440 | tf_op jit(solution)/shard_map/ppermute | solution.py:466
  102.2 3.4 %shard_map.398 = (f32[512,512]{1,0:T(8,128)S(1)}, f32[512,512]{1,0:T(8,128)S(1)}, f32[16,128]{1,0:T(8,128)S(1)}) custom-call(f32[4,512]{1,0:T(4,128)S(1)} %copy-done.14, bf16[512,1536]{1,0:T(8,128)(2,1)S(1)} %get-tuple-element.152.refs_3_.refs_1_, bf16[512,1536]{1,0:T(8,128)(2,1)S(1)} %get-tuple-element.169.refs_5_.refs_12_.refs_2_, ...), custom_call_target="tpu_custom_call" | custom-call | flops 3000000000 | bytes 6000000 | tf_op jit(solution)/shard_map/pallas_call | solution.py:453
  105.7 1.2 collective-permute-done.28
  107.9 2.6 %collective-permute-done.29.refs_6_ = f32[16,128]{1,0:T(8,128)S(1)} collective-permute-done((f32[16,128]{1,0:T(8,128)S(1)}, f32[16,128]{1,0:T(8,128)S(1)}, u32[]{:S(2)}, u32[]{:S(2)}) %collective-permute-start.29) | collective-permute-done | bytes 8224 | tf_op jit(solution)/shard_map/ppermute | solution.py:466
  111.6 1.7 %collective-permute-start.30 = (bf16[512,128]{1,0:T(8,128)(2,1)S(1)}, bf16[512,128]{1,0:T(8,128)(2,1)S(1)}, u32[]{:S(2)}, u32[]{:S(2)}) collective-permute-start(bf16[512,128]{1,0:T(8,128)(2,1)S(1)} %get-tuple-element.204.refs_4_), channel_id=1, source_target_pairs={{0,2},{1,3},{2,0},{3,1},{4,6},{5,7},{6,4},{7,5},{8,10},{9,11},{10,... | collective-permute-start | bytes 393224 | tf_op jit(solution)/shard_map/ppermute | solution.py:466
  113.9 1.1 collective-permute-start.36
  118.3 2.0 %copy.46 = bf16[512,2,512]{2,1,0:T(2,128)(2,1)} copy(bf16[512,2,512]{2,0,1:T(8,128)(2,1)S(1)} %bitcast.88) | data formatting | bytes 2097152
  121.0 3.1 %collective-permute-start.37 = (bf16[2,64,512]{2,1,0:T(8,128)(2,1)S(1)}, bf16[2,64,512]{2,1,0:T(8,128)(2,1)S(1)}, u32[]{:S(2)}, u32[]{:S(2)}) collective-permute-start(bf16[2,64,512]{2,1,0:T(8,128)(2,1)S(1)} %get-tuple-element.225), channel_id=1, source_target_pairs={{0,16},{4,20},{8,24},{12,28},{16,0},{20,4},{24,8},{28,12},{1,17},{... | collective-permute-start | bytes 393224 | tf_op jit(solution)/shard_map/ppermute | solution.py:466
  124.7 1.9 %collective-permute-start.34 = (bf16[288,128]{1,0:T(8,128)(2,1)S(1)}, bf16[288,128]{1,0:T(8,128)(2,1)S(1)}, u32[]{:S(2)}, u32[]{:S(2)}) collective-permute-start(bf16[288,128]{1,0:T(8,128)(2,1)S(1)} %get-tuple-element.216), channel_id=1, source_target_pairs={{0,16},{4,20},{8,24},{12,28},{16,0},{20,4},{24,8},{28,12},{1,17},{... | collective-permute-start | bytes 221192 | tf_op jit(solution)/shard_map/ppermute | solution.py:466
  127.0 2.9 %copy.47 = f32[512,2,512]{2,1,0:T(2,128)} copy(f32[512,2,512]{2,0,1:T(8,128)S(1)} %maximum_bitcast_fusion) | data formatting | bytes 4194304
  129.9 1.1 collective-permute-done.34.refs_2_
  (120 shorter events, 33.5 us)
Async XLA Ops:
  1.6 7.8 %collective-permute-start = (bf16[256,128]{1,0:T(8,128)(2,1)S(1)}, bf16[256,128]{1,0:T(8,128)(2,1)S(1)}, u32[]{:S(2)}, u32[]{:S(2)}) collective-permute-start(bf16[256,128]{1,0:T(8,128)(2,1)S(1)} %bitcast.145), channel_id=1, source_target_pairs={{0,16},{4,20},{8,24},{12,28},{16,0},{20,4},{24,8},{28,12},{1,17},{... | collective-permute-start | bytes 196616 | tf_op jit(solution)/shard_map/ppermute | solution.py:466
  9.9 5.9 %collective-permute-start.5 = (bf16[512,128]{1,0:T(8,128)(2,1)S(1)}, bf16[512,128]{1,0:T(8,128)(2,1)S(1)}, u32[]{:S(2)}, u32[]{:S(2)}) collective-permute-start(bf16[512,128]{1,0:T(8,128)(2,1)S(1)} %bitcast.142), channel_id=1, source_target_pairs={{0,8},{4,12},{8,0},{12,4},{16,24},{20,28},{24,16},{28,20},{1,9},{5... | collective-permute-start | bytes 393224 | tf_op jit(solution)/shard_map/ppermute | solution.py:466
  12.4 9.2 %collective-permute-start.1 = (bf16[128,512]{1,0:T(8,128)(2,1)S(1)}, bf16[128,512]{1,0:T(8,128)(2,1)S(1)}, u32[]{:S(2)}, u32[]{:S(2)}) collective-permute-start(bf16[128,512]{1,0:T(8,128)(2,1)S(1)} %shard_map.378), channel_id=1, source_target_pairs={{0,16},{4,20},{8,24},{12,28},{16,0},{20,4},{24,8},{28,12},{1,17},{... | collective-permute-start | bytes 393224 | tf_op jit(solution)/shard_map/ppermute | solution.py:466
  16.4 5.8 %collective-permute-start.9 = (bf16[512,128]{1,0:T(8,128)(2,1)S(1)}, bf16[512,128]{1,0:T(8,128)(2,1)S(1)}, u32[]{:S(2)}, u32[]{:S(2)}) collective-permute-start(bf16[512,128]{1,0:T(8,128)(2,1)S(1)} %bitcast.138), channel_id=1, source_target_pairs={{0,4},{4,0},{8,12},{12,8},{16,20},{20,16},{24,28},{28,24},{1,5},{5... | collective-permute-start | bytes 393224 | tf_op jit(solution)/shard_map/ppermute | solution.py:466
  18.0 5.0 %collective-permute-start.8 = (bf16[512,128]{1,0:T(8,128)(2,1)S(1)}, bf16[512,128]{1,0:T(8,128)(2,1)S(1)}, u32[]{:S(2)}, u32[]{:S(2)}) collective-permute-start(bf16[512,128]{1,0:T(8,128)(2,1)S(1)} %bitcast.136), channel_id=1, source_target_pairs={{0,2},{1,3},{2,0},{3,1},{4,6},{5,7},{6,4},{7,5},{8,10},{9,11},{10,... | collective-permute-start | bytes 393224 | tf_op jit(solution)/shard_map/ppermute | solution.py:466
  22.1 7.7 %collective-permute-start.2 = (bf16[256,512]{1,0:T(8,128)(2,1)S(1)}, bf16[256,512]{1,0:T(8,128)(2,1)S(1)}, u32[]{:S(2)}, u32[]{:S(2)}) collective-permute-start(bf16[256,512]{1,0:T(8,128)(2,1)S(1)} %bitcast.82), channel_id=1, source_target_pairs={{0,8},{4,12},{8,0},{12,4},{16,24},{20,28},{24,16},{28,20},{1,9},{5... | collective-permute-start | bytes 786440 | tf_op jit(solution)/shard_map/ppermute | solution.py:466
  23.5 12.0 %collective-permute-start.11 = (bf16[1024,128]{1,0:T(8,128)(2,1)S(1)}, bf16[1024,128]{1,0:T(8,128)(2,1)S(1)}, u32[]{:S(2)}, u32[]{:S(2)}) collective-permute-start(bf16[1024,128]{1,0:T(8,128)(2,1)S(1)} %bitcast.127), channel_id=1, source_target_pairs={{0,2},{1,3},{2,0},{3,1},{4,6},{5,7},{6,4},{7,5},{8,10},{9,11},{10,... | collective-permute-start | bytes 786440 | tf_op jit(solution)/shard_map/ppermute | solution.py:466
  25.1 10.4 %collective-permute-start.10 = (bf16[1024,128]{1,0:T(8,128)(2,1)S(1)}, bf16[1024,128]{1,0:T(8,128)(2,1)S(1)}, u32[]{:S(2)}, u32[]{:S(2)}) collective-permute-start(bf16[1024,128]{1,0:T(8,128)(2,1)S(1)} %bitcast.125), channel_id=1, source_target_pairs={{0,4},{4,0},{8,12},{12,8},{16,20},{20,16},{24,28},{28,24},{1,5},{5... | collective-permute-start | bytes 786440 | tf_op jit(solution)/shard_map/ppermute | solution.py:466
  30.4 6.7 %collective-permute-start.4 = (bf16[256,512]{1,0:T(8,128)(2,1)S(1)}, bf16[256,512]{1,0:T(8,128)(2,1)S(1)}, u32[]{:S(2)}, u32[]{:S(2)}) collective-permute-start(bf16[256,512]{1,0:T(8,128)(2,1)S(1)} %bitcast.118), channel_id=1, source_target_pairs={{0,4},{4,0},{8,12},{12,8},{16,20},{20,16},{24,28},{28,24},{1,5},{5... | collective-permute-start | bytes 786440 | tf_op jit(solution)/shard_map/ppermute | solution.py:466
  32.0 10.0 %collective-permute-start.3 = (bf16[256,512]{1,0:T(8,128)(2,1)S(1)}, bf16[256,512]{1,0:T(8,128)(2,1)S(1)}, u32[]{:S(2)}, u32[]{:S(2)}) collective-permute-start(bf16[256,512]{1,0:T(8,128)(2,1)S(1)} %bitcast.97), channel_id=1, source_target_pairs={{0,2},{1,3},{2,0},{3,1},{4,6},{5,7},{6,4},{7,5},{8,10},{9,11},{10,... | collective-permute-start | bytes 786440 | tf_op jit(solution)/shard_map/ppermute | solution.py:466
  36.3 8.1 %collective-permute-start.15 = (bf16[1024,128]{1,0:T(8,128)(2,1)S(1)}, bf16[1024,128]{1,0:T(8,128)(2,1)S(1)}, u32[]{:S(2)}, u32[]{:S(2)}) collective-permute-start(bf16[1024,128]{1,0:T(8,128)(2,1)S(1)} %get-tuple-element.276), channel_id=1, source_target_pairs={{0,1},{1,0},{2,3},{3,2},{4,5},{5,4},{6,7},{7,6},{8,9},{9,8},{10,11... | collective-permute-start | bytes 786440 | tf_op jit(solution)/shard_map/ppermute | solution.py:466
  36.4 8.9 %collective-permute-start.14 = (bf16[1024,128]{1,0:T(8,128)(2,1)S(1)}, bf16[1024,128]{1,0:T(8,128)(2,1)S(1)}, u32[]{:S(2)}, u32[]{:S(2)}) collective-permute-start(bf16[1024,128]{1,0:T(8,128)(2,1)S(1)} %get-tuple-element.277), channel_id=1, source_target_pairs={{0,1},{1,0},{2,3},{3,2},{4,5},{5,4},{6,7},{7,6},{8,9},{9,8},{10,11... | collective-permute-start | bytes 786440 | tf_op jit(solution)/shard_map/ppermute | solution.py:466
  36.9 8.3 %collective-permute-start.17 = (bf16[1024,128]{1,0:T(8,128)(2,1)S(1)}, bf16[1024,128]{1,0:T(8,128)(2,1)S(1)}, u32[]{:S(2)}, u32[]{:S(2)}) collective-permute-start(bf16[1024,128]{1,0:T(8,128)(2,1)S(1)} %get-tuple-element.274), channel_id=1, source_target_pairs={{0,1},{1,0},{2,3},{3,2},{4,5},{5,4},{6,7},{7,6},{8,9},{9,8},{10,11... | collective-permute-start | bytes 786440 | tf_op jit(solution)/shard_map/ppermute | solution.py:466
  37.1 8.2 %collective-permute-start.16 = (bf16[1024,128]{1,0:T(8,128)(2,1)S(1)}, bf16[1024,128]{1,0:T(8,128)(2,1)S(1)}, u32[]{:S(2)}, u32[]{:S(2)}) collective-permute-start(bf16[1024,128]{1,0:T(8,128)(2,1)S(1)} %get-tuple-element.275), channel_id=1, source_target_pairs={{0,1},{1,0},{2,3},{3,2},{4,5},{5,4},{6,7},{7,6},{8,9},{9,8},{10,11... | collective-permute-start | bytes 786440 | tf_op jit(solution)/shard_map/ppermute | solution.py:466
  42.6 14.4 %collective-permute-start.13 = (bf16[512,512]{1,0:T(8,128)(2,1)S(1)}, bf16[512,512]{1,0:T(8,128)(2,1)S(1)}, u32[]{:S(2)}, u32[]{:S(2)}) collective-permute-start(bf16[512,512]{1,0:T(8,128)(2,1)S(1)} %bitcast.108), channel_id=1, source_target_pairs={{0,2},{1,3},{2,0},{3,1},{4,6},{5,7},{6,4},{7,5},{8,10},{9,11},{10,... | collective-permute-start | bytes 1572872 | tf_op jit(solution)/shard_map/ppermute | solution.py:466
  44.4 12.7 %collective-permute-start.12 = (bf16[512,512]{1,0:T(8,128)(2,1)S(1)}, bf16[512,512]{1,0:T(8,128)(2,1)S(1)}, u32[]{:S(2)}, u32[]{:S(2)}) collective-permute-start(bf16[512,512]{1,0:T(8,128)(2,1)S(1)} %bitcast.105), channel_id=1, source_target_pairs={{0,4},{4,0},{8,12},{12,8},{16,20},{20,16},{24,28},{28,24},{1,5},{5... | collective-permute-start | bytes 1572872 | tf_op jit(solution)/shard_map/ppermute | solution.py:466
  58.0 8.1 %collective-permute-start.19 = (bf16[1024,512]{1,0:T(8,128)(2,1)S(1)}, bf16[1024,512]{1,0:T(8,128)(2,1)S(1)}, u32[]{:S(2)}, u32[]{:S(2)}) collective-permute-start(bf16[1024,512]{1,0:T(8,128)(2,1)S(1)} %bitcast.149), channel_id=1, source_target_pairs={{0,1},{1,0},{2,3},{3,2},{4,5},{5,4},{6,7},{7,6},{8,9},{9,8},{10,11... | collective-permute-start | bytes 3145736 | tf_op jit(solution)/shard_map/ppermute | solution.py:466
  58.1 8.0 %collective-permute-start.18 = (bf16[1024,512]{1,0:T(8,128)(2,1)S(1)}, bf16[1024,512]{1,0:T(8,128)(2,1)S(1)}, u32[]{:S(2)}, u32[]{:S(2)}) collective-permute-start(bf16[1024,512]{1,0:T(8,128)(2,1)S(1)} %bitcast.147), channel_id=1, source_target_pairs={{0,1},{1,0},{2,3},{3,2},{4,5},{5,4},{6,7},{7,6},{8,9},{9,8},{10,11... | collective-permute-start | bytes 3145736 | tf_op jit(solution)/shard_map/ppermute | solution.py:466
  74.0 6.2 %collective-permute-start.20 = (bf16[1024,512]{1,0:T(8,128)(2,1)S(1)}, bf16[1024,512]{1,0:T(8,128)(2,1)S(1)}, u32[]{:S(2)}, u32[]{:S(2)}) collective-permute-start(bf16[1024,512]{1,0:T(8,128)(2,1)S(1)} %get-tuple-element.179), channel_id=1, source_target_pairs={{0,1},{1,0},{2,3},{3,2},{4,5},{5,4},{6,7},{7,6},{8,9},{9,8},{10,11... | collective-permute-start | bytes 3145736 | tf_op jit(solution)/shard_map/ppermute | solution.py:466
  74.1 6.1 %collective-permute-start.21 = (bf16[1024,512]{1,0:T(8,128)(2,1)S(1)}, bf16[1024,512]{1,0:T(8,128)(2,1)S(1)}, u32[]{:S(2)}, u32[]{:S(2)}) collective-permute-start(bf16[1024,512]{1,0:T(8,128)(2,1)S(1)} %get-tuple-element.181), channel_id=1, source_target_pairs={{0,1},{1,0},{2,3},{3,2},{4,5},{5,4},{6,7},{7,6},{8,9},{9,8},{10,11... | collective-permute-start | bytes 3145736 | tf_op jit(solution)/shard_map/ppermute | solution.py:466
  81.3 14.0 %collective-permute-start.25 = (bf16[512,512]{1,0:T(8,128)(2,1)S(1)}, bf16[512,512]{1,0:T(8,128)(2,1)S(1)}, u32[]{:S(2)}, u32[]{:S(2)}) collective-permute-start(bf16[512,512]{1,0:T(8,128)(2,1)S(1)} %get-tuple-element.193), channel_id=1, source_target_pairs={{0,2},{1,3},{2,0},{3,1},{4,6},{5,7},{6,4},{7,5},{8,10},{9,11},{10,... | collective-permute-start | bytes 1572872 | tf_op jit(solution)/shard_map/ppermute | solution.py:466
  83.0 13.6 %collective-permute-start.24 = (bf16[512,512]{1,0:T(8,128)(2,1)S(1)}, bf16[512,512]{1,0:T(8,128)(2,1)S(1)}, u32[]{:S(2)}, u32[]{:S(2)}) collective-permute-start(bf16[512,512]{1,0:T(8,128)(2,1)S(1)} %get-tuple-element.182.refs_14_), channel_id=1, source_target_pairs={{0,4},{4,0},{8,12},{12,8},{16,20},{20,16},{24,28},{28,24},{1,5},{5... | collective-permute-start | bytes 1572872 | tf_op jit(solution)/shard_map/ppermute | solution.py:466
  97.4 15.8 %collective-permute-start.32 = (bf16[2,256,512]{2,1,0:T(8,128)(2,1)S(1)}, bf16[2,256,512]{2,1,0:T(8,128)(2,1)S(1)}, u32[]{:S(2)}, u32[]{:S(2)}) collective-permute-start(bf16[2,256,512]{2,1,0:T(8,128)(2,1)S(1)} %get-tuple-element.194.refs_5_), channel_id=1, source_target_pairs={{0,8},{4,12},{8,0},{12,4},{16,24},{20,28},{24,16},{28,20},{1,9},{5... | collective-permute-start | bytes 1572872 | tf_op jit(solution)/shard_map/ppermute | solution.py:466
  100.1 10.4 %collective-permute-start.27 = (bf16[1024,128]{1,0:T(8,128)(2,1)S(1)}, bf16[1024,128]{1,0:T(8,128)(2,1)S(1)}, u32[]{:S(2)}, u32[]{:S(2)}) collective-permute-start(bf16[1024,128]{1,0:T(8,128)(2,1)S(1)} %get-tuple-element.200), channel_id=1, source_target_pairs={{0,2},{1,3},{2,0},{3,1},{4,6},{5,7},{6,4},{7,5},{8,10},{9,11},{10,... | collective-permute-start | bytes 786440 | tf_op jit(solution)/shard_map/ppermute | solution.py:466
  100.5 10.0 %collective-permute-start.26 = (bf16[1024,128]{1,0:T(8,128)(2,1)S(1)}, bf16[1024,128]{1,0:T(8,128)(2,1)S(1)}, u32[]{:S(2)}, u32[]{:S(2)}) collective-permute-start(bf16[1024,128]{1,0:T(8,128)(2,1)S(1)} %get-tuple-element.195.refs_10_), channel_id=1, source_target_pairs={{0,4},{4,0},{8,12},{12,8},{16,20},{20,16},{24,28},{28,24},{1,5},{5... | collective-permute-start | bytes 786440 | tf_op jit(solution)/shard_map/ppermute | solution.py:466
  111.2 6.2 %collective-permute-start.31 = (bf16[544,128]{1,0:T(8,128)(2,1)S(1)}, bf16[544,128]{1,0:T(8,128)(2,1)S(1)}, u32[]{:S(2)}, u32[]{:S(2)}) collective-permute-start(bf16[544,128]{1,0:T(8,128)(2,1)S(1)} %get-tuple-element.205), channel_id=1, source_target_pairs={{0,4},{4,0},{8,12},{12,8},{16,20},{20,16},{24,28},{28,24},{1,5},{5... | collective-permute-start | bytes 417800 | tf_op jit(solution)/shard_map/ppermute | solution.py:466
  111.6 5.4 %collective-permute-start.30 = (bf16[512,128]{1,0:T(8,128)(2,1)S(1)}, bf16[512,128]{1,0:T(8,128)(2,1)S(1)}, u32[]{:S(2)}, u32[]{:S(2)}) collective-permute-start(bf16[512,128]{1,0:T(8,128)(2,1)S(1)} %get-tuple-element.204.refs_4_), channel_id=1, source_target_pairs={{0,2},{1,3},{2,0},{3,1},{4,6},{5,7},{6,4},{7,5},{8,10},{9,11},{10,... | collective-permute-start | bytes 393224 | tf_op jit(solution)/shard_map/ppermute | solution.py:466
  113.9 6.5 %collective-permute-start.36 = (bf16[128,512]{1,0:T(8,128)(2,1)S(1)}, bf16[128,512]{1,0:T(8,128)(2,1)S(1)}, u32[]{:S(2)}, u32[]{:S(2)}) collective-permute-start(bf16[128,512]{1,0:T(8,128)(2,1)S(1)} %get-tuple-element.222), channel_id=1, source_target_pairs={{0,4},{4,0},{8,12},{12,8},{16,20},{20,16},{24,28},{28,24},{1,5},{5... | collective-permute-start | bytes 393224 | tf_op jit(solution)/shard_map/ppermute | solution.py:466
  115.0 5.4 %collective-permute-start.35 = (bf16[128,512]{1,0:T(8,128)(2,1)S(1)}, bf16[128,512]{1,0:T(8,128)(2,1)S(1)}, u32[]{:S(2)}, u32[]{:S(2)}) collective-permute-start(bf16[128,512]{1,0:T(8,128)(2,1)S(1)} %get-tuple-element.209.refs_6_), channel_id=1, source_target_pairs={{0,2},{1,3},{2,0},{3,1},{4,6},{5,7},{6,4},{7,5},{8,10},{9,11},{10,... | collective-permute-start | bytes 393224 | tf_op jit(solution)/shard_map/ppermute | solution.py:466
  117.9 6.2 %collective-permute-start.33 = (bf16[544,128]{1,0:T(8,128)(2,1)S(1)}, bf16[544,128]{1,0:T(8,128)(2,1)S(1)}, u32[]{:S(2)}, u32[]{:S(2)}) collective-permute-start(bf16[544,128]{1,0:T(8,128)(2,1)S(1)} %get-tuple-element.212), channel_id=1, source_target_pairs={{0,8},{4,12},{8,0},{12,4},{16,24},{20,28},{24,16},{28,20},{1,9},{5... | collective-permute-start | bytes 417800 | tf_op jit(solution)/shard_map/ppermute | solution.py:466
  121.0 11.0 %collective-permute-start.37 = (bf16[2,64,512]{2,1,0:T(8,128)(2,1)S(1)}, bf16[2,64,512]{2,1,0:T(8,128)(2,1)S(1)}, u32[]{:S(2)}, u32[]{:S(2)}) collective-permute-start(bf16[2,64,512]{2,1,0:T(8,128)(2,1)S(1)} %get-tuple-element.225), channel_id=1, source_target_pairs={{0,16},{4,20},{8,24},{12,28},{16,0},{20,4},{24,8},{28,12},{1,17},{... | collective-permute-start | bytes 393224 | tf_op jit(solution)/shard_map/ppermute | solution.py:466
  124.7 6.3 %collective-permute-start.34 = (bf16[288,128]{1,0:T(8,128)(2,1)S(1)}, bf16[288,128]{1,0:T(8,128)(2,1)S(1)}, u32[]{:S(2)}, u32[]{:S(2)}) collective-permute-start(bf16[288,128]{1,0:T(8,128)(2,1)S(1)} %get-tuple-element.216), channel_id=1, source_target_pairs={{0,16},{4,20},{8,24},{12,28},{16,0},{20,4},{24,8},{28,12},{1,17},{... | collective-permute-start | bytes 221192 | tf_op jit(solution)/shard_map/ppermute | solution.py:466
  (25 other events, 118.9 us)

commit v3 on v2

--- a/solution.py
+++ b/solution.py
@@ -233,12 +233,10 @@
 def gelu_parts(value):
     slope = math.sqrt(2.0 / math.pi)
     square = value * value
-    tanh = jnp.tanh(value * (slope + (slope * 0.044715) * square))
-    half = 0.5 + 0.5 * tanh
-    curve = half + (0.5 * value) * (1.0 - tanh * tanh) * (
-        slope + (slope * 3.0 * 0.044715) * square
-    )
-    return value * half, curve
+    half = 0.5 + 0.5 * jnp.tanh(value * (slope + (slope * 0.044715) * square))
+    active = value * half
+    curve = half + (active * (1.0 - half)) * (2.0 * slope + (slope * 6.0 * 0.044715) * square)
+    return active, curve
 
 
 def feed_half(
@@ -654,6 +652,7 @@
 
 def update_feed_kernel(keep_e, keep_r, got_ref, *refs):
     states, outs = refs[:6], refs[6:]
+    outs[10][...] = jnp.zeros_like(outs[10])
     for i, keep in enumerate((keep_e, keep_r)):
         gradient = keep[...] + got_ref[i].astype(f32)
         state = [ref[...] for ref in states[3 * i : 3 * i + 3]]
@@ -892,13 +891,14 @@
             keep_e, keep_r, two_got, weight_expand, moment_expand, average_expand,
             weight_reduce, moment_reduce, average_reduce,
         ),
-        weighed(weight_expand) + weighed(weight_reduce),
+        weighed(weight_expand) + weighed(weight_reduce) + [((8, 128), f32)],
         flops=1e8,
         smem=0,
         mib=8,
     )
     gradient_expand, mom_expand, avg_expand, new_expand, low_expand = updated[:5]
-    gradient_reduce, mom_reduce, avg_reduce, new_reduce, low_reduce = updated[5:]
+    gradient_reduce, mom_reduce, avg_reduce, new_reduce, low_reduce = updated[5:10]
+    fed_done = updated[10]
     updated = call(
         update_rest_kernel,
         (
@@ -906,6 +906,7 @@
             weight_combine, moment_combine, average_combine, norm_params, norm_moment, norm_average,
         ),
         weighed(weight_project) + weighed(weight_combine) + plain(norm_params),
+        waits=(fed_done,),
         flops=1e8,
         smem=0,
         mib=8,

time: 133 us -> 133 us (level)
  no operation moved by 1% of the time
where the time goes in v3:
time: 133 us
  Pallas kernels  60.9 us (46%)
  starting transfers between devices  44.4 us (33%)
  waiting for transfers between devices  16.9 us (13%)
  local copies, waits for them, and re-layouts  8.05 us (6%)
  between operations  1.41 us (1%)
    pallas_call x29, Pallas kernels, call(): pl.pallas_call(body, out_shape=tuple((jax.ShapeDtypeStruct(shape, kind) f...  60.9 us
    ppermute x37, starting transfers between devices, swap(): return lax.ppermute(value, axis, [(i, i ^ 1 << bit) for i in range(n)])  43.8 us
    ppermute x37, waiting for transfers between devices, swap(): return lax.ppermute(value, axis, [(i, i ^ 1 << bit) for i in range(n)])  16.9 us
    unnamed x40, local copies, waits for them, and re-layouts  6.89 us
  transfers between devices with their start and end apart: 38, of which 15 were waited for; matrix products, arithmetic and copies ran while one was open for 5% of the time, Pallas kernels for 37%

profile of v3, /device:TPU:0, one launch (start us, length us, event | category | flops | bytes accessed | tf_op | source)
XLA Modules:
  0.0 132.8 jit_solution(14986746927075572658)
XLA Ops:
  1.6 4.1 %collective-permute-start = (bf16[256,128]{1,0:T(8,128)(2,1)S(1)}, bf16[256,128]{1,0:T(8,128)(2,1)S(1)}, u32[]{:S(2)}, u32[]{:S(2)}) collective-permute-start(bf16[256,128]{1,0:T(8,128)(2,1)S(1)} %bitcast.145), channel_id=1, source_target_pairs={{0,16},{4,20},{8,24},{12,28},{16,0},{20,4},{24,8},{28,12},{1,17},{... | collective-permute-start | bytes 196616 | tf_op jit(solution)/shard_map/ppermute | solution.py:464
  6.4 2.9 %collective-permute-done = bf16[256,128]{1,0:T(8,128)(2,1)S(1)} collective-permute-done((bf16[256,128]{1,0:T(8,128)(2,1)S(1)}, bf16[256,128]{1,0:T(8,128)(2,1)S(1)}, u32[]{:S(2)}, u32[]{:S(2)}) %collective-permute-start) | collective-permute-done | bytes 65568 | tf_op jit(solution)/shard_map/ppermute | solution.py:464
  12.4 3.4 %collective-permute-start.1 = (bf16[128,512]{1,0:T(8,128)(2,1)S(1)}, bf16[128,512]{1,0:T(8,128)(2,1)S(1)}, u32[]{:S(2)}, u32[]{:S(2)}) collective-permute-start(bf16[128,512]{1,0:T(8,128)(2,1)S(1)} %shard_map.378), channel_id=1, source_target_pairs={{0,16},{4,20},{8,24},{12,28},{16,0},{20,4},{24,8},{28,12},{1,17},{... | collective-permute-start | bytes 393224 | tf_op jit(solution)/shard_map/ppermute | solution.py:464
  16.4 1.6 %collective-permute-start.9 = (bf16[512,128]{1,0:T(8,128)(2,1)S(1)}, bf16[512,128]{1,0:T(8,128)(2,1)S(1)}, u32[]{:S(2)}, u32[]{:S(2)}) collective-permute-start(bf16[512,128]{1,0:T(8,128)(2,1)S(1)} %bitcast.138), channel_id=1, source_target_pairs={{0,4},{4,0},{8,12},{12,8},{16,20},{20,16},{24,28},{28,24},{1,5},{5... | collective-permute-start | bytes 393224 | tf_op jit(solution)/shard_map/ppermute | solution.py:464
  18.0 1.5 %collective-permute-start.8 = (bf16[512,128]{1,0:T(8,128)(2,1)S(1)}, bf16[512,128]{1,0:T(8,128)(2,1)S(1)}, u32[]{:S(2)}, u32[]{:S(2)}) collective-permute-start(bf16[512,128]{1,0:T(8,128)(2,1)S(1)} %bitcast.136), channel_id=1, source_target_pairs={{0,2},{1,3},{2,0},{3,1},{4,6},{5,7},{6,4},{7,5},{8,10},{9,11},{10,... | collective-permute-start | bytes 393224 | tf_op jit(solution)/shard_map/ppermute | solution.py:464
  19.5 2.1 %collective-permute-done.1 = bf16[128,512]{1,0:T(8,128)(2,1)S(1)} collective-permute-done((bf16[128,512]{1,0:T(8,128)(2,1)S(1)}, bf16[128,512]{1,0:T(8,128)(2,1)S(1)}, u32[]{:S(2)}, u32[]{:S(2)}) %collective-permute-start.1) | collective-permute-done | bytes 131104 | tf_op jit(solution)/shard_map/ppermute | solution.py:464
  23.5 1.6 %collective-permute-start.11 = (bf16[1024,128]{1,0:T(8,128)(2,1)S(1)}, bf16[1024,128]{1,0:T(8,128)(2,1)S(1)}, u32[]{:S(2)}, u32[]{:S(2)}) collective-permute-start(bf16[1024,128]{1,0:T(8,128)(2,1)S(1)} %bitcast.127), channel_id=1, source_target_pairs={{0,2},{1,3},{2,0},{3,1},{4,6},{5,7},{6,4},{7,5},{8,10},{9,11},{10,... | collective-permute-start | bytes 786440 | tf_op jit(solution)/shard_map/ppermute | solution.py:464
  30.4 1.6 %collective-permute-start.4 = (bf16[256,512]{1,0:T(8,128)(2,1)S(1)}, bf16[256,512]{1,0:T(8,128)(2,1)S(1)}, u32[]{:S(2)}, u32[]{:S(2)}) collective-permute-start(bf16[256,512]{1,0:T(8,128)(2,1)S(1)} %bitcast.118), channel_id=1, source_target_pairs={{0,4},{4,0},{8,12},{12,8},{16,20},{20,16},{24,28},{28,24},{1,5},{5... | collective-permute-start | bytes 786440 | tf_op jit(solution)/shard_map/ppermute | solution.py:464
  32.0 3.6 %collective-permute-start.3 = (bf16[256,512]{1,0:T(8,128)(2,1)S(1)}, bf16[256,512]{1,0:T(8,128)(2,1)S(1)}, u32[]{:S(2)}, u32[]{:S(2)}) collective-permute-start(bf16[256,512]{1,0:T(8,128)(2,1)S(1)} %bitcast.97), channel_id=1, source_target_pairs={{0,2},{1,3},{2,0},{3,1},{4,6},{5,7},{6,4},{7,5},{8,10},{9,11},{10,... | collective-permute-start | bytes 786440 | tf_op jit(solution)/shard_map/ppermute | solution.py:464
  37.1 2.7 %collective-permute-start.16 = (bf16[1024,128]{1,0:T(8,128)(2,1)S(1)}, bf16[1024,128]{1,0:T(8,128)(2,1)S(1)}, u32[]{:S(2)}, u32[]{:S(2)}) collective-permute-start(bf16[1024,128]{1,0:T(8,128)(2,1)S(1)} %get-tuple-element.277), channel_id=1, source_target_pairs={{0,1},{1,0},{2,3},{3,2},{4,5},{5,4},{6,7},{7,6},{8,9},{9,8},{10,11... | collective-permute-start | bytes 786440 | tf_op jit(solution)/shard_map/ppermute | solution.py:464
  40.7 1.3 collective-permute-done.3
  42.6 1.8 %collective-permute-start.13 = (bf16[512,512]{1,0:T(8,128)(2,1)S(1)}, bf16[512,512]{1,0:T(8,128)(2,1)S(1)}, u32[]{:S(2)}, u32[]{:S(2)}) collective-permute-start(bf16[512,512]{1,0:T(8,128)(2,1)S(1)} %bitcast.108), channel_id=1, source_target_pairs={{0,2},{1,3},{2,0},{3,1},{4,6},{5,7},{6,4},{7,5},{8,10},{9,11},{10,... | collective-permute-start | bytes 1572872 | tf_op jit(solution)/shard_map/ppermute | solution.py:464
  45.2 5.1 %shard_map.388 = (bf16[544,1536]{1,0:T(8,128)(2,1)S(1)}, f32[5,4,112,256]{3,2,1,0:T(8,128)S(1)}, bf16[512,512]{1,0:T(8,128)(2,1)S(1)}, bf16[528,512]{1,0:T(8,128...) custom-call(s32[8]{0:T(128)S(1)} %concatenate.6.refs_0_, ...), custom_call_target="tpu_custom_call" | custom-call | flops 5000000000 | bytes 6000000 | tf_op jit(solution)/shard_map/pallas_call | solution.py:451
  50.4 6.0 %shard_map.389 = (bf16[544,1536]{1,0:T(8,128)(2,1)S(1)}, f32[5,4,112,256]{3,2,1,0:T(8,128)S(1)}, bf16[512,512]{1,0:T(8,128)(2,1)S(1)}, bf16[528,512]{1,0:T(8,128...) custom-call(s32[8]{0:T(128)S(1)} %concatenate.6.refs_0_, ...), custom_call_target="tpu_custom_call" | custom-call | flops 5000000000 | bytes 6000000 | tf_op jit(solution)/shard_map/pallas_call | solution.py:451
  58.6 7.6 %shard_map.391 = (f32[2,512,512]{2,1,0:T(8,128)S(1)}, f32[2,528,512]{2,1,0:T(8,128)S(1)}, bf16[1024,512]{1,0:T(8,128)(2,1)S(1)}, bf16[1024,512]{1,0:T(8,128)(2,1)S(1)}) custom-call(bf16[1024,512]{1,0:T(8,128)(2,1)S(1)} %bitcast.148, bf16[1024,512]{1,0:T(8,128)(2,1)S(1)} %bitcast.150, bf16[528,512]{1,0:T(8,128)(2,1)S(1)} %get-tuple-element.158.refs_2_, ...), custom_call_target="tpu_custom_call" | custom-call | flops 8000000000 | bytes 6000000 | tf_op jit(solution)/shard_map/pallas_call | solution.py:451
  66.2 7.8 %shard_map.392 = (bf16[2,512,512]{2,1,0:T(8,128)(2,1)S(1)}, f32[2,528,512]{2,1,0:T(8,128)S(1)}, bf16[1024,512]{1,0:T(8,128)(2,1)S(1)}, bf16[1024,512]{1,0:T(8,128)(2,1)S(1)}) custom-call(bf16[1024,512]{1,0:T(8,128)(2,1)S(1)} %collective-permute-done.18.refs_0_, bf16[1024,512]{1,0:T(8,128)(2,1)S(1)} %collective-permute-done.19.refs_1_, ...), custom_call_target="tpu_custom_call" | custom-call | flops 8000000000 | bytes 6000000 | tf_op jit(solution)/shard_map/pallas_call | solution.py:451
  74.6 5.6 %shard_map.393 = (f32[512,512]{1,0:T(8,128)S(1)}, bf16[512,512]{1,0:T(8,128)(2,1)S(1)}, bf16[512,1536]{1,0:T(8,128)(2,1)S(1)}, f32[2,512]{1,0:T(2,128)S(1)}) custom-call(f32[2,528,512]{2,1,0:T(8,128)S(1)} %get-tuple-element.167.refs_0_.refs_1_, f32[528,512]{1,0:T(8,128)S(1)} %get-tuple-element.164.refs_7_.refs_1_, ...), custom_call_target="tpu_custom_call" | custom-call | flops 8000000000 | bytes 6000000 | tf_op jit(solution)/shard_map/pallas_call | solution.py:451
  81.3 1.7 %collective-permute-start.25 = (bf16[512,512]{1,0:T(8,128)(2,1)S(1)}, bf16[512,512]{1,0:T(8,128)(2,1)S(1)}, u32[]{:S(2)}, u32[]{:S(2)}) collective-permute-start(bf16[512,512]{1,0:T(8,128)(2,1)S(1)} %get-tuple-element.194), channel_id=1, source_target_pairs={{0,2},{1,3},{2,0},{3,1},{4,6},{5,7},{6,4},{7,5},{8,10},{9,11},{10,... | collective-permute-start | bytes 1572872 | tf_op jit(solution)/shard_map/ppermute | solution.py:464
  83.8 10.5 %shard_map.395 = (f32[512,512]{1,0:T(8,128)S(1)}, bf16[512,512]{1,0:T(8,128)(2,1)}, bf16[512,1536]{1,0:T(8,128)(2,1)S(1)}, f32[2,512]{1,0:T(2,128)S(1)}, bf16[20...) custom-call(s32[8]{0:T(128)S(1)} %concatenate.6.refs_0_, ...), custom_call_target="tpu_custom_call" | custom-call | flops 10000000000 | bytes 6000000 | tf_op jit(solution)/shard_map/pallas_call | solution.py:451
  95.5 1.4 %collective-permute-done.24 = bf16[512,512]{1,0:T(8,128)(2,1)S(1)} collective-permute-done((bf16[512,512]{1,0:T(8,128)(2,1)S(1)}, bf16[512,512]{1,0:T(8,128)(2,1)S(1)}, u32[]{:S(2)}, u32[]{:S(2)}) %collective-permute-start.24) | collective-permute-done | bytes 524320 | tf_op jit(solution)/shard_map/ppermute | solution.py:464
  97.7 1.8 %collective-permute-start.32 = (bf16[2,256,512]{2,1,0:T(8,128)(2,1)S(1)}, bf16[2,256,512]{2,1,0:T(8,128)(2,1)S(1)}, u32[]{:S(2)}, u32[]{:S(2)}) collective-permute-start(bf16[2,256,512]{2,1,0:T(8,128)(2,1)S(1)} %get-tuple-element.195.refs_5_), channel_id=1, source_target_pairs={{0,8},{4,12},{8,0},{12,4},{16,24},{20,28},{24,16},{28,20},{1,9},{5... | collective-permute-start | bytes 1572872 | tf_op jit(solution)/shard_map/ppermute | solution.py:464
  100.8 1.7 %collective-permute-start.26 = (bf16[1024,128]{1,0:T(8,128)(2,1)S(1)}, bf16[1024,128]{1,0:T(8,128)(2,1)S(1)}, u32[]{:S(2)}, u32[]{:S(2)}) collective-permute-start(bf16[1024,128]{1,0:T(8,128)(2,1)S(1)} %get-tuple-element.196.refs_10_), channel_id=1, source_target_pairs={{0,4},{4,0},{8,12},{12,8},{16,20},{20,16},{24,28},{28,24},{1,5},{5... | collective-permute-start | bytes 786440 | tf_op jit(solution)/shard_map/ppermute | solution.py:464
  102.4 3.4 %shard_map.398 = (f32[512,512]{1,0:T(8,128)S(1)}, f32[512,512]{1,0:T(8,128)S(1)}, f32[16,128]{1,0:T(8,128)S(1)}) custom-call(f32[4,512]{1,0:T(4,128)S(1)} %copy-done.14, bf16[512,1536]{1,0:T(8,128)(2,1)S(1)} %get-tuple-element.153.refs_3_.refs_1_, bf16[512,1536]{1,0:T(8,128)(2,1)S(1)} %get-tuple-element.170.refs_5_.refs_12_.refs_2_, ...), custom_call_target="tpu_custom_call" | custom-call | flops 3000000000 | bytes 6000000 | tf_op jit(solution)/shard_map/pallas_call | solution.py:451
  105.9 1.2 collective-permute-done.28
  108.2 2.6 %collective-permute-done.29.refs_6_ = f32[16,128]{1,0:T(8,128)S(1)} collective-permute-done((f32[16,128]{1,0:T(8,128)S(1)}, f32[16,128]{1,0:T(8,128)S(1)}, u32[]{:S(2)}, u32[]{:S(2)}) %collective-permute-start.29) | collective-permute-done | bytes 8224 | tf_op jit(solution)/shard_map/ppermute | solution.py:464
  111.8 1.7 %collective-permute-start.30 = (bf16[512,128]{1,0:T(8,128)(2,1)S(1)}, bf16[512,128]{1,0:T(8,128)(2,1)S(1)}, u32[]{:S(2)}, u32[]{:S(2)}) collective-permute-start(bf16[512,128]{1,0:T(8,128)(2,1)S(1)} %get-tuple-element.205.refs_4_), channel_id=1, source_target_pairs={{0,2},{1,3},{2,0},{3,1},{4,6},{5,7},{6,4},{7,5},{8,10},{9,11},{10,... | collective-permute-start | bytes 393224 | tf_op jit(solution)/shard_map/ppermute | solution.py:464
  114.1 1.1 collective-permute-start.36
  118.6 2.0 %copy.46 = bf16[512,2,512]{2,1,0:T(2,128)(2,1)} copy(bf16[512,2,512]{2,0,1:T(8,128)(2,1)S(1)} %bitcast.88) | data formatting | bytes 2097152
  121.3 3.1 %collective-permute-start.37 = (bf16[2,64,512]{2,1,0:T(8,128)(2,1)S(1)}, bf16[2,64,512]{2,1,0:T(8,128)(2,1)S(1)}, u32[]{:S(2)}, u32[]{:S(2)}) collective-permute-start(bf16[2,64,512]{2,1,0:T(8,128)(2,1)S(1)} %get-tuple-element.224), channel_id=1, source_target_pairs={{0,16},{4,20},{8,24},{12,28},{16,0},{20,4},{24,8},{28,12},{1,17},{... | collective-permute-start | bytes 393224 | tf_op jit(solution)/shard_map/ppermute | solution.py:464
  125.0 1.9 %collective-permute-start.34 = (bf16[288,128]{1,0:T(8,128)(2,1)S(1)}, bf16[288,128]{1,0:T(8,128)(2,1)S(1)}, u32[]{:S(2)}, u32[]{:S(2)}) collective-permute-start(bf16[288,128]{1,0:T(8,128)(2,1)S(1)} %get-tuple-element.217), channel_id=1, source_target_pairs={{0,16},{4,20},{8,24},{12,28},{16,0},{20,4},{24,8},{28,12},{1,17},{... | collective-permute-start | bytes 221192 | tf_op jit(solution)/shard_map/ppermute | solution.py:464
  127.3 2.9 %copy.47 = f32[512,2,512]{2,1,0:T(2,128)} copy(f32[512,2,512]{2,0,1:T(8,128)S(1)} %maximum_bitcast_fusion) | data formatting | bytes 4194304
  130.5 1.1 shard_map.404
  (120 shorter events, 32.9 us)
Async XLA Ops:
  1.6 7.8 %collective-permute-start = (bf16[256,128]{1,0:T(8,128)(2,1)S(1)}, bf16[256,128]{1,0:T(8,128)(2,1)S(1)}, u32[]{:S(2)}, u32[]{:S(2)}) collective-permute-start(bf16[256,128]{1,0:T(8,128)(2,1)S(1)} %bitcast.145), channel_id=1, source_target_pairs={{0,16},{4,20},{8,24},{12,28},{16,0},{20,4},{24,8},{28,12},{1,17},{... | collective-permute-start | bytes 196616 | tf_op jit(solution)/shard_map/ppermute | solution.py:464
  9.9 5.9 %collective-permute-start.5 = (bf16[512,128]{1,0:T(8,128)(2,1)S(1)}, bf16[512,128]{1,0:T(8,128)(2,1)S(1)}, u32[]{:S(2)}, u32[]{:S(2)}) collective-permute-start(bf16[512,128]{1,0:T(8,128)(2,1)S(1)} %bitcast.142), channel_id=1, source_target_pairs={{0,8},{4,12},{8,0},{12,4},{16,24},{20,28},{24,16},{28,20},{1,9},{5... | collective-permute-start | bytes 393224 | tf_op jit(solution)/shard_map/ppermute | solution.py:464
  12.4 9.2 %collective-permute-start.1 = (bf16[128,512]{1,0:T(8,128)(2,1)S(1)}, bf16[128,512]{1,0:T(8,128)(2,1)S(1)}, u32[]{:S(2)}, u32[]{:S(2)}) collective-permute-start(bf16[128,512]{1,0:T(8,128)(2,1)S(1)} %shard_map.378), channel_id=1, source_target_pairs={{0,16},{4,20},{8,24},{12,28},{16,0},{20,4},{24,8},{28,12},{1,17},{... | collective-permute-start | bytes 393224 | tf_op jit(solution)/shard_map/ppermute | solution.py:464
  16.4 5.8 %collective-permute-start.9 = (bf16[512,128]{1,0:T(8,128)(2,1)S(1)}, bf16[512,128]{1,0:T(8,128)(2,1)S(1)}, u32[]{:S(2)}, u32[]{:S(2)}) collective-permute-start(bf16[512,128]{1,0:T(8,128)(2,1)S(1)} %bitcast.138), channel_id=1, source_target_pairs={{0,4},{4,0},{8,12},{12,8},{16,20},{20,16},{24,28},{28,24},{1,5},{5... | collective-permute-start | bytes 393224 | tf_op jit(solution)/shard_map/ppermute | solution.py:464
  22.1 7.7 %collective-permute-start.2 = (bf16[256,512]{1,0:T(8,128)(2,1)S(1)}, bf16[256,512]{1,0:T(8,128)(2,1)S(1)}, u32[]{:S(2)}, u32[]{:S(2)}) collective-permute-start(bf16[256,512]{1,0:T(8,128)(2,1)S(1)} %bitcast.82), channel_id=1, source_target_pairs={{0,8},{4,12},{8,0},{12,4},{16,24},{20,28},{24,16},{28,20},{1,9},{5... | collective-permute-start | bytes 786440 | tf_op jit(solution)/shard_map/ppermute | solution.py:464
  23.5 12.0 %collective-permute-start.11 = (bf16[1024,128]{1,0:T(8,128)(2,1)S(1)}, bf16[1024,128]{1,0:T(8,128)(2,1)S(1)}, u32[]{:S(2)}, u32[]{:S(2)}) collective-permute-start(bf16[1024,128]{1,0:T(8,128)(2,1)S(1)} %bitcast.127), channel_id=1, source_target_pairs={{0,2},{1,3},{2,0},{3,1},{4,6},{5,7},{6,4},{7,5},{8,10},{9,11},{10,... | collective-permute-start | bytes 786440 | tf_op jit(solution)/shard_map/ppermute | solution.py:464
  25.1 10.4 %collective-permute-start.10 = (bf16[1024,128]{1,0:T(8,128)(2,1)S(1)}, bf16[1024,128]{1,0:T(8,128)(2,1)S(1)}, u32[]{:S(2)}, u32[]{:S(2)}) collective-permute-start(bf16[1024,128]{1,0:T(8,128)(2,1)S(1)} %bitcast.125), channel_id=1, source_target_pairs={{0,4},{4,0},{8,12},{12,8},{16,20},{20,16},{24,28},{28,24},{1,5},{5... | collective-permute-start | bytes 786440 | tf_op jit(solution)/shard_map/ppermute | solution.py:464
  30.4 6.7 %collective-permute-start.4 = (bf16[256,512]{1,0:T(8,128)(2,1)S(1)}, bf16[256,512]{1,0:T(8,128)(2,1)S(1)}, u32[]{:S(2)}, u32[]{:S(2)}) collective-permute-start(bf16[256,512]{1,0:T(8,128)(2,1)S(1)} %bitcast.118), channel_id=1, source_target_pairs={{0,4},{4,0},{8,12},{12,8},{16,20},{20,16},{24,28},{28,24},{1,5},{5... | collective-permute-start | bytes 786440 | tf_op jit(solution)/shard_map/ppermute | solution.py:464
  32.0 10.0 %collective-permute-start.3 = (bf16[256,512]{1,0:T(8,128)(2,1)S(1)}, bf16[256,512]{1,0:T(8,128)(2,1)S(1)}, u32[]{:S(2)}, u32[]{:S(2)}) collective-permute-start(bf16[256,512]{1,0:T(8,128)(2,1)S(1)} %bitcast.97), channel_id=1, source_target_pairs={{0,2},{1,3},{2,0},{3,1},{4,6},{5,7},{6,4},{7,5},{8,10},{9,11},{10,... | collective-permute-start | bytes 786440 | tf_op jit(solution)/shard_map/ppermute | solution.py:464
  36.3 8.1 %collective-permute-start.15 = (bf16[1024,128]{1,0:T(8,128)(2,1)S(1)}, bf16[1024,128]{1,0:T(8,128)(2,1)S(1)}, u32[]{:S(2)}, u32[]{:S(2)}) collective-permute-start(bf16[1024,128]{1,0:T(8,128)(2,1)S(1)} %get-tuple-element.278), channel_id=1, source_target_pairs={{0,1},{1,0},{2,3},{3,2},{4,5},{5,4},{6,7},{7,6},{8,9},{9,8},{10,11... | collective-permute-start | bytes 786440 | tf_op jit(solution)/shard_map/ppermute | solution.py:464
  36.4 8.9 %collective-permute-start.14 = (bf16[1024,128]{1,0:T(8,128)(2,1)S(1)}, bf16[1024,128]{1,0:T(8,128)(2,1)S(1)}, u32[]{:S(2)}, u32[]{:S(2)}) collective-permute-start(bf16[1024,128]{1,0:T(8,128)(2,1)S(1)} %get-tuple-element.279), channel_id=1, source_target_pairs={{0,1},{1,0},{2,3},{3,2},{4,5},{5,4},{6,7},{7,6},{8,9},{9,8},{10,11... | collective-permute-start | bytes 786440 | tf_op jit(solution)/shard_map/ppermute | solution.py:464
  36.9 8.3 %collective-permute-start.17 = (bf16[1024,128]{1,0:T(8,128)(2,1)S(1)}, bf16[1024,128]{1,0:T(8,128)(2,1)S(1)}, u32[]{:S(2)}, u32[]{:S(2)}) collective-permute-start(bf16[1024,128]{1,0:T(8,128)(2,1)S(1)} %get-tuple-element.276), channel_id=1, source_target_pairs={{0,1},{1,0},{2,3},{3,2},{4,5},{5,4},{6,7},{7,6},{8,9},{9,8},{10,11... | collective-permute-start | bytes 786440 | tf_op jit(solution)/shard_map/ppermute | solution.py:464
  37.1 8.2 %collective-permute-start.16 = (bf16[1024,128]{1,0:T(8,128)(2,1)S(1)}, bf16[1024,128]{1,0:T(8,128)(2,1)S(1)}, u32[]{:S(2)}, u32[]{:S(2)}) collective-permute-start(bf16[1024,128]{1,0:T(8,128)(2,1)S(1)} %get-tuple-element.277), channel_id=1, source_target_pairs={{0,1},{1,0},{2,3},{3,2},{4,5},{5,4},{6,7},{7,6},{8,9},{9,8},{10,11... | collective-permute-start | bytes 786440 | tf_op jit(solution)/shard_map/ppermute | solution.py:464
  42.6 14.4 %collective-permute-start.13 = (bf16[512,512]{1,0:T(8,128)(2,1)S(1)}, bf16[512,512]{1,0:T(8,128)(2,1)S(1)}, u32[]{:S(2)}, u32[]{:S(2)}) collective-permute-start(bf16[512,512]{1,0:T(8,128)(2,1)S(1)} %bitcast.108), channel_id=1, source_target_pairs={{0,2},{1,3},{2,0},{3,1},{4,6},{5,7},{6,4},{7,5},{8,10},{9,11},{10,... | collective-permute-start | bytes 1572872 | tf_op jit(solution)/shard_map/ppermute | solution.py:464
  44.4 12.7 %collective-permute-start.12 = (bf16[512,512]{1,0:T(8,128)(2,1)S(1)}, bf16[512,512]{1,0:T(8,128)(2,1)S(1)}, u32[]{:S(2)}, u32[]{:S(2)}) collective-permute-start(bf16[512,512]{1,0:T(8,128)(2,1)S(1)} %bitcast.105), channel_id=1, source_target_pairs={{0,4},{4,0},{8,12},{12,8},{16,20},{20,16},{24,28},{28,24},{1,5},{5... | collective-permute-start | bytes 1572872 | tf_op jit(solution)/shard_map/ppermute | solution.py:464
  58.0 8.1 %collective-permute-start.19 = (bf16[1024,512]{1,0:T(8,128)(2,1)S(1)}, bf16[1024,512]{1,0:T(8,128)(2,1)S(1)}, u32[]{:S(2)}, u32[]{:S(2)}) collective-permute-start(bf16[1024,512]{1,0:T(8,128)(2,1)S(1)} %bitcast.149), channel_id=1, source_target_pairs={{0,1},{1,0},{2,3},{3,2},{4,5},{5,4},{6,7},{7,6},{8,9},{9,8},{10,11... | collective-permute-start | bytes 3145736 | tf_op jit(solution)/shard_map/ppermute | solution.py:464
  58.1 8.1 %collective-permute-start.18 = (bf16[1024,512]{1,0:T(8,128)(2,1)S(1)}, bf16[1024,512]{1,0:T(8,128)(2,1)S(1)}, u32[]{:S(2)}, u32[]{:S(2)}) collective-permute-start(bf16[1024,512]{1,0:T(8,128)(2,1)S(1)} %bitcast.147), channel_id=1, source_target_pairs={{0,1},{1,0},{2,3},{3,2},{4,5},{5,4},{6,7},{7,6},{8,9},{9,8},{10,11... | collective-permute-start | bytes 3145736 | tf_op jit(solution)/shard_map/ppermute | solution.py:464
  74.0 6.2 %collective-permute-start.20 = (bf16[1024,512]{1,0:T(8,128)(2,1)S(1)}, bf16[1024,512]{1,0:T(8,128)(2,1)S(1)}, u32[]{:S(2)}, u32[]{:S(2)}) collective-permute-start(bf16[1024,512]{1,0:T(8,128)(2,1)S(1)} %get-tuple-element.180), channel_id=1, source_target_pairs={{0,1},{1,0},{2,3},{3,2},{4,5},{5,4},{6,7},{7,6},{8,9},{9,8},{10,11... | collective-permute-start | bytes 3145736 | tf_op jit(solution)/shard_map/ppermute | solution.py:464
  74.2 6.1 %collective-permute-start.21 = (bf16[1024,512]{1,0:T(8,128)(2,1)S(1)}, bf16[1024,512]{1,0:T(8,128)(2,1)S(1)}, u32[]{:S(2)}, u32[]{:S(2)}) collective-permute-start(bf16[1024,512]{1,0:T(8,128)(2,1)S(1)} %get-tuple-element.182), channel_id=1, source_target_pairs={{0,1},{1,0},{2,3},{3,2},{4,5},{5,4},{6,7},{7,6},{8,9},{9,8},{10,11... | collective-permute-start | bytes 3145736 | tf_op jit(solution)/shard_map/ppermute | solution.py:464
  81.3 14.2 %collective-permute-start.25 = (bf16[512,512]{1,0:T(8,128)(2,1)S(1)}, bf16[512,512]{1,0:T(8,128)(2,1)S(1)}, u32[]{:S(2)}, u32[]{:S(2)}) collective-permute-start(bf16[512,512]{1,0:T(8,128)(2,1)S(1)} %get-tuple-element.194), channel_id=1, source_target_pairs={{0,2},{1,3},{2,0},{3,1},{4,6},{5,7},{6,4},{7,5},{8,10},{9,11},{10,... | collective-permute-start | bytes 1572872 | tf_op jit(solution)/shard_map/ppermute | solution.py:464
  83.1 13.9 %collective-permute-start.24 = (bf16[512,512]{1,0:T(8,128)(2,1)S(1)}, bf16[512,512]{1,0:T(8,128)(2,1)S(1)}, u32[]{:S(2)}, u32[]{:S(2)}) collective-permute-start(bf16[512,512]{1,0:T(8,128)(2,1)S(1)} %get-tuple-element.183.refs_14_), channel_id=1, source_target_pairs={{0,4},{4,0},{8,12},{12,8},{16,20},{20,16},{24,28},{28,24},{1,5},{5... | collective-permute-start | bytes 1572872 | tf_op jit(solution)/shard_map/ppermute | solution.py:464
  94.3 5.2 %collective-permute-start.22 = (bf16[2048,128]{1,0:T(8,128)(2,1)S(1)}, bf16[2048,128]{1,0:T(8,128)(2,1)S(1)}, u32[]{:S(2)}, u32[]{:S(2)}) collective-permute-start(bf16[2048,128]{1,0:T(8,128)(2,1)S(1)} %get-tuple-element.189), channel_id=1, source_target_pairs={{0,1},{1,0},{2,3},{3,2},{4,5},{5,4},{6,7},{7,6},{8,9},{9,8},{10,11... | collective-permute-start | bytes 1572872 | tf_op jit(solution)/shard_map/ppermute | solution.py:464
  97.7 15.8 %collective-permute-start.32 = (bf16[2,256,512]{2,1,0:T(8,128)(2,1)S(1)}, bf16[2,256,512]{2,1,0:T(8,128)(2,1)S(1)}, u32[]{:S(2)}, u32[]{:S(2)}) collective-permute-start(bf16[2,256,512]{2,1,0:T(8,128)(2,1)S(1)} %get-tuple-element.195.refs_5_), channel_id=1, source_target_pairs={{0,8},{4,12},{8,0},{12,4},{16,24},{20,28},{24,16},{28,20},{1,9},{5... | collective-permute-start | bytes 1572872 | tf_op jit(solution)/shard_map/ppermute | solution.py:464
  100.3 10.4 %collective-permute-start.27 = (bf16[1024,128]{1,0:T(8,128)(2,1)S(1)}, bf16[1024,128]{1,0:T(8,128)(2,1)S(1)}, u32[]{:S(2)}, u32[]{:S(2)}) collective-permute-start(bf16[1024,128]{1,0:T(8,128)(2,1)S(1)} %get-tuple-element.201), channel_id=1, source_target_pairs={{0,2},{1,3},{2,0},{3,1},{4,6},{5,7},{6,4},{7,5},{8,10},{9,11},{10,... | collective-permute-start | bytes 786440 | tf_op jit(solution)/shard_map/ppermute | solution.py:464
  100.8 10.0 %collective-permute-start.26 = (bf16[1024,128]{1,0:T(8,128)(2,1)S(1)}, bf16[1024,128]{1,0:T(8,128)(2,1)S(1)}, u32[]{:S(2)}, u32[]{:S(2)}) collective-permute-start(bf16[1024,128]{1,0:T(8,128)(2,1)S(1)} %get-tuple-element.196.refs_10_), channel_id=1, source_target_pairs={{0,4},{4,0},{8,12},{12,8},{16,20},{20,16},{24,28},{28,24},{1,5},{5... | collective-permute-start | bytes 786440 | tf_op jit(solution)/shard_map/ppermute | solution.py:464
  111.4 6.2 %collective-permute-start.31 = (bf16[544,128]{1,0:T(8,128)(2,1)S(1)}, bf16[544,128]{1,0:T(8,128)(2,1)S(1)}, u32[]{:S(2)}, u32[]{:S(2)}) collective-permute-start(bf16[544,128]{1,0:T(8,128)(2,1)S(1)} %get-tuple-element.206), channel_id=1, source_target_pairs={{0,4},{4,0},{8,12},{12,8},{16,20},{20,16},{24,28},{28,24},{1,5},{5... | collective-permute-start | bytes 417800 | tf_op jit(solution)/shard_map/ppermute | solution.py:464
  111.8 5.4 %collective-permute-start.30 = (bf16[512,128]{1,0:T(8,128)(2,1)S(1)}, bf16[512,128]{1,0:T(8,128)(2,1)S(1)}, u32[]{:S(2)}, u32[]{:S(2)}) collective-permute-start(bf16[512,128]{1,0:T(8,128)(2,1)S(1)} %get-tuple-element.205.refs_4_), channel_id=1, source_target_pairs={{0,2},{1,3},{2,0},{3,1},{4,6},{5,7},{6,4},{7,5},{8,10},{9,11},{10,... | collective-permute-start | bytes 393224 | tf_op jit(solution)/shard_map/ppermute | solution.py:464
  114.1 6.5 %collective-permute-start.36 = (bf16[128,512]{1,0:T(8,128)(2,1)S(1)}, bf16[128,512]{1,0:T(8,128)(2,1)S(1)}, u32[]{:S(2)}, u32[]{:S(2)}) collective-permute-start(bf16[128,512]{1,0:T(8,128)(2,1)S(1)} %get-tuple-element.221), channel_id=1, source_target_pairs={{0,4},{4,0},{8,12},{12,8},{16,20},{20,16},{24,28},{28,24},{1,5},{5... | collective-permute-start | bytes 393224 | tf_op jit(solution)/shard_map/ppermute | solution.py:464
  115.3 5.4 %collective-permute-start.35 = (bf16[128,512]{1,0:T(8,128)(2,1)S(1)}, bf16[128,512]{1,0:T(8,128)(2,1)S(1)}, u32[]{:S(2)}, u32[]{:S(2)}) collective-permute-start(bf16[128,512]{1,0:T(8,128)(2,1)S(1)} %get-tuple-element.210.refs_6_), channel_id=1, source_target_pairs={{0,2},{1,3},{2,0},{3,1},{4,6},{5,7},{6,4},{7,5},{8,10},{9,11},{10,... | collective-permute-start | bytes 393224 | tf_op jit(solution)/shard_map/ppermute | solution.py:464
  118.2 6.2 %collective-permute-start.33 = (bf16[544,128]{1,0:T(8,128)(2,1)S(1)}, bf16[544,128]{1,0:T(8,128)(2,1)S(1)}, u32[]{:S(2)}, u32[]{:S(2)}) collective-permute-start(bf16[544,128]{1,0:T(8,128)(2,1)S(1)} %get-tuple-element.213), channel_id=1, source_target_pairs={{0,8},{4,12},{8,0},{12,4},{16,24},{20,28},{24,16},{28,20},{1,9},{5... | collective-permute-start | bytes 417800 | tf_op jit(solution)/shard_map/ppermute | solution.py:464
  121.3 9.2 %collective-permute-start.37 = (bf16[2,64,512]{2,1,0:T(8,128)(2,1)S(1)}, bf16[2,64,512]{2,1,0:T(8,128)(2,1)S(1)}, u32[]{:S(2)}, u32[]{:S(2)}) collective-permute-start(bf16[2,64,512]{2,1,0:T(8,128)(2,1)S(1)} %get-tuple-element.224), channel_id=1, source_target_pairs={{0,16},{4,20},{8,24},{12,28},{16,0},{20,4},{24,8},{28,12},{1,17},{... | collective-permute-start | bytes 393224 | tf_op jit(solution)/shard_map/ppermute | solution.py:464
  125.0 6.6 %collective-permute-start.34 = (bf16[288,128]{1,0:T(8,128)(2,1)S(1)}, bf16[288,128]{1,0:T(8,128)(2,1)S(1)}, u32[]{:S(2)}, u32[]{:S(2)}) collective-permute-start(bf16[288,128]{1,0:T(8,128)(2,1)S(1)} %get-tuple-element.217), channel_id=1, source_target_pairs={{0,16},{4,20},{8,24},{12,28},{16,0},{20,4},{24,8},{28,12},{1,17},{... | collective-permute-start | bytes 221192 | tf_op jit(solution)/shard_map/ppermute | solution.py:464
  (25 other events, 110.5 us)
